TPU v7x, 512 devices: a whole 4x4x16 slice. The times are simulated.
512 devices in a mesh: season: 4 (over x_lo, core), gx: 8 (over y, x_hi), gy: 16 (over z).
Axes of the slice: x: 4 (x_hi: 2, x_lo: 2; x = x_hi * 2 + x_lo), y: 4, z: 16, core: 2. Of those that a mesh axis runs over, the one named last changes fastest.
Arguments:
- zone_ids: int32 [32, 64, 2048], P(None, 'gx', 'gy'), may hold values from 0 to 63
- log_perm: float32 [64], replicated, may hold values from -1 to 1
- log_disp: float32 [64], replicated, may hold values from -1 to 1
- temp_start: float32 [4, 32, 64, 2048], P('season', None, 'gx', 'gy'), may hold values from -6 to 6
- pressure_start: float32 [4, 32, 64, 2048], P('season', None, 'gx', 'gy'), may hold values from -6 to 6
- temp_observed: float32 [4, 32, 64, 2048], P('season', None, 'gx', 'gy'), may hold values from -6 to 6
- well_cells: int32 [2048], replicated, may hold values from 0 to 4194303
- well_flow: float32 [2048], replicated, may hold values from 0.5 to 2
- plan: int32 [4, 2048], P('season'), may hold values from -3 to 3
- inject_temp: float32 [4, 2048], P('season'), may hold values from -6 to 6
Outputs:
- temp_end: float32 [4, 32, 64, 2048], P('season', None, 'gx', 'gy')
- perm_sensitivity: float32 [4, 32, 64, 2048], P('season', None, 'gx', 'gy')
- zone_gradient: float32 [2, 64], replicated
All inputs are finite; a program needn't handle non-finite values.
Results may differ from a plain program's by a relative error of at most 0.0003.
Values sent between devices are 32-bit elements; how exact they have to be, the bound alone decides.
No kernel may reach another device: no remote copies, remote signals or barrier semaphores. Data moves between devices by JAX's collectives and lax.ppermute only.
A program may use at most 64 MiB of HBM per device.

v0:
```python
import jax
import jax.numpy as jnp
from jax import lax
from jax.sharding import PartitionSpec as P

ITERS = 4


STORAGE = 0.5
CONDUCT = 0.1
SMOOTH = 0.01
TIME_STEP = 0.02
HEAT_GAIN = 10.0


def padded(array, sides, width):
    for axis, dim in sides:
        size, length = (lax.axis_size(axis), array.shape[dim])
        up = [(i, (i + 1) % size) for i in range(size - 1)]
        down = [(j, i) for i, j in up]
        last = lax.slice_in_dim(array, length - width, length, axis=dim)
        first = lax.slice_in_dim(array, 0, width, axis=dim)
        before = lax.ppermute(last, axis, up)
        after = lax.ppermute(first, axis, down)
        array = jnp.concatenate([before, array, after], axis=dim)
    return array


def beside_all(field):
    centre = field[:, 1:-1, 1:-1]
    stacked = jnp.pad(centre, ((1, 1), (0, 0), (0, 0)))
    sides = (
        field[:, :-2, 1:-1],
        field[:, 2:, 1:-1],
        field[:, 1:-1, :-2],
        field[:, 1:-1, 2:],
        stacked[:-2],
        stacked[2:],
    )
    return (centre, sides)


def relax_pressure(pressure, perm, source, inside):
    press_mid, press_side = beside_all(pressure)
    perm_mid, perm_side = beside_all(perm)
    numer = source
    denom = STORAGE
    for press_other, perm_other in zip(press_side, perm_side):
        trans = 0.5 * (perm_mid + perm_other)
        numer = numer + trans * press_other
        denom = denom + trans
    return jnp.where(inside, numer / denom, 0.0)


def transport(temp, pressure, perm, disp, heating):
    temp_mid, temp_side = beside_all(temp)
    press_mid, press_side = beside_all(pressure)
    perm_mid, perm_side = beside_all(perm)
    disp_mid, disp_side = beside_all(disp)
    change = HEAT_GAIN * heating
    for index in range(6):
        trans = 0.5 * (perm_mid + perm_side[index])
        flow = trans * (press_mid - press_side[index])
        speed = jnp.sqrt(flow * flow + SMOOTH)
        spread = CONDUCT + 0.5 * (disp_mid + disp_side[index]) * speed
        flux = spread * (temp_mid - temp_side[index]) + 0.5 * flow * (temp_mid + temp_side[index])
        change = change - flux
    return temp_mid + TIME_STEP * change


def trim_margin(field, amount):
    return field[:, amount:-amount, amount:-amount]


def pieces(count, width):
    return ((2 * width, count, 0), (0, width, 0), (count + 3 * width, width, count - width))


def gather_back(widened, width):
    tile_rows = widened.shape[1] - 4 * width
    tile_cols = widened.shape[2] - 4 * width
    result = jnp.zeros((widened.shape[0], tile_rows, tile_cols), jnp.float32)
    for row_rank, row_piece in enumerate(pieces(tile_rows, width)):
        for col_rank, col_piece in enumerate(pieces(tile_cols, width)):
            if row_rank > 0 and col_rank > 0:
                continue
            block = widened[
                :,
                row_piece[0] : row_piece[0] + row_piece[1],
                col_piece[0] : col_piece[0] + col_piece[1],
            ]
            result = result.at[
                :,
                row_piece[2] : row_piece[2] + row_piece[1],
                col_piece[2] : col_piece[2] + col_piece[1],
            ].add(block)
    return result


def lookup(zone_ids, log_perm, log_disp):
    table = jnp.stack([log_perm, log_disp])
    labels = jnp.arange(table.shape[1], dtype=jnp.int32)

    def lookup_one_layer(zone_layer):
        onehot = (labels[:, None] == zone_layer.reshape(-1)[None, :]).astype(jnp.float32)
        return jnp.dot(table, onehot, precision=lax.Precision.HIGHEST)

    values = lax.map(lookup_one_layer, zone_ids)
    return (values[:, 0].reshape(zone_ids.shape), values[:, 1].reshape(zone_ids.shape))


def zone_sums(zone_ids, sens_perm, sens_disp, zones_total):
    labels = jnp.arange(zones_total, dtype=jnp.int32)

    def zone_one_layer(carry, layer_parts):
        zone_layer, perm_layer, disp_layer = layer_parts
        onehot = (labels[:, None] == zone_layer.reshape(-1)[None, :]).astype(jnp.float32)
        values = jnp.stack([perm_layer.reshape(-1), disp_layer.reshape(-1)])
        added = lax.dot_general(
            values, onehot, (((1,), (1,)), ((), ())), precision=lax.Precision.HIGHEST
        )
        return (carry + added, None)

    start = jnp.zeros((2, zones_total), jnp.float32)
    totals, unused = lax.scan(zone_one_layer, start, (zone_ids, sens_perm, sens_disp))
    return totals


def body(
    zone_ids,
    log_perm,
    log_disp,
    temp_start,
    pressure_start,
    temp_observed,
    well_cells,
    well_flow,
    plan,
    inject_temp,
):
    layers, tile_rows, tile_cols = zone_ids.shape
    zones_total = log_perm.shape[0]
    grid_rows = tile_rows * lax.axis_size("gx")
    grid_cols = tile_cols * lax.axis_size("gy")
    row_start = lax.axis_index("gx") * tile_rows
    col_start = lax.axis_index("gy") * tile_cols
    margin = 1
    log_perm_cells, log_disp_cells = lookup(zone_ids, log_perm, log_disp)
    perm = jnp.exp(log_perm_cells)
    disp = jnp.exp(log_disp_cells)
    rate = plan[0].astype(jnp.float32) * well_flow
    warmth = jnp.maximum(rate, 0.0) * inject_temp[0]
    layer_of = well_cells // (grid_rows * grid_cols)
    local_row = well_cells // grid_cols % grid_rows - row_start + margin
    local_col = well_cells % grid_cols - col_start + margin
    wide_rows = tile_rows + 2 * margin
    wide_cols = tile_cols + 2 * margin
    valid = (local_row >= 0) & (local_row < wide_rows) & (local_col >= 0) & (local_col < wide_cols)
    clipped_row = jnp.clip(local_row, 0, wide_rows - 1)
    clipped_col = jnp.clip(local_col, 0, wide_cols - 1)
    empty = jnp.zeros((layers, wide_rows, wide_cols), jnp.float32)
    source = empty.at[layer_of, clipped_row, clipped_col].add(jnp.where(valid, rate, 0.0))
    heating = empty.at[layer_of, clipped_row, clipped_col].add(jnp.where(valid, warmth, 0.0))
    global_row = jnp.arange(wide_rows, dtype=jnp.int32) - margin + row_start
    global_col = jnp.arange(wide_cols, dtype=jnp.int32) - margin + col_start
    row_ok = (global_row >= 0) & (global_row < grid_rows)
    col_ok = (global_col >= 0) & (global_col < grid_cols)
    inside = jnp.broadcast_to(
        row_ok[None, :, None] & col_ok[None, None, :], (layers, wide_rows, wide_cols)
    )
    temp_begin = temp_start[0]
    press_begin = pressure_start[0]
    observed = temp_observed[0]
    perm_ext, disp_ext, temp_ext = (
        padded(perm, (("gx", 1), ("gy", 2)), 1),
        padded(disp, (("gx", 1), ("gy", 2)), 1),
        padded(temp_begin, (("gx", 1), ("gy", 2)), 1),
    )
    source_mid = trim_margin(source, 1)
    inside_mid = trim_margin(inside, 1)
    heating_mid = trim_margin(heating, 1)
    kept = []
    pressure = press_begin
    for sweep_index in range(ITERS + 1):
        press_ext = padded(pressure, (("gx", 1), ("gy", 2)), 1)
        kept.append(press_ext)
        if sweep_index < ITERS:
            pressure = relax_pressure(press_ext, perm_ext, source_mid, inside_mid)

    def heat_local(press_wide, perm_wide, disp_wide):
        return transport(temp_ext, press_wide, perm_wide, disp_wide, heating_mid)

    temp_final, pull = jax.vjp(heat_local, kept[ITERS], perm_ext, disp_ext)
    misfit = temp_final - observed
    grad_press, grad_perm_ext, grad_disp_ext = pull(misfit)

    def relax_local(press_wide, perm_wide):
        return relax_pressure(press_wide, perm_wide, source_mid, inside_mid)

    for sweep_index in reversed(range(ITERS)):
        returned = padded(grad_press, (("gx", 1), ("gy", 2)), 1)
        grad_here = gather_back(returned, 1)
        unused, pull_sweep = jax.vjp(relax_local, kept[sweep_index], perm_ext)
        grad_press, grad_perm_more = pull_sweep(grad_here)
        grad_perm_ext = grad_perm_ext + grad_perm_more
    back_perm, back_disp = (
        padded(grad_perm_ext, (("gx", 1), ("gy", 2)), 1),
        padded(grad_disp_ext, (("gx", 1), ("gy", 2)), 1),
    )
    grad_perm = gather_back(back_perm, 1)
    grad_disp = gather_back(back_disp, 1)
    sens_perm = grad_perm * perm
    sens_disp = grad_disp * disp
    partial_totals = zone_sums(zone_ids, sens_perm, sens_disp, zones_total)
    totals = lax.psum(partial_totals, ("season", "gx", "gy"))
    factor = (lax.axis_size("season") * layers * grid_rows * grid_cols / zones_total) ** (-0.5)
    return (temp_final[None], sens_perm[None], totals * factor)


def solution(mesh):
    in_specs = (
        P(None, "gx", "gy"),
        P(),
        P(),
        P("season", None, "gx", "gy"),
        P("season", None, "gx", "gy"),
        P("season", None, "gx", "gy"),
        P(),
        P(),
        P("season", None),
        P("season", None),
    )
    out_specs = (P("season", None, "gx", "gy"), P("season", None, "gx", "gy"), P())
    return jax.shard_map(body, mesh=mesh, in_specs=in_specs, out_specs=out_specs, check_vma=False)
```

profile of v0, /device:TPU:1, one launch (start us, length us, event | category | flops | bytes accessed | tf_op | source)
XLA Modules:
  0.0 497.7 jit_solution(11964580275629166877)
XLA Ops:
  1.3 28.8 %while.58 = (s32[]{:T(128)}, f32[32,2,1024]{2,1,0:T(2,128)S(1)}, s32[32,8,128]{2,1,0:T(8,128)}, f32[2,64]{1,0:T(2,128)S(1)}, s32[]{:T(128)}) while((s32[]{:T(128)}, f32[32,2,1024]{2,1,0:T(2,128)S(1)}, s32[32,8,128]{2,1,0:T(8,128)}, f32[2,64]{1,0:T(2,128)S(1)}, s32[]{:T(128)}) %tuple.302), condition=%wide.region_2.3_spmd.clone, body=%wide.region_1.2_spmd.clone.sunk | while | flops 1638402 | bytes 21573 | solution.py:108
  30.5 5.5 %collective-permute-start.1 = (f32[32,1,128]{2,0,1:T(8,128)S(1)}, f32[32,1,128]{2,0,1:T(8,128)S(1)}, u32[]{:S(2)}, u32[]{:S(2)}) collective-permute-start(f32[32,1,128]{2,0,1:T(8,128)S(1)} %get-tuple-element.700), channel_id=1, source_target_pairs={{0,16},{16,32},{32,48},{48,64},{64,80},{80,96},{96,112},{1,17},{17... | collective-permute-start | bytes 49160 | tf_op jit(solution)/shard_map/ppermute | solution.py:23
  37.3 5.5 %collective-permute-start.2 = (f32[32,1,128]{2,0,1:T(8,128)S(1)}, f32[32,1,128]{2,0,1:T(8,128)S(1)}, u32[]{:S(2)}, u32[]{:S(2)}) collective-permute-start(f32[32,1,128]{2,0,1:T(8,128)S(1)} %get-tuple-element.698), channel_id=1, source_target_pairs={{0,16},{16,32},{32,48},{48,64},{64,80},{80,96},{96,112},{1,17},{17... | collective-permute-start | bytes 49160 | tf_op jit(solution)/shard_map/ppermute | solution.py:23
  44.2 5.5 %collective-permute-start = (f32[32,1,128]{2,0,1:T(8,128)S(1)}, f32[32,1,128]{2,0,1:T(8,128)S(1)}, u32[]{:S(2)}, u32[]{:S(2)}) collective-permute-start(f32[32,1,128]{2,0,1:T(8,128)S(1)} %get-tuple-element.697), channel_id=1, source_target_pairs={{0,16},{16,32},{32,48},{48,64},{64,80},{80,96},{96,112},{1,17},{17... | collective-permute-start | bytes 49160 | tf_op jit(solution)/shard_map/ppermute | solution.py:23
  64.7 11.3 %scatter_custom_fusion.1 = f32[41600]{0:T(1024)S(1)} fusion(s32[2048]{0:T(1024)S(1)} %broadcast_select_fusion.1, f32[2048]{0:T(1024)S(1)} %get-tuple-element.608, f32[]{:T(128)} %constant.807.clone.1), kind=kCustom, calls=%fused_computation.268 | custom fusion | flops 2048 | bytes 166404
  80.5 6.2 %collective-permute-start.9 = (f32[32,1,128]{2,0,1:T(8,128)S(1)}, f32[32,1,128]{2,0,1:T(8,128)S(1)}, u32[]{:S(2)}, u32[]{:S(2)}) collective-permute-start(f32[32,1,128]{2,0,1:T(8,128)S(1)} %get-tuple-element.694), channel_id=1, source_target_pairs={{0,16},{16,32},{32,48},{48,64},{64,80},{80,96},{96,112},{1,17},{17... | collective-permute-start | bytes 49160 | tf_op jit(solution)/shard_map/ppermute | solution.py:23
  86.7 5.8 %collective-permute-start.22 = (f32[32,1,128]{2,0,1:T(8,128)S(1)}, f32[32,1,128]{2,0,1:T(8,128)S(1)}, u32[]{:S(2)}, u32[]{:S(2)}) collective-permute-start(f32[32,1,128]{2,0,1:T(8,128)S(1)} %get-tuple-element.702), channel_id=1, source_target_pairs={{0,16},{16,32},{32,48},{48,64},{64,80},{80,96},{96,112},{1,17},{17... | collective-permute-start | bytes 49160 | tf_op jit(solution)/shard_map/ppermute | solution.py:23
  100.4 5.2 %collective-permute-done.12 = f32[32,10,1]{2,0,1:T(8,128)S(1)} collective-permute-done((f32[32,10,1]{2,0,1:T(8,128)S(1)}, f32[32,10,1]{2,0,1:T(8,128)S(1)}, u32[]{:S(2)}, u32[]{:S(2)}) %collective-permute-start.12) | collective-permute-done | bytes 1312 | tf_op jit(solution)/shard_map/ppermute | solution.py:24
  106.5 5.5 %collective-permute-start.13 = (f32[32,1,128]{2,0,1:T(8,128)S(1)}, f32[32,1,128]{2,0,1:T(8,128)S(1)}, u32[]{:S(2)}, u32[]{:S(2)}) collective-permute-start(f32[32,1,128]{2,0,1:T(8,128)S(1)} %get-tuple-element.692), channel_id=1, source_target_pairs={{0,16},{16,32},{32,48},{48,64},{64,80},{80,96},{96,112},{1,17},{17... | collective-permute-start | bytes 49160 | tf_op jit(solution)/shard_map/ppermute | solution.py:23
  113.3 5.5 %collective-permute-done.14 = f32[32,1,128]{2,0,1:T(8,128)S(1)} collective-permute-done((f32[32,1,128]{2,0,1:T(8,128)S(1)}, f32[32,1,128]{2,0,1:T(8,128)S(1)}, u32[]{:S(2)}, u32[]{:S(2)}) %collective-permute-start.14) | collective-permute-done | bytes 16416 | tf_op jit(solution)/shard_map/ppermute | solution.py:24
  119.0 4.6 collective-permute-start.15
  125.8 5.0 %collective-permute-done.16 = f32[32,10,1]{2,0,1:T(8,128)S(1)} collective-permute-done((f32[32,10,1]{2,0,1:T(8,128)S(1)}, f32[32,10,1]{2,0,1:T(8,128)S(1)}, u32[]{:S(2)}, u32[]{:S(2)}) %collective-permute-start.16) | collective-permute-done | bytes 1312 | tf_op jit(solution)/shard_map/ppermute | solution.py:24
  131.7 5.8 %collective-permute-start.17 = (f32[32,1,128]{2,0,1:T(8,128)S(1)}, f32[32,1,128]{2,0,1:T(8,128)S(1)}, u32[]{:S(2)}, u32[]{:S(2)}) collective-permute-start(f32[32,1,128]{2,0,1:T(8,128)S(1)} %get-tuple-element.690), channel_id=1, source_target_pairs={{0,16},{16,32},{32,48},{48,64},{64,80},{80,96},{96,112},{1,17},{17... | collective-permute-start | bytes 49160 | tf_op jit(solution)/shard_map/ppermute | solution.py:23
  139.5 5.5 %collective-permute-start.26 = (f32[32,10,1]{2,0,1:T(8,128)S(1)}, f32[32,10,1]{2,0,1:T(8,128)}, u32[]{:S(2)}, u32[]{:S(2)}) collective-permute-start(f32[32,10,1]{2,0,1:T(8,128)S(1)} %get-tuple-element.659), channel_id=1, source_target_pairs={{0,1},{1,2},{2,3},{3,4},{4,5},{5,6},{6,7},{7,8},{8,9},{9,10},{10,1... | collective-permute-start | bytes 3848 | tf_op jit(solution)/shard_map/ppermute | solution.py:23
  157.4 5.5 %collective-permute-start.21 = (f32[32,1,128]{2,0,1:T(8,128)S(1)}, f32[32,1,128]{2,0,1:T(8,128)S(1)}, u32[]{:S(2)}, u32[]{:S(2)}) collective-permute-start(f32[32,1,128]{2,0,1:T(8,128)S(1)} %get-tuple-element.688), channel_id=1, source_target_pairs={{0,16},{16,32},{32,48},{48,64},{64,80},{80,96},{96,112},{1,17},{17... | collective-permute-start | bytes 49160 | tf_op jit(solution)/shard_map/ppermute | solution.py:23
  171.3 5.1 %collective-permute-start.27 = (f32[32,10,1]{2,0,1:T(8,128)}, f32[32,10,1]{2,0,1:T(8,128)S(1)}, u32[]{:S(2)}, u32[]{:S(2)}) collective-permute-start(f32[32,10,1]{2,0,1:T(8,128)} %get-tuple-element.652), channel_id=1, source_target_pairs={{0,1},{1,2},{2,3},{3,4},{4,5},{5,6},{6,7},{7,8},{8,9},{9,10},{10,1... | collective-permute-start | bytes 3848 | tf_op jit(solution)/shard_map/ppermute | solution.py:23
  178.3 11.4 %scatter_custom_fusion = f32[41600]{0:T(1024)S(1)} fusion(s32[2048]{0:T(1024)} %copy-done.73, f32[2048]{0:T(1024)} %multiply_select_fusion, f32[]{:T(128)} %constant.807.clone.1), kind=kCustom, calls=%fused_computation.270 | custom fusion | flops 2048 | bytes 166912
  197.7 5.5 %collective-permute-start.32 = (f32[32,1,130]{2,0,1:T(8,128)S(1)}, f32[32,1,130]{2,0,1:T(8,128)S(1)}, u32[]{:S(2)}, u32[]{:S(2)}) collective-permute-start(f32[32,1,130]{2,0,1:T(8,128)S(1)} %get-tuple-element.637), channel_id=1, source_target_pairs={{0,16},{16,32},{32,48},{48,64},{64,80},{80,96},{96,112},{1,17},{17... | collective-permute-start | bytes 49928 | tf_op jit(solution)/shard_map/ppermute | solution.py:23
  204.9 4.5 collective-permute-done.33
  210.1 5.2 %collective-permute-start.34 = (f32[32,12,1]{2,0,1:T(8,128)S(1)}, f32[32,12,1]{2,0,1:T(8,128)S(1)}, u32[]{:S(2)}, u32[]{:S(2)}) collective-permute-start(f32[32,12,1]{2,0,1:T(8,128)S(1)} %get-tuple-element.626), channel_id=1, source_target_pairs={{0,1},{1,2},{2,3},{3,4},{4,5},{5,6},{6,7},{7,8},{8,9},{9,10},{10,1... | collective-permute-start | bytes 4616 | tf_op jit(solution)/shard_map/ppermute | solution.py:23
  227.4 4.7 collective-permute-start.36
  233.6 5.5 %collective-permute-start.52 = (f32[32,1,130]{2,0,1:T(8,128)S(1)}, f32[32,1,130]{2,0,1:T(8,128)S(1)}, u32[]{:S(2)}, u32[]{:S(2)}) collective-permute-start(f32[32,1,130]{2,0,1:T(8,128)S(1)} %get-tuple-element.627), channel_id=1, source_target_pairs={{0,16},{16,32},{32,48},{48,64},{64,80},{80,96},{96,112},{1,17},{17... | collective-permute-start | bytes 49928 | tf_op jit(solution)/shard_map/ppermute | solution.py:23
  250.7 4.3 collective-permute-done.39
  260.8 5.7 %collective-permute-start.40 = (f32[32,1,130]{2,0,1:T(8,128)S(1)}, f32[32,1,130]{2,0,1:T(8,128)S(1)}, u32[]{:S(2)}, u32[]{:S(2)}) collective-permute-start(f32[32,1,130]{2,0,1:T(8,128)S(1)} %get-tuple-element.633), channel_id=1, source_target_pairs={{0,16},{16,32},{32,48},{48,64},{64,80},{80,96},{96,112},{1,17},{17... | collective-permute-start | bytes 49928 | tf_op jit(solution)/shard_map/ppermute | solution.py:23
  268.5 4.3 collective-permute-start.54
  274.2 4.7 collective-permute-start.42
  289.6 5.8 %collective-permute-start.44 = (f32[32,1,130]{2,0,1:T(8,128)S(1)}, f32[32,1,130]{2,0,1:T(8,128)S(1)}, u32[]{:S(2)}, u32[]{:S(2)}) collective-permute-start(f32[32,1,130]{2,0,1:T(8,128)S(1)} %get-tuple-element.631), channel_id=1, source_target_pairs={{0,16},{16,32},{32,48},{48,64},{64,80},{80,96},{96,112},{1,17},{17... | collective-permute-start | bytes 49928 | tf_op jit(solution)/shard_map/ppermute | solution.py:23
  298.5 4.3 collective-permute-done.45
  316.9 5.8 %collective-permute-start.48 = (f32[32,1,130]{2,0,1:T(8,128)S(1)}, f32[32,1,130]{2,0,1:T(8,128)S(1)}, u32[]{:S(2)}, u32[]{:S(2)}) collective-permute-start(f32[32,1,130]{2,0,1:T(8,128)S(1)} %get-tuple-element.629), channel_id=1, source_target_pairs={{0,16},{16,32},{32,48},{48,64},{64,80},{80,96},{96,112},{1,17},{17... | collective-permute-start | bytes 49928 | tf_op jit(solution)/shard_map/ppermute | solution.py:23
  324.0 4.8 collective-permute-done.49
  340.9 30.8 %while.59 = (s32[]{:T(128)}, f32[2,64]{1,0:T(2,128)S(1)}, f32[32,8,128]{2,0,1:T(8,128)S(1)}, f32[32,8,128]{2,0,1:T(8,128)S(1)}, s32[32,8,128]{2,1,0:T(8,128)}, /*index=5*/s32[]{:T(128)}, s32[]{:T(128)}) while((s32[]{:T(128)}, f32[2,64]{1,0:T(2,128)S(1)}, f32[32,8,128]{2,0,1:T(8,128)S(1)}, f32[32,8,128]{2,0,1:T(8,128)S(1)}, ...), condition=%wide.region_5.6_spmd.clone, body=%wide.region_4.5_spmd.clone.sunk | while | flops 1640707 | bytes 37983 | solution.py:125
  371.7 124.7 %psum.7 = f32[2,64]{1,0:T(2,128)S(1)} all-reduce(f32[2,64]{1,0:T(2,128)S(1)} %get-tuple-element.471), channel_id=1, replica_groups=mesh['season'=4,'gx'=8,'gy'=16] {'season','gx','gy'}, use_global_device_ids=true, to_apply=%region_6.7 | all-reduce | flops 128 | bytes 1024 | tf_op jit(solution)/shard_map/psum | solution.py:215
  (550 shorter events, 205.3 us)
Async XLA Ops:
  30.5 23.4 %collective-permute-start.1 = (f32[32,1,128]{2,0,1:T(8,128)S(1)}, f32[32,1,128]{2,0,1:T(8,128)S(1)}, u32[]{:S(2)}, u32[]{:S(2)}) collective-permute-start(f32[32,1,128]{2,0,1:T(8,128)S(1)} %get-tuple-element.700), channel_id=1, source_target_pairs={{0,16},{16,32},{32,48},{48,64},{64,80},{80,96},{96,112},{1,17},{17... | collective-permute-start | bytes 49160 | tf_op jit(solution)/shard_map/ppermute | solution.py:23
  36.0 18.0 %collective-permute-start.3 = (f32[32,1,128]{2,0,1:T(8,128)S(1)}, f32[32,1,128]{2,0,1:T(8,128)S(1)}, u32[]{:S(2)}, u32[]{:S(2)}) collective-permute-start(f32[32,1,128]{2,0,1:T(8,128)S(1)} %get-tuple-element.701), channel_id=1, source_target_pairs={{16,0},{32,16},{48,32},{64,48},{80,64},{96,80},{112,96},{17,1},{33... | collective-permute-start | bytes 49160 | tf_op jit(solution)/shard_map/ppermute | solution.py:24
  37.3 21.6 %collective-permute-start.2 = (f32[32,1,128]{2,0,1:T(8,128)S(1)}, f32[32,1,128]{2,0,1:T(8,128)S(1)}, u32[]{:S(2)}, u32[]{:S(2)}) collective-permute-start(f32[32,1,128]{2,0,1:T(8,128)S(1)} %get-tuple-element.698), channel_id=1, source_target_pairs={{0,16},{16,32},{32,48},{48,64},{64,80},{80,96},{96,112},{1,17},{17... | collective-permute-start | bytes 49160 | tf_op jit(solution)/shard_map/ppermute | solution.py:23
  42.8 16.1 %collective-permute-start.4 = (f32[32,1,128]{2,0,1:T(8,128)S(1)}, f32[32,1,128]{2,0,1:T(8,128)S(1)}, u32[]{:S(2)}, u32[]{:S(2)}) collective-permute-start(f32[32,1,128]{2,0,1:T(8,128)S(1)} %get-tuple-element.699), channel_id=1, source_target_pairs={{16,0},{32,16},{48,32},{64,48},{80,64},{96,80},{112,96},{17,1},{33... | collective-permute-start | bytes 49160 | tf_op jit(solution)/shard_map/ppermute | solution.py:24
  44.2 53.9 %collective-permute-start = (f32[32,1,128]{2,0,1:T(8,128)S(1)}, f32[32,1,128]{2,0,1:T(8,128)S(1)}, u32[]{:S(2)}, u32[]{:S(2)}) collective-permute-start(f32[32,1,128]{2,0,1:T(8,128)S(1)} %get-tuple-element.697), channel_id=1, source_target_pairs={{0,16},{16,32},{32,48},{48,64},{64,80},{80,96},{96,112},{1,17},{17... | collective-permute-start | bytes 49160 | tf_op jit(solution)/shard_map/ppermute | solution.py:23
  54.1 22.8 %collective-permute-start.5 = (f32[32,10,1]{2,0,1:T(8,128)S(1)}, f32[32,10,1]{2,0,1:T(8,128)S(1)}, u32[]{:S(2)}, u32[]{:S(2)}) collective-permute-start(f32[32,10,1]{2,0,1:T(8,128)S(1)} %get-tuple-element.664), channel_id=1, source_target_pairs={{0,1},{1,2},{2,3},{3,4},{4,5},{5,6},{6,7},{7,8},{8,9},{9,10},{10,1... | collective-permute-start | bytes 3848 | tf_op jit(solution)/shard_map/ppermute | solution.py:23
  57.6 20.5 %collective-permute-start.7 = (f32[32,10,1]{2,0,1:T(8,128)S(1)}, f32[32,10,1]{2,0,1:T(8,128)S(1)}, u32[]{:S(2)}, u32[]{:S(2)}) collective-permute-start(f32[32,10,1]{2,0,1:T(8,128)S(1)} %get-tuple-element.663), channel_id=1, source_target_pairs={{1,0},{2,1},{3,2},{4,3},{5,4},{6,5},{7,6},{8,7},{9,8},{10,9},{11,1... | collective-permute-start | bytes 3848 | tf_op jit(solution)/shard_map/ppermute | solution.py:24
  59.1 19.1 %collective-permute-start.6 = (f32[32,10,1]{2,0,1:T(8,128)S(1)}, f32[32,10,1]{2,0,1:T(8,128)S(1)}, u32[]{:S(2)}, u32[]{:S(2)}) collective-permute-start(f32[32,10,1]{2,0,1:T(8,128)S(1)} %get-tuple-element.665), channel_id=1, source_target_pairs={{0,1},{1,2},{2,3},{3,4},{4,5},{5,6},{6,7},{7,8},{8,9},{9,10},{10,1... | collective-permute-start | bytes 3848 | tf_op jit(solution)/shard_map/ppermute | solution.py:23
  63.3 14.9 %collective-permute-start.8 = (f32[32,10,1]{2,0,1:T(8,128)S(1)}, f32[32,10,1]{2,0,1:T(8,128)S(1)}, u32[]{:S(2)}, u32[]{:S(2)}) collective-permute-start(f32[32,10,1]{2,0,1:T(8,128)S(1)} %get-tuple-element.666), channel_id=1, source_target_pairs={{1,0},{2,1},{3,2},{4,3},{5,4},{6,5},{7,6},{8,7},{9,8},{10,9},{11,1... | collective-permute-start | bytes 3848 | tf_op jit(solution)/shard_map/ppermute | solution.py:24
  76.9 48.0 %collective-permute-start.23 = (f32[32,1,128]{2,0,1:T(8,128)S(1)}, f32[32,1,128]{2,0,1:T(8,128)S(1)}, u32[]{:S(2)}, u32[]{:S(2)}) collective-permute-start(f32[32,1,128]{2,0,1:T(8,128)S(1)} %get-tuple-element.696), channel_id=1, source_target_pairs={{16,0},{32,16},{48,32},{64,48},{80,64},{96,80},{112,96},{17,1},{33... | collective-permute-start | bytes 49160 | tf_op jit(solution)/shard_map/ppermute | solution.py:24
  79.2 13.3 %collective-permute-start.10 = (f32[32,1,128]{2,0,1:T(8,128)S(1)}, f32[32,1,128]{2,0,1:T(8,128)S(1)}, u32[]{:S(2)}, u32[]{:S(2)}) collective-permute-start(f32[32,1,128]{2,0,1:T(8,128)S(1)} %get-tuple-element.695), channel_id=1, source_target_pairs={{16,0},{32,16},{48,32},{64,48},{80,64},{96,80},{112,96},{17,1},{33... | collective-permute-start | bytes 49160 | tf_op jit(solution)/shard_map/ppermute | solution.py:24
  80.5 13.3 %collective-permute-start.9 = (f32[32,1,128]{2,0,1:T(8,128)S(1)}, f32[32,1,128]{2,0,1:T(8,128)S(1)}, u32[]{:S(2)}, u32[]{:S(2)}) collective-permute-start(f32[32,1,128]{2,0,1:T(8,128)S(1)} %get-tuple-element.694), channel_id=1, source_target_pairs={{0,16},{16,32},{32,48},{48,64},{64,80},{80,96},{96,112},{1,17},{17... | collective-permute-start | bytes 49160 | tf_op jit(solution)/shard_map/ppermute | solution.py:23
  86.7 63.7 %collective-permute-start.22 = (f32[32,1,128]{2,0,1:T(8,128)S(1)}, f32[32,1,128]{2,0,1:T(8,128)S(1)}, u32[]{:S(2)}, u32[]{:S(2)}) collective-permute-start(f32[32,1,128]{2,0,1:T(8,128)S(1)} %get-tuple-element.702), channel_id=1, source_target_pairs={{0,16},{16,32},{32,48},{48,64},{64,80},{80,96},{96,112},{1,17},{17... | collective-permute-start | bytes 49160 | tf_op jit(solution)/shard_map/ppermute | solution.py:23
  92.5 59.3 %collective-permute-start.25 = (f32[32,1,128]{2,0,1:T(8,128)S(1)}, f32[32,1,128]{2,0,1:T(8,128)S(1)}, u32[]{:S(2)}, u32[]{:S(2)}) collective-permute-start(f32[32,1,128]{2,0,1:T(8,128)S(1)} %get-tuple-element.703), channel_id=1, source_target_pairs={{16,0},{32,16},{48,32},{64,48},{80,64},{96,80},{112,96},{17,1},{33... | collective-permute-start | bytes 49160 | tf_op jit(solution)/shard_map/ppermute | solution.py:24
  131.7 13.3 %collective-permute-start.17 = (f32[32,1,128]{2,0,1:T(8,128)S(1)}, f32[32,1,128]{2,0,1:T(8,128)S(1)}, u32[]{:S(2)}, u32[]{:S(2)}) collective-permute-start(f32[32,1,128]{2,0,1:T(8,128)S(1)} %get-tuple-element.690), channel_id=1, source_target_pairs={{0,16},{16,32},{32,48},{48,64},{64,80},{80,96},{96,112},{1,17},{17... | collective-permute-start | bytes 49160 | tf_op jit(solution)/shard_map/ppermute | solution.py:23
  137.5 8.8 %collective-permute-start.18 = (f32[32,1,128]{2,0,1:T(8,128)S(1)}, f32[32,1,128]{2,0,1:T(8,128)S(1)}, u32[]{:S(2)}, u32[]{:S(2)}) collective-permute-start(f32[32,1,128]{2,0,1:T(8,128)S(1)} %get-tuple-element.691), channel_id=1, source_target_pairs={{16,0},{32,16},{48,32},{64,48},{80,64},{96,80},{112,96},{17,1},{33... | collective-permute-start | bytes 49160 | tf_op jit(solution)/shard_map/ppermute | solution.py:24
  139.5 36.9 %collective-permute-start.26 = (f32[32,10,1]{2,0,1:T(8,128)S(1)}, f32[32,10,1]{2,0,1:T(8,128)}, u32[]{:S(2)}, u32[]{:S(2)}) collective-permute-start(f32[32,10,1]{2,0,1:T(8,128)S(1)} %get-tuple-element.659), channel_id=1, source_target_pairs={{0,1},{1,2},{2,3},{3,4},{4,5},{5,6},{6,7},{7,8},{8,9},{9,10},{10,1... | collective-permute-start | bytes 3848 | tf_op jit(solution)/shard_map/ppermute | solution.py:23
  145.0 45.9 %collective-permute-start.29 = (f32[32,10,1]{2,0,1:T(8,128)}, f32[32,10,1]{2,0,1:T(8,128)}, u32[]{:S(2)}, u32[]{:S(2)}) collective-permute-start(f32[32,10,1]{2,0,1:T(8,128)} %get-tuple-element.660), channel_id=1, source_target_pairs={{1,0},{2,1},{3,2},{4,3},{5,4},{6,5},{7,6},{8,7},{9,8},{10,9},{11,1... | collective-permute-start | bytes 3848 | tf_op jit(solution)/shard_map/ppermute | solution.py:24
  157.4 11.1 %collective-permute-start.21 = (f32[32,1,128]{2,0,1:T(8,128)S(1)}, f32[32,1,128]{2,0,1:T(8,128)S(1)}, u32[]{:S(2)}, u32[]{:S(2)}) collective-permute-start(f32[32,1,128]{2,0,1:T(8,128)S(1)} %get-tuple-element.688), channel_id=1, source_target_pairs={{0,16},{16,32},{32,48},{48,64},{64,80},{80,96},{96,112},{1,17},{17... | collective-permute-start | bytes 49160 | tf_op jit(solution)/shard_map/ppermute | solution.py:23
  165.0 25.9 %collective-permute-start.28 = (f32[32,10,1]{2,0,1:T(8,128)}, f32[32,10,1]{2,0,1:T(8,128)S(1)}, u32[]{:S(2)}, u32[]{:S(2)}) collective-permute-start(f32[32,10,1]{2,0,1:T(8,128)} %get-tuple-element.661), channel_id=1, source_target_pairs={{0,1},{1,2},{2,3},{3,4},{4,5},{5,6},{6,7},{7,8},{8,9},{9,10},{10,1... | collective-permute-start | bytes 3848 | tf_op jit(solution)/shard_map/ppermute | solution.py:23
  168.6 22.3 %collective-permute-start.31 = (f32[32,10,1]{2,0,1:T(8,128)}, f32[32,10,1]{2,0,1:T(8,128)S(1)}, u32[]{:S(2)}, u32[]{:S(2)}) collective-permute-start(f32[32,10,1]{2,0,1:T(8,128)} %get-tuple-element.662), channel_id=1, source_target_pairs={{1,0},{2,1},{3,2},{4,3},{5,4},{6,5},{7,6},{8,7},{9,8},{10,9},{11,1... | collective-permute-start | bytes 3848 | tf_op jit(solution)/shard_map/ppermute | solution.py:24
  171.3 19.6 %collective-permute-start.27 = (f32[32,10,1]{2,0,1:T(8,128)}, f32[32,10,1]{2,0,1:T(8,128)S(1)}, u32[]{:S(2)}, u32[]{:S(2)}) collective-permute-start(f32[32,10,1]{2,0,1:T(8,128)} %get-tuple-element.652), channel_id=1, source_target_pairs={{0,1},{1,2},{2,3},{3,4},{4,5},{5,6},{6,7},{7,8},{8,9},{9,10},{10,1... | collective-permute-start | bytes 3848 | tf_op jit(solution)/shard_map/ppermute | solution.py:23
  176.4 14.5 %collective-permute-start.30 = (f32[32,10,1]{2,0,1:T(8,128)}, f32[32,10,1]{2,0,1:T(8,128)}, u32[]{:S(2)}, u32[]{:S(2)}) collective-permute-start(f32[32,10,1]{2,0,1:T(8,128)} %get-tuple-element.651), channel_id=1, source_target_pairs={{1,0},{2,1},{3,2},{4,3},{5,4},{6,5},{7,6},{8,7},{9,8},{10,9},{11,1... | collective-permute-start | bytes 3848 | tf_op jit(solution)/shard_map/ppermute | solution.py:24
  210.1 7.8 %collective-permute-start.34 = (f32[32,12,1]{2,0,1:T(8,128)S(1)}, f32[32,12,1]{2,0,1:T(8,128)S(1)}, u32[]{:S(2)}, u32[]{:S(2)}) collective-permute-start(f32[32,12,1]{2,0,1:T(8,128)S(1)} %get-tuple-element.626), channel_id=1, source_target_pairs={{0,1},{1,2},{2,3},{3,4},{4,5},{5,6},{6,7},{7,8},{8,9},{9,10},{10,1... | collective-permute-start | bytes 4616 | tf_op jit(solution)/shard_map/ppermute | solution.py:23
  227.4 13.7 %collective-permute-start.36 = (f32[32,1,130]{2,0,1:T(8,128)S(1)}, f32[32,1,130]{2,0,1:T(8,128)S(1)}, u32[]{:S(2)}, u32[]{:S(2)}) collective-permute-start(f32[32,1,130]{2,0,1:T(8,128)S(1)} %get-tuple-element.635), channel_id=1, source_target_pairs={{0,16},{16,32},{32,48},{48,64},{64,80},{80,96},{96,112},{1,17},{17... | collective-permute-start | bytes 49928 | tf_op jit(solution)/shard_map/ppermute | solution.py:23
  232.2 9.0 %collective-permute-start.37 = (f32[32,1,130]{2,0,1:T(8,128)S(1)}, f32[32,1,130]{2,0,1:T(8,128)S(1)}, u32[]{:S(2)}, u32[]{:S(2)}) collective-permute-start(f32[32,1,130]{2,0,1:T(8,128)S(1)} %get-tuple-element.636), channel_id=1, source_target_pairs={{16,0},{32,16},{48,32},{64,48},{80,64},{96,80},{112,96},{17,1},{33... | collective-permute-start | bytes 49928 | tf_op jit(solution)/shard_map/ppermute | solution.py:24
  233.6 12.8 %collective-permute-start.52 = (f32[32,1,130]{2,0,1:T(8,128)S(1)}, f32[32,1,130]{2,0,1:T(8,128)S(1)}, u32[]{:S(2)}, u32[]{:S(2)}) collective-permute-start(f32[32,1,130]{2,0,1:T(8,128)S(1)} %get-tuple-element.627), channel_id=1, source_target_pairs={{0,16},{16,32},{32,48},{48,64},{64,80},{80,96},{96,112},{1,17},{17... | collective-permute-start | bytes 49928 | tf_op jit(solution)/shard_map/ppermute | solution.py:23
  247.1 7.9 %collective-permute-start.39 = (f32[32,12,1]{2,0,1:T(8,128)}, f32[32,12,1]{2,0,1:T(8,128)}, u32[]{:S(2)}, u32[]{:S(2)}) collective-permute-start(f32[32,12,1]{2,0,1:T(8,128)} %get-tuple-element.623), channel_id=1, source_target_pairs={{1,0},{2,1},{3,2},{4,3},{5,4},{6,5},{7,6},{8,7},{9,8},{10,9},{11,1... | collective-permute-start | bytes 4616 | tf_op jit(solution)/shard_map/ppermute | solution.py:24
  260.8 13.3 %collective-permute-start.40 = (f32[32,1,130]{2,0,1:T(8,128)S(1)}, f32[32,1,130]{2,0,1:T(8,128)S(1)}, u32[]{:S(2)}, u32[]{:S(2)}) collective-permute-start(f32[32,1,130]{2,0,1:T(8,128)S(1)} %get-tuple-element.633), channel_id=1, source_target_pairs={{0,16},{16,32},{32,48},{48,64},{64,80},{80,96},{96,112},{1,17},{17... | collective-permute-start | bytes 49928 | tf_op jit(solution)/shard_map/ppermute | solution.py:23
  268.5 10.4 %collective-permute-start.54 = (f32[32,12,1]{2,0,1:T(8,128)S(1)}, f32[32,12,1]{2,0,1:T(8,128)S(1)}, u32[]{:S(2)}, u32[]{:S(2)}) collective-permute-start(f32[32,12,1]{2,0,1:T(8,128)S(1)} %get-tuple-element.616), channel_id=1, source_target_pairs={{0,1},{1,2},{2,3},{3,4},{4,5},{5,6},{6,7},{7,8},{8,9},{9,10},{10,1... | collective-permute-start | bytes 4616 | tf_op jit(solution)/shard_map/ppermute | solution.py:23
  272.8 23.9 %collective-permute-start.55 = (f32[32,12,1]{2,0,1:T(8,128)}, f32[32,12,1]{2,0,1:T(8,128)}, u32[]{:S(2)}, u32[]{:S(2)}) collective-permute-start(f32[32,12,1]{2,0,1:T(8,128)} %get-tuple-element.615), channel_id=1, source_target_pairs={{1,0},{2,1},{3,2},{4,3},{5,4},{6,5},{7,6},{8,7},{9,8},{10,9},{11,1... | collective-permute-start | bytes 4616 | tf_op jit(solution)/shard_map/ppermute | solution.py:24
  289.6 8.8 %collective-permute-start.44 = (f32[32,1,130]{2,0,1:T(8,128)S(1)}, f32[32,1,130]{2,0,1:T(8,128)S(1)}, u32[]{:S(2)}, u32[]{:S(2)}) collective-permute-start(f32[32,1,130]{2,0,1:T(8,128)S(1)} %get-tuple-element.631), channel_id=1, source_target_pairs={{0,16},{16,32},{32,48},{48,64},{64,80},{80,96},{96,112},{1,17},{17... | collective-permute-start | bytes 49928 | tf_op jit(solution)/shard_map/ppermute | solution.py:23
  (103 other events, 523.7 us)
where the time goes:
time: 502 us; the launch traced here: 498 us
  starting transfers between devices  173 us (34%)
  blocking collectives  125 us (25%)
  local copies, waits for them, and re-layouts  76.1 us (15%)
  waiting for transfers between devices  58.6 us (12%)
  other arithmetic  48.1 us (10%)
  matrix products  12.7 us (3%)
    ppermute x28, starting transfers between devices, padded(): before = lax.ppermute(last, axis, up)  137 us
    psum x1, blocking collectives, body(): totals = lax.psum(partial_totals, ('season', 'gx', 'gy'))  125 us
    ppermute x28, waiting for transfers between devices, padded(): after = lax.ppermute(first, axis, down)  52.7 us
    ppermute x28, starting transfers between devices, padded(): after = lax.ppermute(first, axis, down)  36.3 us
    unnamed x6, other arithmetic  22.9 us
    eq x32, local copies, waits for them, and re-layouts, zone_one_layer(): labels[:, None] == zone_layer.reshape(-1)[None, :]  22.2 us
    eq x32, local copies, waits for them, and re-layouts, lookup_one_layer(): labels[:, None] == zone_layer.reshape(-1)[None, :]  22.1 us
    unnamed x168, local copies, waits for them, and re-layouts  18.8 us
  transfers between devices with their start and end apart: 56, of which 20 were waited for; matrix products, arithmetic and copies ran while one was open for 9% of the time, Pallas kernels for 0%

commit v1 on v0

v1 whole, which is shorter than its diff:
```python
import jax
import jax.numpy as jnp
from jax import lax
from jax.experimental import pallas as pl
from jax.experimental.pallas import tpu as pltpu
from jax.sharding import PartitionSpec as P

STORAGE = 0.5
CONDUCT = 0.1
SMOOTH = 0.01
TIME_STEP = 0.02
HEAT_GAIN = 10.0

NZ = 32
BX = 8
BY = 128
RAD = 10
WX = BX + 2 * RAD
WY = 2 * BY
OWN = RAD
SIDE = 31
FAR = 6
NWELL = 2048

VMEM = pl.BlockSpec(memory_space=pltpu.VMEM)
SMEM = pl.BlockSpec(memory_space=pltpu.SMEM)
PARAMS = pltpu.CompilerParams(vmem_limit_bytes=48 * 1024 * 1024)


def lanes(shape):
    return lax.broadcasted_iota(jnp.int32, shape, len(shape) - 1)


def rows_of(ref, x):
    return ref[pl.ds(x, NZ, stride=BX), :]


def roll(a, by, axis):
    return pltpu.roll(a, by % a.shape[axis], axis)


def edges_kernel(zone, press, temp, seen, right_o, left_o):
    lane = lanes((NZ, BY))
    for group in range(2):
        right = jnp.zeros((NZ, BY), jnp.float32)
        left = jnp.zeros((NZ, BY), jnp.float32)
        for j in range(4):
            x = 4 * group + j
            p = rows_of(press, x)
            z = (rows_of(zone, x) + 1).astype(jnp.float32)
            t = rows_of(temp, x)
            o = rows_of(seen, x)
            c = jnp.where(lane >= 118, p, roll(z, -10, 1))
            c = jnp.where(lane >= 108, c, roll(t, -20, 1))
            c = jnp.where(lane >= 102, c, roll(o, -26, 1))
            c = roll(c, -32 * j, 1)
            right = jnp.where(lane // 32 == 3 - j, c, right)
            e = jnp.where(lane < 10, p, roll(z, 10, 1))
            e = jnp.where(lane < 20, e, roll(t, 20, 1))
            e = jnp.where(lane < 26, e, roll(o, 26, 1))
            e = roll(e, 32 * j, 1)
            left = jnp.where(lane // 32 == j, e, left)
        right_o[group] = right
        left_o[group] = left


def sides_kernel(zone, press, temp, seen, left, right, up_o, down_o, up2_o, down2_o):
    for x in range(BX):
        p = rows_of(press, x)
        z = (rows_of(zone, x) + 1).astype(jnp.float32)
        t = rows_of(temp, x)
        o = rows_of(seen, x)
        up_o[x] = p
        down_o[x] = p
        up_o[8 + x] = z
        down_o[8 + x] = z
        if x >= 2:
            up_o[14 + x] = t
        if x < 6:
            down_o[16 + x] = t
        if x >= 3:
            up_o[19 + x] = o
        if x < 5:
            down_o[22 + x] = o
        if x >= 6:
            up2_o[x - 6] = p
            up2_o[x - 4] = z
        if x < 2:
            down2_o[x] = p
            down2_o[x + 2] = z
    for g in range(2):
        up_o[27 + g] = left[g]
        up_o[29 + g] = right[g]
        down_o[27 + g] = left[g]
        down_o[29 + g] = right[g]
    up2_o[4] = left[1]
    up2_o[5] = right[1]
    down2_o[4] = left[0]
    down2_o[5] = right[0]


def wells_kernel(grid_rows, grid_cols, where_ref, cells, flow, plan, inject, q_o, h_o, hit, val):
    cell = cells[...]
    layer = cell // (grid_rows * grid_cols)
    x = cell // grid_cols % grid_rows - (where_ref[0] - RAD)
    y = cell % grid_cols - where_ref[1]
    ok = (x >= 0) & (x < WX) & (y >= -RAD) & (y < BY + RAD)
    spot = jnp.where(ok, x * NZ + layer, -1)
    lane = jnp.where(y < 0, y + WY, y)
    rate = plan[...].astype(jnp.float32) * flow[...]
    warm = jnp.maximum(rate, 0.0) * inject[...]
    across = lax.broadcasted_iota(jnp.int32, (WY, NWELL), 0) == lane
    for i, field in enumerate((rate, warm)):
        high = field.astype(jnp.bfloat16).astype(jnp.float32)
        low = field - high
        val[2 * i] = jnp.where(across, high, 0.0).astype(jnp.bfloat16)
        val[2 * i + 1] = jnp.where(across, low, 0.0).astype(jnp.bfloat16)
    for part in range(4):
        size = WX * NZ // 4
        index = lax.broadcasted_iota(jnp.int32, (size, NWELL), 0) + part * size
        hit[pl.ds(part * size, size), :] = jnp.where(index == spot, 1.0, 0.0).astype(jnp.bfloat16)

    @pl.loop(0, 4)
    def _(part):
        size = WX * NZ // 4
        mine = hit[pl.ds(pl.multiple_of(part * size, 32), size), :]
        for i, out in enumerate((q_o, h_o)):
            total = jnp.zeros((size, WY), jnp.float32)
            for half in range(2):
                total = total + lax.dot_general(
                    mine,
                    val[2 * i + half],
                    (((1,), (1,)), ((), ())),
                    preferred_element_type=jnp.float32,
                )
            out[pl.ds(part * (WX // 4), WX // 4)] = total.reshape(WX // 4, NZ, WY)


def face(t, pi, pj, ti, tj, di, dj):
    dp = pi - pj
    u = t * dp
    v = u * u + SMOOTH
    inv = lax.rsqrt(v)
    speed = v * inv
    db = 0.5 * (di + dj)
    dt = ti - tj
    st = 0.5 * (ti + tj)
    flux = (CONDUCT + db * speed) * dt + u * st
    e = db * (u * inv) * dt + st
    return flux, e * t, e * dp, speed * dt


def main_kernel(
    zone, press, temp, seen, left, right, up, down, up2, down2, source, heat, table,
    temp_o, sens_o, sums_o,
    K, D, T, O, PR, TX, TY, TZ, R, M, MU, W,
    AX, AY, AZ, AB, BXX, BYY, BZZ, BBB, CXX, CYY, CZZ, CBB, SP, SD, PART,
):
    lane = lanes((NZ, BY))
    zi = lax.broadcasted_iota(jnp.int32, (NZ, WY), 0)
    top = zi == NZ - 1
    bottom = zi == 0
    perm_table = jnp.broadcast_to(table[0:1], (NZ, BY))
    disp_table = jnp.broadcast_to(table[1:2], (NZ, BY))

    def look(tab, index):
        return jnp.take_along_axis(tab, index, axis=1, mode="promise_in_bounds")

    def ahead(a):
        return roll(a, -1, 1)

    def behind(a):
        return roll(a, 1, 1)

    def above(a):
        return roll(a, -1, 0)

    def below(a):
        return roll(a, 1, 0)

    for r in range(WX):
        t = o = None
        if r < 2:
            p, z, cl, cr, j = up2[r], up2[2 + r], up2[4], up2[5], r + 6
        elif r < 10:
            j = r - 2
            p, z, cl, cr = up[j], up[8 + j], up[27 + j // 4], up[29 + j // 4]
            if j >= 2:
                t = up[14 + j]
            if j >= 3:
                o = up[19 + j]
        elif r < 18:
            j = r - 10
            p, z, cl, cr = rows_of(press, j), rows_of(zone, j) + 1, left[j // 4], right[j // 4]
            t, o = rows_of(temp, j), rows_of(seen, j)
        elif r < 26:
            j = r - 18
            p, z, cl, cr = down[j], down[8 + j], down[27 + j // 4], down[29 + j // 4]
            if j < 6:
                t = down[16 + j]
            if j < 5:
                o = down[22 + j]
        else:
            j = r - 26
            p, z, cl, cr = down2[j], down2[2 + j], down2[4], down2[5]
        cl = roll(cl, 32 * (j % 4), 1)
        cr = roll(cr, -32 * (j % 4), 1)
        PR[0, r, :, 0:BY] = p
        PR[0, r, :, BY:WY] = jnp.where(lane >= 118, cl, jnp.where(lane < 10, cr, 0.0))
        z = z.astype(jnp.int32)
        zh = jnp.where(lane >= 118, roll(cl, 10, 1), jnp.where(lane < 10, roll(cr, -10, 1), 0.0))
        zh = zh.astype(jnp.int32)
        K[r, :, 0:BY] = look(perm_table, z)
        K[r, :, BY:WY] = look(perm_table, zh)
        if 4 <= r < 24:
            D[r, :, 0:BY] = look(disp_table, z)
            D[r, :, BY:WY] = look(disp_table, zh)
            T[r, :, 0:BY] = t
            T[r, :, BY:WY] = jnp.where(lane >= 122, roll(cl, 20, 1), jnp.where(lane < 6, roll(cr, -20, 1), 0.0))
        if 5 <= r < 23:
            O[r, :, 0:BY] = o
            O[r, :, BY:WY] = jnp.where(lane >= 123, roll(cl, 26, 1), jnp.where(lane < 5, roll(cr, -26, 1), 0.0))

    TX[0] = 0.5 * (K[0] + K[1])

    def coefficients(x, carry):
        k = K[x]
        tx = 0.5 * (k + K[x + 1])
        ty = 0.5 * (k + ahead(k))
        half = 0.5 * k
        tz = jnp.where(top, 0.0, half + above(half))
        total = STORAGE + TX[x - 1] + tx + ty + behind(ty) + tz + below(tz)
        total = total + jnp.where(top | bottom, half, 0.0)
        TX[x] = tx
        TY[x] = ty
        TZ[x] = tz
        R[x] = jnp.where(k > 0.0, 1.0 / total, 0.0)
        return carry

    lax.fori_loop(1, WX - 1, coefficients, 0)

    def spread(ref, x):
        a = ref[x]
        ty, tz = TY[x], TZ[x]
        return (
            TX[x] * ref[x + 1]
            + TX[x - 1] * ref[x - 1]
            + ty * ahead(a)
            + behind(ty * a)
            + tz * above(a)
            + below(tz * a)
        )

    for s in range(1, 5):

        def sweep(x, carry, s=s):
            PR[s, x] = (source[x] + spread(PR.at[s - 1], x)) * R[x]
            return carry

        lax.fori_loop(s, WX - s, sweep, 0)

    PE = PR.at[4]

    def face_x(x):
        return face(TX[x], PE[x], PE[x + 1], T[x], T[x + 1], D[x], D[x + 1])

    def transport(keep):
        def step(x, before):
            t, p, d = T[x], PE[x], D[x]
            fx, ax, bx, cx = face_x(x)
            fy, ay, by, cy = face(TY[x], p, ahead(p), t, ahead(t), d, ahead(d))
            half = 0.5 * K[x]
            tz = TZ[x] + jnp.where(top, half, 0.0)

            def over(a):
                return jnp.where(top, 0.0, above(a))

            fz, az, bz, cz = face(tz, p, over(p), t, over(t), d, over(d))
            fb, ab, bb, cb = face(half[0:8], p[0:8], 0.0, t[0:8], 0.0, d[0:8], 0.0)
            fall = jnp.concatenate([-fb, jnp.zeros((NZ - 8, WY), jnp.float32)], axis=0)
            out = fx - before + fy - behind(fy) + fz - jnp.where(bottom, fall, below(fz))
            end = t + TIME_STEP * (HEAT_GAIN * heat[x] - out)
            M[x] = jnp.where(R[x] > 0.0, (-TIME_STEP) * (end - O[x]), 0.0)
            AX[x], AY[x], AZ[x], AB[x] = ax, ay, az, ab
            if keep:
                BXX[x], BYY[x], BZZ[x], BBB[x] = bx, by, bz, bb
                CXX[x], CYY[x], CZZ[x], CBB[x] = cx, cy, cz, cb
                SP[x - 9] = end[:, 0:BY]
            return fx

        return step

    first = face_x(4)[0]
    first = lax.fori_loop(5, 9, transport(False), first)
    first = lax.fori_loop(9, 18, transport(True), first)
    lax.fori_loop(18, 23, transport(False), first)
    for x in range(BX):
        temp_o[pl.ds(x, NZ, stride=BX), :] = SP[x + 1]

    def lift(a, b8):
        wide = jnp.concatenate([b8, jnp.zeros((NZ - 8, WY), jnp.float32)], axis=0)
        return jnp.where(bottom, wide, a)

    def pull_press(x, before):
        m = M[x]
        gx = (m - M[x + 1]) * AX[x]
        gy = (m - ahead(m)) * AY[x]
        gz = (m - jnp.where(top, 0.0, above(m))) * AZ[x]
        gb = m[0:8] * AB[x]
        lam = gx - before + gy - behind(gy) + gz + lift(-below(gz), gb)
        MU[3, x] = lam * R[x]
        return gx

    lax.fori_loop(6, 22, pull_press, (M[5] - M[6]) * AX[5])

    for s in range(3, 0, -1):

        def sweep_back(x, carry, s=s):
            MU[s - 1, x] = spread(MU.at[s], x) * R[x]
            return carry

        lax.fori_loop(10 - s, 18 + s, sweep_back, 0)

    def products(x, carry):
        total = MU[0, x] * PR[1, x]
        for s in range(1, 4):
            total = total + MU[s, x] * PR[s + 1, x]
        W[x] = total
        return carry

    lax.fori_loop(9, 19, products, 0)

    def around(ref, x):
        a = ref[x]
        return (
            ref[x - 1]
            + ref[x + 1]
            + ahead(a)
            + behind(a)
            + jnp.where(top, 0.0, above(a))
            + jnp.where(bottom, 0.0, below(a))
        )

    def sensitivities(x, carry):
        m = M[x]
        gx = m - M[x + 1]
        gw = M[x - 1] - m
        gy = m - ahead(m)
        gz = m - jnp.where(top, 0.0, above(m))
        gb = m[0:8]

        def both(fx, fy, fz, fb):
            ay = gy * fy[x]
            az = gz * fz[x]
            return gx * fx[x] + gw * fx[x - 1] + ay + behind(ay) + az + lift(below(az), gb * fb[x])

        gk = both(BXX, BYY, BZZ, BBB)
        gd = both(CXX, CYY, CZZ, CBB)
        gk = gk - 6.0 * W[x] - around(W, x)
        for s in range(4):
            gk = gk + MU[s, x] * around(PR.at[s], x) + PR[s, x] * around(MU.at[s], x)
        SP[x - OWN] = (0.5 * gk * K[x])[:, 0:BY]
        SD[x - OWN] = (0.5 * gd * D[x])[:, 0:BY]
        return carry

    lax.fori_loop(OWN, OWN + BX, sensitivities, 0)
    for x in range(BX):
        sens_o[pl.ds(x, NZ, stride=BX), :] = SP[x]

    for x in range(BX):
        O[x, :, 0:BY] = rows_of(zone, x).astype(jnp.float32)

    def of_zone(z, carry):
        zf = z.astype(jnp.float32)
        total_p = jnp.zeros((NZ, BY), jnp.float32)
        total_d = jnp.zeros((NZ, BY), jnp.float32)
        for x in range(BX):
            here = O[x, :, 0:BY] == zf
            total_p = total_p + jnp.where(here, SP[x], 0.0)
            total_d = total_d + jnp.where(here, SD[x], 0.0)
        PART[z] = jnp.sum(total_p.reshape(4, 8, BY), axis=0)
        PART[z + 64] = jnp.sum(total_d.reshape(4, 8, BY), axis=0)
        return carry

    lax.fori_loop(0, 64, of_zone, 0)
    per_lane = jnp.sum(PART[...], axis=1)
    sums_o[...] = lax.dot_general(
        jnp.ones((8, BY), jnp.float32),
        per_lane,
        (((1,), (1,)), ((), ())),
        precision=lax.Precision.HIGHEST,
        preferred_element_type=jnp.float32,
    )


def shifted(array, axis, by):
    size = lax.axis_size(axis)
    pairs = [(i, i + by) for i in range(size) if 0 <= i + by < size]
    return lax.ppermute(array, axis, pairs)


def spread_sum(array, axis):
    size = lax.axis_size(axis)
    copies = jnp.broadcast_to(array[None], (size,) + array.shape)
    return lax.all_to_all(copies, axis, 0, 0).sum(0)


def f32(*shape):
    return jax.ShapeDtypeStruct(shape, jnp.float32)


def buf(*shape):
    return pltpu.VMEM(shape, jnp.float32)


def body(zone_ids, log_perm, log_disp, temp_start, pressure_start, temp_observed, well_cells, well_flow, plan, inject_temp):
    flat = (NZ * BX, BY)
    zone = zone_ids.reshape(flat)
    press = pressure_start.reshape(flat)
    temp = temp_start.reshape(flat)
    seen = temp_observed.reshape(flat)
    grid_rows = BX * lax.axis_size("gx")
    grid_cols = BY * lax.axis_size("gy")

    to_right, to_left = pl.pallas_call(
        edges_kernel,
        out_shape=(f32(2, NZ, BY), f32(2, NZ, BY)),
        in_specs=[VMEM] * 4,
        out_specs=(VMEM, VMEM),
        compiler_params=PARAMS,
        name="edges",
    )(zone, press, temp, seen)
    left = shifted(to_right, "gy", 1)
    right = shifted(to_left, "gy", -1)

    corner = jnp.stack([lax.axis_index("gx") * BX, lax.axis_index("gy") * BY]).astype(jnp.int32)
    source, heat = pl.pallas_call(
        lambda *refs: wells_kernel(grid_rows, grid_cols, *refs),
        out_shape=(f32(WX, NZ, WY), f32(WX, NZ, WY)),
        in_specs=[SMEM] + [VMEM] * 4,
        out_specs=(VMEM, VMEM),
        scratch_shapes=[pltpu.VMEM((WX * NZ, NWELL), jnp.bfloat16), pltpu.VMEM((4, WY, NWELL), jnp.bfloat16)],
        compiler_params=PARAMS,
        cost_estimate=pl.CostEstimate(flops=2 * 896 * 2048 * 1024, bytes_accessed=2 << 20, transcendentals=0),
        name="wells",
    )(corner, well_cells[None], well_flow[None], plan, inject_temp)

    to_up, to_down, to_up2, to_down2 = pl.pallas_call(
        sides_kernel,
        out_shape=(f32(SIDE, NZ, BY), f32(SIDE, NZ, BY), f32(FAR, NZ, BY), f32(FAR, NZ, BY)),
        in_specs=[VMEM] * 6,
        out_specs=(VMEM,) * 4,
        compiler_params=PARAMS,
        name="sides",
    )(zone, press, temp, seen, left, right)
    up = shifted(to_up, "gx", 1)
    down = shifted(to_down, "gx", -1)
    up2 = shifted(to_up2, "gx", 2)
    down2 = shifted(to_down2, "gx", -2)

    table = jnp.pad(jnp.exp(jnp.stack([log_perm, log_disp])), ((0, 6), (1, BY - 65)))
    temp_end, sens, sums = pl.pallas_call(
        main_kernel,
        out_shape=(f32(*flat), f32(*flat), f32(8, BY)),
        in_specs=[VMEM] * 13,
        out_specs=(VMEM,) * 3,
        scratch_shapes=[buf(WX, NZ, WY)] * 4
        + [buf(5, WX, NZ, WY)]
        + [buf(WX, NZ, WY)] * 5
        + [buf(4, WX, NZ, WY)]
        + [buf(WX, NZ, WY)]
        + ([buf(23, NZ, WY)] * 3 + [buf(23, 8, WY)]) * 3
        + [buf(9, NZ, BY), buf(9, NZ, BY), buf(128, 8, BY)],
        compiler_params=PARAMS,
        name="aquifer",
    )(zone, press, temp, seen, left, right, up, down, up2, down2, source, heat, table)

    totals = lax.psum(sums[0:1], "season")
    totals = spread_sum(totals, "gx")
    totals = spread_sum(totals, "gy")
    cells = lax.axis_size("season") * NZ * grid_rows * grid_cols
    gradient = totals.reshape(2, 64) * (cells / 64) ** (-0.5)
    return (temp_end.reshape(temp_start.shape), sens.reshape(temp_start.shape), gradient)


def solution(mesh):
    in_specs = (
        P(None, "gx", "gy"),
        P(),
        P(),
        P("season", None, "gx", "gy"),
        P("season", None, "gx", "gy"),
        P("season", None, "gx", "gy"),
        P(),
        P(),
        P("season", None),
        P("season", None),
    )
    out_specs = (P("season", None, "gx", "gy"), P("season", None, "gx", "gy"), P())
    return jax.shard_map(body, mesh=mesh, in_specs=in_specs, out_specs=out_specs, check_vma=False)
```

time: 502 us -> 123 us (0.25)
  starting transfers between devices: 173 us -> 17.8 us
  blocking collectives: 125 us -> 48.3 us
  local copies, waits for them, and re-layouts: 76.1 us -> 5.04 us
  waiting for transfers between devices: 58.6 us -> 9.22 us
  other arithmetic: 48.1 us -> 0.13 us
  Pallas kernels: 0 us -> 39.6 us
  matrix products: 12.7 us -> 0 us
    ppermute x56 -> x6, starting transfers between devices: 173 us -> 17.8 us  [shifted(): return lax.ppermute(array, axis, pairs)]
    psum x1, blocking collectives: 125 us -> 7.83 us  [body(): totals = lax.psum(sums[0:1], 'season')]
    ppermute x56 -> x6, waiting for transfers between devices: 58.6 us -> 9.22 us  [shifted(): return lax.ppermute(array, axis, pairs)]
    eq x64 -> x0, local copies, waits for them, and re-layouts: 44.3 us -> none  [the longest x32 22.2 us: zone_one_layer(): labels[:, None] == zone_layer.reshape(-1)[None, :]]
    all_to_all x0 -> x2, blocking collectives: none -> 40.4 us  [spread_sum(): return lax.all_to_all(copies, axis, 0, 0).sum(0)]
    pallas_call x0 -> x4, Pallas kernels: none -> 39.6 us  [the longest x1 31 us: body(): pl.pallas_call(main_kernel, out_shape=(f32(*flat), f32(*flat), f32(8, BY)...]
    unnamed x6 -> x0, other arithmetic: 22.9 us -> none
    unnamed x168 -> x28, local copies, waits for them, and re-layouts: 18.8 us -> 4.31 us
  transfers between devices with their start and end apart: 56 -> 6, of which waited for: 20 -> 3; matrix products, arithmetic and copies ran while one was open for 9% -> 0% of each run, Pallas kernels for 0% -> 6%
where the time goes in v1:
time: 123 us; the launch traced here: 121 us
  blocking collectives  48.3 us (39%)
  Pallas kernels  39.6 us (32%)
  starting transfers between devices  17.8 us (14%)
  waiting for transfers between devices  9.22 us (7%)
  local copies, waits for them, and re-layouts  5.04 us (4%)
    all_to_all x2, blocking collectives, spread_sum(): return lax.all_to_all(copies, axis, 0, 0).sum(0)  40.4 us
    pallas_call x1, Pallas kernels, body(): pl.pallas_call(main_kernel, out_shape=(f32(*flat), f32(*flat), f32(8, BY)...  31 us
    ppermute x6, starting transfers between devices, shifted(): return lax.ppermute(array, axis, pairs)  17.8 us
    ppermute x6, waiting for transfers between devices, shifted(): return lax.ppermute(array, axis, pairs)  9.22 us
    psum x1, blocking collectives, body(): totals = lax.psum(sums[0:1], 'season')  7.83 us
    pallas_call x1, Pallas kernels, body(): pl.pallas_call(lambda *refs: wells_kernel(grid_rows, grid_cols, *refs), o...  7.68 us
    unnamed x28, local copies, waits for them, and re-layouts  4.31 us
  transfers between devices with their start and end apart: 6, of which 3 were waited for; matrix products, arithmetic and copies ran while one was open for 0% of the time, Pallas kernels for 6%

profile of v1, /device:TPU:1, one launch (start us, length us, event | category | flops | bytes accessed | tf_op | source)
XLA Modules:
  0.0 120.9 jit_solution(1824521338214195327)
XLA Ops:
  0.6 0.9 copy-done
  1.5 0.9 copy-done.2
  2.4 0.9 copy-done.4
  3.3 0.9 copy-done.6
  4.3 0.7 edges.1
  5.0 4.4 %collective-permute-start = (f32[2,32,128]{2,1,0:T(8,128)S(1)}, f32[2,32,128]{2,1,0:T(8,128)S(1)}, u32[]{:S(2)}, u32[]{:S(2)}) collective-permute-start(f32[2,32,128]{2,1,0:T(8,128)S(1)} %get-tuple-element.14), channel_id=1, source_target_pairs={{0,1},{1,2},{2,3},{3,4},{4,5},{5,6},{6,7},{7,8},{8,9},{9,10},{10,1... | collective-permute-start | bytes 98312 | tf_op jit(solution)/shard_map/ppermute | solution.py:399
  9.4 1.3 %collective-permute-start.1 = (f32[2,32,128]{2,1,0:T(8,128)S(1)}, f32[2,32,128]{2,1,0:T(8,128)S(1)}, u32[]{:S(2)}, u32[]{:S(2)}) collective-permute-start(f32[2,32,128]{2,1,0:T(8,128)S(1)} %get-tuple-element.15), channel_id=1, source_target_pairs={{1,0},{2,1},{3,2},{4,3},{5,4},{6,5},{7,6},{8,7},{9,8},{10,9},{11,1... | collective-permute-start | bytes 98312 | tf_op jit(solution)/shard_map/ppermute | solution.py:399
  10.7 0.0 collective-permute-done.left
  10.7 3.5 %collective-permute-done.1.right = f32[2,32,128]{2,1,0:T(8,128)S(1)} collective-permute-done((f32[2,32,128]{2,1,0:T(8,128)S(1)}, f32[2,32,128]{2,1,0:T(8,128)S(1)}, u32[]{:S(2)}, u32[]{:S(2)}) %collective-permute-start.1) | collective-permute-done | bytes 32800 | tf_op jit(solution)/shard_map/ppermute | solution.py:399
  14.2 0.0 copy-start.9
  14.3 0.0 copy-start.10
  14.3 0.0 copy-start.11
  14.3 0.1 sides.1
  14.4 0.0 copy-start.8
  14.4 4.7 %collective-permute-start.2 = (f32[31,32,128]{2,1,0:T(8,128)S(1)}, f32[31,32,128]{2,1,0:T(8,128)S(1)}, u32[]{:S(2)}, u32[]{:S(2)}) collective-permute-start(f32[31,32,128]{2,1,0:T(8,128)S(1)} %get-tuple-element.16), channel_id=1, source_target_pairs={{0,16},{16,32},{32,48},{48,64},{64,80},{80,96},{96,112},{1,17},{17... | collective-permute-start | bytes 1523720 | tf_op jit(solution)/shard_map/ppermute | solution.py:399
  19.1 1.3 %collective-permute-start.3 = (f32[31,32,128]{2,1,0:T(8,128)S(1)}, f32[31,32,128]{2,1,0:T(8,128)S(1)}, u32[]{:S(2)}, u32[]{:S(2)}) collective-permute-start(f32[31,32,128]{2,1,0:T(8,128)S(1)} %get-tuple-element.17), channel_id=1, source_target_pairs={{16,0},{32,16},{48,32},{64,48},{80,64},{96,80},{112,96},{17,1},{33... | collective-permute-start | bytes 1523720 | tf_op jit(solution)/shard_map/ppermute | solution.py:399
  20.4 0.1 pad_add_fusion.refs_0_
  20.5 7.7 %wells.1 = (f32[28,32,256]{2,1,0:T(8,128)S(1)}, f32[28,32,256]{2,1,0:T(8,128)S(1)}) custom-call(s32[2]{0:T(128)S(1)} %pad_add_fusion.refs_0_, s32[1,2048]{1,0:T(1,128)S(1)} %bitcast.28, f32[1,2048]{1,0:T(1,128)S(1)} %bitcast.29, s32[1,2048]{1,0:T(1,128)S(1)} %copy-done.10, f32[1,2048]{1,0:T(1,128)S(1)} %copy-done.11), custom_call_target="tpu_custom_call" | custom-call | flops 3758096384 | bytes 2097152 | tf_op jit(solution)/shard_map/wells/pallas_call | solution.py:437
  28.2 4.9 %collective-permute-start.4 = (f32[6,32,128]{2,1,0:T(8,128)S(1)}, f32[6,32,128]{2,1,0:T(8,128)S(1)}, u32[]{:S(2)}, u32[]{:S(2)}) collective-permute-start(f32[6,32,128]{2,1,0:T(8,128)S(1)} %get-tuple-element.18), channel_id=1, source_target_pairs={{0,32},{16,48},{32,64},{48,80},{64,96},{80,112},{1,33},{17,49},{33... | collective-permute-start | bytes 294920 | tf_op jit(solution)/shard_map/ppermute | solution.py:399
  33.1 1.3 %collective-permute-start.5 = (f32[6,32,128]{2,1,0:T(8,128)S(1)}, f32[6,32,128]{2,1,0:T(8,128)S(1)}, u32[]{:S(2)}, u32[]{:S(2)}) collective-permute-start(f32[6,32,128]{2,1,0:T(8,128)S(1)} %get-tuple-element.19), channel_id=1, source_target_pairs={{32,0},{48,16},{64,32},{80,48},{96,64},{112,80},{33,1},{49,17},{65... | collective-permute-start | bytes 294920 | tf_op jit(solution)/shard_map/ppermute | solution.py:399
  34.4 0.0 copy-start.12
  34.4 0.0 copy-start.13
  34.4 0.6 copy-done.12
  35.1 0.0 copy-done.13
  35.1 0.1 pad.4.table
  35.2 3.6 %collective-permute-done.5.down2 = f32[6,32,128]{2,1,0:T(8,128)S(1)} collective-permute-done((f32[6,32,128]{2,1,0:T(8,128)S(1)}, f32[6,32,128]{2,1,0:T(8,128)S(1)}, u32[]{:S(2)}, u32[]{:S(2)}) %collective-permute-start.5) | collective-permute-done | bytes 98336 | tf_op jit(solution)/shard_map/ppermute | solution.py:399
  38.8 2.1 %collective-permute-done.3.down = f32[31,32,128]{2,1,0:T(8,128)S(1)} collective-permute-done((f32[31,32,128]{2,1,0:T(8,128)S(1)}, f32[31,32,128]{2,1,0:T(8,128)S(1)}, u32[]{:S(2)}, u32[]{:S(2)}) %collective-permute-start.3) | collective-permute-done | bytes 507936 | tf_op jit(solution)/shard_map/ppermute | solution.py:399
  40.9 31.0 %aquifer.1 = (f32[256,128]{1,0:T(8,128)}, f32[256,128]{1,0:T(8,128)}, f32[8,128]{1,0:T(8,128)S(1)}) custom-call(s32[256,128]{1,0:T(8,128)S(1)} %bitcast.18, f32[256,128]{1,0:T(8,128)S(1)} %bitcast.21, f32[256,128]{1,0:T(8,128)S(1)} %bitcast.24, f32[256,128]{1,0:T(8,128)S(1)} %bitcast.27, f32[2,32,128]{2,1,0:T(8,128)S(1)} %collective-permute-done.left, ...), custom_call_target="tpu_custom_call" | custom-call | tf_op jit(solution)/shard_map/aquifer/pallas_call | solution.py:462
  71.9 7.8 %psum.7 = f32[128]{0:T(128)S(1)} all-reduce(f32[128]{0:T(128)S(1)} %slice_bitcast_fusion), channel_id=1, replica_groups=mesh['season'=4,'gx'=8,'gy'=16] {'season'}, use_global_device_ids=true, to_apply=%region_0.1 | all-reduce | flops 128 | bytes 1024 | tf_op jit(solution)/shard_map/psum | solution.py:478
  79.7 14.8 %all_to_all.10 = f32[8,1,128]{2,1,0:T(1,128)S(1)} all-to-all(f32[8,1,128]{2,1,0:T(1,128)S(1)} %broadcast_in_dim.23), channel_id=1, replica_groups=mesh['season'=4,'gx'=8,'gy'=16] {'gx'}, dimensions={0} | all-to-all | bytes 8192 | tf_op jit(solution)/shard_map/all_to_all | solution.py:405
  94.5 25.7 %all_to_all.11 = f32[16,1,128]{2,1,0:T(1,128)S(1)} all-to-all(f32[16,1,128]{2,1,0:T(1,128)S(1)} %broadcast_in_dim.24), channel_id=1, replica_groups=mesh['season'=4,'gx'=8,'gy'=16] {'gy'}, dimensions={0} | all-to-all | bytes 16384 | tf_op jit(solution)/shard_map/all_to_all | solution.py:405
  120.2 0.6 mul.19
  (25 shorter events, 0.1 us)
Async XLA Ops:
  0.6 0.9 copy-start
  1.5 0.9 copy-start.2
  2.4 0.9 copy-start.4
  3.3 0.9 copy-start.6
  4.3 10.0 %copy-start.1 = (s32[32,8,128]{2,1,0:T(8,128)S(1)}, s32[32,8,128]{2,1,0:T(8,128)}, u32[]{:S(2)}) copy-start(s32[32,8,128]{2,1,0:T(8,128)} %param.10) | copy-start | bytes 393220
  4.3 10.0 %copy-start.3 = (f32[1,32,8,128]{3,2,1,0:T(8,128)S(1)}, f32[1,32,8,128]{3,2,1,0:T(8,128)}, u32[]{:S(2)}) copy-start(f32[1,32,8,128]{3,2,1,0:T(8,128)} %param.14) | copy-start | bytes 393220
  4.3 10.0 %copy-start.5 = (f32[1,32,8,128]{3,2,1,0:T(8,128)S(1)}, f32[1,32,8,128]{3,2,1,0:T(8,128)}, u32[]{:S(2)}) copy-start(f32[1,32,8,128]{3,2,1,0:T(8,128)} %param.13) | copy-start | bytes 393220
  4.3 10.0 %copy-start.7 = (f32[1,32,8,128]{3,2,1,0:T(8,128)S(1)}, f32[1,32,8,128]{3,2,1,0:T(8,128)}, u32[]{:S(2)}) copy-start(f32[1,32,8,128]{3,2,1,0:T(8,128)} %param.15) | copy-start | bytes 393220
  5.0 5.7 %collective-permute-start = (f32[2,32,128]{2,1,0:T(8,128)S(1)}, f32[2,32,128]{2,1,0:T(8,128)S(1)}, u32[]{:S(2)}, u32[]{:S(2)}) collective-permute-start(f32[2,32,128]{2,1,0:T(8,128)S(1)} %get-tuple-element.14), channel_id=1, source_target_pairs={{0,1},{1,2},{2,3},{3,4},{4,5},{5,6},{6,7},{7,8},{8,9},{9,10},{10,1... | collective-permute-start | bytes 98312 | tf_op jit(solution)/shard_map/ppermute | solution.py:399
  9.4 4.8 %collective-permute-start.1 = (f32[2,32,128]{2,1,0:T(8,128)S(1)}, f32[2,32,128]{2,1,0:T(8,128)S(1)}, u32[]{:S(2)}, u32[]{:S(2)}) collective-permute-start(f32[2,32,128]{2,1,0:T(8,128)S(1)} %get-tuple-element.15), channel_id=1, source_target_pairs={{1,0},{2,1},{3,2},{4,3},{5,4},{6,5},{7,6},{8,7},{9,8},{10,9},{11,1... | collective-permute-start | bytes 98312 | tf_op jit(solution)/shard_map/ppermute | solution.py:399
  14.2 6.2 %copy-start.9 = (f32[2048]{0:T(1024)S(1)}, f32[2048]{0:T(1024)}, u32[]{:S(2)}) copy-start(f32[2048]{0:T(1024)} %param.17) | copy-start | bytes 24580
  14.3 6.2 %copy-start.10 = (s32[1,2048]{1,0:T(1,128)S(1)}, s32[1,2048]{1,0:T(1,128)}, u32[]{:S(2)}) copy-start(s32[1,2048]{1,0:T(1,128)} %refs_3_.1) | copy-start | bytes 24580
  14.3 6.2 %copy-start.11 = (f32[1,2048]{1,0:T(1,128)S(1)}, f32[1,2048]{1,0:T(1,128)}, u32[]{:S(2)}) copy-start(f32[1,2048]{1,0:T(1,128)} %refs_4_.1) | copy-start | bytes 24580
  14.4 6.1 %copy-start.8 = (s32[2048]{0:T(1024)S(1)}, s32[2048]{0:T(1024)}, u32[]{:S(2)}) copy-start(s32[2048]{0:T(1024)} %param.16) | copy-start | bytes 24580
  14.4 24.3 %collective-permute-start.2 = (f32[31,32,128]{2,1,0:T(8,128)S(1)}, f32[31,32,128]{2,1,0:T(8,128)S(1)}, u32[]{:S(2)}, u32[]{:S(2)}) collective-permute-start(f32[31,32,128]{2,1,0:T(8,128)S(1)} %get-tuple-element.16), channel_id=1, source_target_pairs={{0,16},{16,32},{32,48},{48,64},{64,80},{80,96},{96,112},{1,17},{17... | collective-permute-start | bytes 1523720 | tf_op jit(solution)/shard_map/ppermute | solution.py:399
  19.1 21.8 %collective-permute-start.3 = (f32[31,32,128]{2,1,0:T(8,128)S(1)}, f32[31,32,128]{2,1,0:T(8,128)S(1)}, u32[]{:S(2)}, u32[]{:S(2)}) collective-permute-start(f32[31,32,128]{2,1,0:T(8,128)S(1)} %get-tuple-element.17), channel_id=1, source_target_pairs={{16,0},{32,16},{48,32},{64,48},{80,64},{96,80},{112,96},{17,1},{33... | collective-permute-start | bytes 1523720 | tf_op jit(solution)/shard_map/ppermute | solution.py:399
  28.2 7.0 %collective-permute-start.4 = (f32[6,32,128]{2,1,0:T(8,128)S(1)}, f32[6,32,128]{2,1,0:T(8,128)S(1)}, u32[]{:S(2)}, u32[]{:S(2)}) collective-permute-start(f32[6,32,128]{2,1,0:T(8,128)S(1)} %get-tuple-element.18), channel_id=1, source_target_pairs={{0,32},{16,48},{32,64},{48,80},{64,96},{80,112},{1,33},{17,49},{33... | collective-permute-start | bytes 294920 | tf_op jit(solution)/shard_map/ppermute | solution.py:399
  33.1 5.7 %collective-permute-start.5 = (f32[6,32,128]{2,1,0:T(8,128)S(1)}, f32[6,32,128]{2,1,0:T(8,128)S(1)}, u32[]{:S(2)}, u32[]{:S(2)}) collective-permute-start(f32[6,32,128]{2,1,0:T(8,128)S(1)} %get-tuple-element.19), channel_id=1, source_target_pairs={{32,0},{48,16},{64,32},{80,48},{96,64},{112,80},{33,1},{49,17},{65... | collective-permute-start | bytes 294920 | tf_op jit(solution)/shard_map/ppermute | solution.py:399
  34.4 0.7 copy-start.12
  34.4 0.7 copy-start.13

commit v2 on v1

v2 whole, which is shorter than its diff:
```python
import jax
import jax.numpy as jnp
from jax import lax
from jax.experimental import pallas as pl
from jax.experimental.pallas import tpu as pltpu
from jax.sharding import PartitionSpec as P

STORAGE = 0.5
CONDUCT = 0.1
SMOOTH = 0.01
TIME_STEP = 0.02
HEAT_GAIN = 10.0

NZ = 32
BX = 8
BY = 128
RAD = 10
WX = BX + 2 * RAD
WY = 2 * BY
OWN = RAD
SIDE = 27
FAR = 5
PAIR = 62
PRESS, ZONE, TEMP, SEEN = (0, 10), (20, 10), (36, 6), (47, 5)
NWELL = 2048
PICK = 256

VMEM = pl.BlockSpec(memory_space=pltpu.VMEM)
SMEM = pl.BlockSpec(memory_space=pltpu.SMEM)
FULL = pltpu.CompilerParams(vmem_limit_bytes=60 * 1024 * 1024)
PARAMS = pltpu.CompilerParams(vmem_limit_bytes=48 * 1024 * 1024)


def lanes(shape):
    return lax.broadcasted_iota(jnp.int32, shape, len(shape) - 1)


def rows_of(ref, x):
    return jnp.concatenate([ref[pl.ds(x + BX * v, 8, stride=4 * BX), :] for v in range(4)], axis=0)


def put_rows(ref, x, value):
    for v in range(4):
        ref[pl.ds(x + BX * v, 8, stride=4 * BX), :] = value[8 * v : 8 * v + 8]


def roll(a, by, axis):
    return pltpu.roll(a, by % a.shape[axis], axis)


def between(lane, low, high):
    if low < 0:
        return (lane >= low + BY) | (lane < high)
    return (lane >= low) & (lane < high)


def pack_rows_kernel(zone, press, temp, seen, up_o, down_o):
    for x in range(BX):
        p = rows_of(press, x)
        z = (rows_of(zone, x) + 1).astype(jnp.float32)
        t = rows_of(temp, x)
        o = rows_of(seen, x)
        up_o[x] = p
        down_o[x] = p
        up_o[8 + x] = z
        down_o[8 + x] = z
        if x >= 2:
            up_o[14 + x] = t
        if x < 6:
            down_o[16 + x] = t
        if x >= 3:
            up_o[19 + x] = o
        if x < 5:
            down_o[22 + x] = o


def pack_columns_kernel(zone, press, temp, seen, after, right_o, left_o):
    lane = lanes((NZ, BY))
    for x in range(BX):
        p = rows_of(press, x)
        z = (rows_of(zone, x) + 1).astype(jnp.float32)
        t = rows_of(temp, x)
        o = rows_of(seen, x)
        if x % 2 == 0:
            right = left = jnp.zeros((NZ, BY), jnp.float32)
        for field, (spot, reach) in ((p, PRESS), (z, ZONE), (t, TEMP), (o, SEEN)):
            spot = spot + PAIR * (x % 2)
            moved = roll(field, spot, 1) if spot else field
            start = spot - reach if spot else BY - reach
            right = jnp.where(between(lane, start, start + reach), moved, right)
            left = jnp.where(between(lane, spot, spot + reach), moved, left)
        right_o[x // 2] = right
        left_o[x // 2] = left


def corner_kernel(zone, press, left, right, after, edge_o, up2_o, down2_o):
    for i in range(BX // 2):
        edge_o[i] = left[i] + right[i]
    for i in range(2):
        up2_o[i] = rows_of(press, BX - 2 + i)
        up2_o[2 + i] = (rows_of(zone, BX - 2 + i) + 1).astype(jnp.float32)
        down2_o[i] = rows_of(press, i)
        down2_o[2 + i] = (rows_of(zone, i) + 1).astype(jnp.float32)
    up2_o[4] = left[3] + right[3]
    down2_o[4] = left[0] + right[0]


def wells_kernel(grid_rows, grid_cols, where_ref, cells, flow, plan, inject, perm_logs, disp_logs, q_o, h_o, table_o):
    lane = lanes((1, BY))
    for i, logs in enumerate((perm_logs, disp_logs)):
        row = jnp.concatenate([jnp.exp(logs[...]), jnp.zeros((1, BY - 64), jnp.float32)], axis=1)
        table_o[i : i + 1, :] = roll(row, 1, 1)

    cell = cells[...]
    layer = cell // (grid_rows * grid_cols)
    layer = layer % 4 * 8 + layer // 4
    x = cell // grid_cols % grid_rows - (where_ref[0] - RAD)
    y = cell % grid_cols - where_ref[1]
    near = (x >= 0) & (x < WX) & (y >= -RAD) & (y < BY + RAD)
    near = jnp.where(near, 1.0, 0.0)
    rate = plan[...].astype(jnp.float32) * flow[...]
    warm = jnp.maximum(rate, 0.0) * inject[...]

    def halves(field):
        high = field.astype(jnp.bfloat16).astype(jnp.float32)
        return [high, field - high]

    place = [x.astype(jnp.float32), layer.astype(jnp.float32), jnp.where(y < 0, y + WY, y).astype(jnp.float32)]
    facts = jnp.concatenate(place + [near] + halves(rate) + halves(warm), axis=0).astype(jnp.bfloat16)

    chunks = [slice(c, c + PICK) for c in range(0, NWELL, PICK)]
    across = lax.broadcasted_iota(jnp.int32, (PICK, PICK), 1)
    down = lax.broadcasted_iota(jnp.int32, (PICK, PICK), 0)
    upto = jnp.where(down <= across, 1.0, 0.0).astype(jnp.bfloat16)
    marks = jnp.concatenate([near[:, c] for c in chunks], axis=0)
    counts = jnp.dot(marks.astype(jnp.bfloat16), upto, preferred_element_type=jnp.float32)
    before = jnp.zeros((1, 1), jnp.float32)
    number = []
    for i, c in enumerate(chunks):
        number.append(jnp.where(near[:, c] > 0.0, counts[i : i + 1] + (before - 1.0), -1.0).astype(jnp.int32))
        before = before + counts[i : i + 1, PICK - 1 : PICK]
    total = jnp.sum(near).astype(jnp.int32)

    def slab(start, first):
        picked = jnp.zeros((8, PICK), jnp.float32)
        for i, c in enumerate(chunks):
            chosen = jnp.where(down + start == number[i], 1.0, 0.0).astype(jnp.bfloat16)
            picked = picked + lax.dot_general(
                facts[:, c], chosen, (((1,), (1,)), ((), ())), preferred_element_type=jnp.float32
            )
        spot = jnp.where(picked[3:4] > 0.5, picked[0:1] * NZ + picked[1:2], -1.0).astype(jnp.int32)
        column = down == picked[2:3].astype(jnp.int32)
        for i, out in enumerate((q_o, h_o)):
            parts = [jnp.where(column, picked[4 + 2 * i + j : 5 + 2 * i + j], 0.0).astype(jnp.bfloat16) for j in range(2)]
            for x0, x1 in ((1, 14), (14, 27)) if i == 0 else ((5, 14), (14, 23)):
                index = lax.broadcasted_iota(jnp.int32, ((x1 - x0) * NZ, PICK), 0) + x0 * NZ
                hit = jnp.where(index == spot, 1.0, 0.0).astype(jnp.bfloat16)
                value = jnp.zeros(((x1 - x0) * NZ, WY), jnp.float32)
                for part in parts:
                    value = value + lax.dot_general(
                        hit, part, (((1,), (1,)), ((), ())), preferred_element_type=jnp.float32
                    )
                value = value.reshape(x1 - x0, NZ, WY)
                out[x0:x1] = value if first else out[x0:x1] + value

    slab(0, True)

    @pl.loop(1, (total + (PICK - 1)) // PICK)
    def _(i):
        slab(i * PICK, False)


def face(t, pi, pj, ti, tj, di, dj):
    dp = pi - pj
    u = t * dp
    v = u * u + SMOOTH
    inv = lax.rsqrt(v)
    speed = v * inv
    db = 0.5 * (di + dj)
    dt = ti - tj
    st = 0.5 * (ti + tj)
    flux = (CONDUCT + db * speed) * dt + u * st
    e = db * (u * inv) * dt + st
    return flux, e * t, e * dp, speed * dt


def main_kernel(
    zone, press, temp, seen, edge, up, down, edge_up, edge_down, up2, down2, source, heat, table,
    temp_o, sens_o, sums_o,
    K, D, T, O, P0, P1, P2, P3, P4, TX, TY, TZ, R, M, U0, U1, U2, U3, W,
    AX, AY, AZ, AB, BXX, BYY, BZZ, BBB, CXX, CYY, CZZ, CBB, SP, SD, PART,
):
    PR = (P0, P1, P2, P3, P4)
    MU = (U0, U1, U2, U3)
    lane = lanes((NZ, BY))
    zi = lax.broadcasted_iota(jnp.int32, (NZ, WY), 0)
    top = zi == NZ - 1
    bottom = zi == 0
    perm_table = jnp.broadcast_to(table[0:1], (NZ, BY))
    disp_table = jnp.broadcast_to(table[1:2], (NZ, BY))

    def look(tab, index):
        return jnp.take_along_axis(tab, index, axis=1, mode="promise_in_bounds")

    def ahead(a):
        return roll(a, -1, 1)

    def behind(a):
        return roll(a, 1, 1)

    def above(a):
        return jnp.concatenate([a[8:], roll(a[:8], -1, 0)], axis=0)

    def below(a):
        return jnp.concatenate([roll(a[24:], 1, 0), a[:24]], axis=0)

    def halo(packed, place, j):
        spot, reach = place
        spot = spot + PAIR * (j % 2)
        moved = roll(packed, -spot, 1) if spot else packed
        return jnp.where(between(lane, -reach, reach), moved, 0.0)

    zone_lanes = between(lane, 10, 30) | between(lane, 10 + PAIR, 30 + PAIR)

    def looked(packed):
        index = jnp.where(zone_lanes, packed, 0.0).astype(jnp.int32)
        return look(perm_table, index), look(disp_table, index)

    for r in range(0, WX, 2):
        if r < 2:
            packed = up2[4]
        elif r < 10:
            packed = edge_up[(r - 2) // 2]
        elif r < 18:
            packed = edge[(r - 10) // 2]
        elif r < 26:
            packed = edge_down[(r - 18) // 2]
        else:
            packed = down2[4]
        packed_k, packed_d = looked(packed)
        for r in (r, r + 1):
            t = o = None
            if r < 2:
                p, z = up2[r], up2[2 + r]
            elif r < 10:
                j = r - 2
                p, z = up[j], up[8 + j]
                t = up[14 + j] if j >= 2 else None
                o = up[19 + j] if j >= 3 else None
            elif r < 18:
                j = r - 10
                p, z = rows_of(press, j), rows_of(zone, j) + 1
                t, o = rows_of(temp, j), rows_of(seen, j)
            elif r < 26:
                j = r - 18
                p, z = down[j], down[8 + j]
                t = down[16 + j] if j < 6 else None
                o = down[22 + j] if j < 5 else None
            else:
                j = r - 26
                p, z = down2[j], down2[2 + j]
            z = z.astype(jnp.int32)
            PR[0][r, :, 0:BY] = p
            PR[0][r, :, BY:WY] = halo(packed, PRESS, r)
            K[r, :, 0:BY] = look(perm_table, z)
            K[r, :, BY:WY] = halo(packed_k, ZONE, r)
            if 4 <= r < 24:
                D[r, :, 0:BY] = look(disp_table, z)
                D[r, :, BY:WY] = halo(packed_d, ZONE, r)
                T[r, :, 0:BY] = t
                T[r, :, BY:WY] = halo(packed, TEMP, r)
            if 5 <= r < 23:
                O[r, :, 0:BY] = o
                O[r, :, BY:WY] = halo(packed, SEEN, r)

    def coefficients(x, before):
        k = K[x]
        tx = 0.5 * (k + K[x + 1])
        ty = 0.5 * (k + ahead(k))
        half = 0.5 * k
        tz = jnp.where(top, 0.0, half + above(half))
        total = STORAGE + before + tx + ty + behind(ty) + tz + below(tz)
        total = total + jnp.where(top | bottom, half, 0.0)
        TX[x] = tx
        TY[x] = ty
        TZ[x] = tz
        R[x] = jnp.where(k > 0.0, 1.0 / total, 0.0)
        return tx

    TX[0] = 0.5 * (K[0] + K[1])
    lax.fori_loop(1, WX - 1, coefficients, 0.5 * (K[0] + K[1]), unroll=13)

    def spread(ref, x):
        a = ref[x]
        ty, tz = TY[x], TZ[x]
        return (
            TX[x] * ref[x + 1]
            + TX[x - 1] * ref[x - 1]
            + ty * ahead(a)
            + behind(ty * a)
            + tz * above(a)
            + below(tz * a)
        )

    for s in range(1, 5):

        def sweep(x, carry, s=s):
            PR[s][x] = (source[x] + spread(PR[s - 1], x)) * R[x]
            return carry

        lax.fori_loop(s, WX - s, sweep, 0, unroll=True)

    PE = PR[4]

    def face_x(x):
        return face(TX[x], PE[x], PE[x + 1], T[x], T[x + 1], D[x], D[x + 1])

    def transport(keep):
        def step(x, before):
            t, p, d = T[x], PE[x], D[x]
            fx, ax, bx, cx = face_x(x)
            fy, ay, by, cy = face(TY[x], p, ahead(p), t, ahead(t), d, ahead(d))
            half = 0.5 * K[x]
            tz = TZ[x] + jnp.where(top, half, 0.0)

            def over(a):
                return jnp.where(top, 0.0, above(a))

            fz, az, bz, cz = face(tz, p, over(p), t, over(t), d, over(d))
            fb, ab, bb, cb = face(half[0:8], p[0:8], 0.0, t[0:8], 0.0, d[0:8], 0.0)
            fall = jnp.concatenate([-fb, jnp.zeros((NZ - 8, WY), jnp.float32)], axis=0)
            out = fx - before + fy - behind(fy) + fz - jnp.where(bottom, fall, below(fz))
            end = t + TIME_STEP * (HEAT_GAIN * heat[x] - out)
            M[x] = jnp.where(R[x] > 0.0, (-TIME_STEP) * (end - O[x]), 0.0)
            AX[x], AY[x], AZ[x], AB[x] = ax, ay, az, ab
            if keep:
                BXX[x], BYY[x], BZZ[x], BBB[x] = bx, by, bz, bb
                CXX[x], CYY[x], CZZ[x], CBB[x] = cx, cy, cz, cb
                SP[x - 9] = end[:, 0:BY]
            return fx

        return step

    first = face_x(4)[0]
    first = lax.fori_loop(5, 9, transport(False), first, unroll=True)
    first = lax.fori_loop(9, 18, transport(True), first, unroll=True)
    lax.fori_loop(18, 23, transport(False), first, unroll=True)
    for x in range(BX):
        put_rows(temp_o, x, SP[x + 1])

    def lift(a, b8):
        wide = jnp.concatenate([b8, jnp.zeros((NZ - 8, WY), jnp.float32)], axis=0)
        return jnp.where(bottom, wide, a)

    def pull_press(x, before):
        m = M[x]
        gx = (m - M[x + 1]) * AX[x]
        gy = (m - ahead(m)) * AY[x]
        gz = (m - jnp.where(top, 0.0, above(m))) * AZ[x]
        gb = m[0:8] * AB[x]
        lam = gx - before + gy - behind(gy) + gz + lift(-below(gz), gb)
        MU[3][x] = lam * R[x]
        return gx

    lax.fori_loop(6, 22, pull_press, (M[5] - M[6]) * AX[5], unroll=8)

    for s in range(3, 0, -1):

        def sweep_back(x, carry, s=s):
            MU[s - 1][x] = spread(MU[s], x) * R[x]
            return carry

        lax.fori_loop(10 - s, 18 + s, sweep_back, 0, unroll=True)

    def products(x, carry):
        total = MU[0][x] * PR[1][x]
        for s in range(1, 4):
            total = total + MU[s][x] * PR[s + 1][x]
        W[x] = total
        return carry

    lax.fori_loop(9, 19, products, 0, unroll=True)

    def around(ref, x):
        a = ref[x]
        return (
            ref[x - 1]
            + ref[x + 1]
            + ahead(a)
            + behind(a)
            + jnp.where(top, 0.0, above(a))
            + jnp.where(bottom, 0.0, below(a))
        )

    def sensitivities(x, carry):
        m = M[x]
        gx = m - M[x + 1]
        gw = M[x - 1] - m
        gy = m - ahead(m)
        gz = m - jnp.where(top, 0.0, above(m))
        gb = m[0:8]

        def both(fx, fy, fz, fb):
            ay = gy * fy[x]
            az = gz * fz[x]
            return gx * fx[x] + gw * fx[x - 1] + ay + behind(ay) + az + lift(below(az), gb * fb[x])

        gk = both(BXX, BYY, BZZ, BBB)
        gd = both(CXX, CYY, CZZ, CBB)
        gk = gk - 6.0 * W[x] - around(W, x)
        for s in range(4):
            gk = gk + MU[s][x] * around(PR[s], x) + PR[s][x] * around(MU[s], x)
        SP[x - OWN] = (0.5 * gk * K[x])[:, 0:BY]
        SD[x - OWN] = (0.5 * gd * D[x])[:, 0:BY]
        return carry

    lax.fori_loop(OWN, OWN + BX, sensitivities, 0, unroll=True)
    for x in range(BX):
        put_rows(sens_o, x, SP[x])

    for x in range(BX):
        O[x, :, 0:BY] = rows_of(zone, x).astype(jnp.float32)

    def of_zone(z, carry):
        zf = z.astype(jnp.float32)
        total_p = jnp.zeros((NZ, BY), jnp.float32)
        total_d = jnp.zeros((NZ, BY), jnp.float32)
        for x in range(BX):
            here = O[x, :, 0:BY] == zf
            total_p = total_p + jnp.where(here, SP[x], 0.0)
            total_d = total_d + jnp.where(here, SD[x], 0.0)
        PART[z] = jnp.sum(total_p.reshape(4, 8, BY), axis=0)
        PART[z + 64] = jnp.sum(total_d.reshape(4, 8, BY), axis=0)
        return carry

    lax.fori_loop(0, 64, of_zone, 0, unroll=8)
    per_lane = jnp.sum(PART[...], axis=1)
    sums_o[...] = lax.dot_general(
        jnp.ones((8, BY), jnp.float32),
        per_lane,
        (((1,), (1,)), ((), ())),
        precision=lax.Precision.HIGHEST,
        preferred_element_type=jnp.float32,
    )


def shifted(array, axis, by):
    size = lax.axis_size(axis)
    pairs = [(i, i + by) for i in range(size) if 0 <= i + by < size]
    return lax.ppermute(array, axis, pairs)


def spread_sum(array, axis):
    size = lax.axis_size(axis)
    copies = jnp.broadcast_to(array[None], (size,) + array.shape)
    return lax.all_to_all(copies, axis, 0, 0).sum(0)


def f32(*shape):
    return jax.ShapeDtypeStruct(shape, jnp.float32)


def buf(*shape):
    return pltpu.VMEM(shape, jnp.float32)


def body(zone_ids, log_perm, log_disp, temp_start, pressure_start, temp_observed, well_cells, well_flow, plan, inject_temp):
    flat = (NZ * BX, BY)
    zone = zone_ids.reshape(flat)
    press = pressure_start.reshape(flat)
    temp = temp_start.reshape(flat)
    seen = temp_observed.reshape(flat)
    grid_rows = BX * lax.axis_size("gx")
    grid_cols = BY * lax.axis_size("gy")

    to_up, to_down = pl.pallas_call(
        pack_rows_kernel,
        out_shape=(f32(SIDE, NZ, BY), f32(SIDE, NZ, BY)),
        in_specs=[VMEM] * 4,
        out_specs=(VMEM,) * 2,
        compiler_params=FULL,
        name="pack_rows",
    )(zone, press, temp, seen)
    up = shifted(to_up, "gx", 1)
    down = shifted(to_down, "gx", -1)
    to_right, to_left = pl.pallas_call(
        pack_columns_kernel,
        out_shape=(f32(4, NZ, BY), f32(4, NZ, BY)),
        in_specs=[VMEM] * 4 + [pl.BlockSpec(memory_space=pl.ANY)],
        out_specs=(VMEM,) * 2,
        compiler_params=FULL,
        name="pack_columns",
    )(zone, press, temp, seen, to_up)
    left = shifted(to_right, "gy", 1)
    right = shifted(to_left, "gy", -1)
    corner = jnp.stack([lax.axis_index("gx") * BX, lax.axis_index("gy") * BY]).astype(jnp.int32)
    source, heat, table = pl.pallas_call(
        lambda *refs: wells_kernel(grid_rows, grid_cols, *refs),
        out_shape=(f32(WX, NZ, WY), f32(WX, NZ, WY), f32(8, BY)),
        in_specs=[SMEM] + [VMEM] * 6,
        out_specs=(VMEM,) * 3,
        compiler_params=PARAMS,
        cost_estimate=pl.CostEstimate(flops=1 << 28, bytes_accessed=2 << 20, transcendentals=0),
        name="wells",
    )(corner, well_cells[None], well_flow[None], plan, inject_temp, log_perm[None], log_disp[None])

    edge, to_up2, to_down2 = pl.pallas_call(
        corner_kernel,
        out_shape=(f32(4, NZ, BY), f32(FAR, NZ, BY), f32(FAR, NZ, BY)),
        in_specs=[VMEM] * 4 + [pl.BlockSpec(memory_space=pl.ANY)],
        out_specs=(VMEM,) * 3,
        compiler_params=PARAMS,
        name="corners",
    )(zone, press, left, right, table)
    edge_up = shifted(edge, "gx", 1)
    edge_down = shifted(edge, "gx", -1)
    up2 = shifted(to_up2, "gx", 2)
    down2 = shifted(to_down2, "gx", -2)

    temp_end, sens, sums = pl.pallas_call(
        main_kernel,
        out_shape=(f32(*flat), f32(*flat), f32(8, BY)),
        in_specs=[VMEM] * 14,
        out_specs=(VMEM,) * 3,
        scratch_shapes=[buf(WX, NZ, WY)] * 19
        + ([buf(23, NZ, WY)] * 3 + [buf(23, 8, WY)]) * 3
        + [buf(9, NZ, BY), buf(9, NZ, BY), buf(128, 8, BY)],
        compiler_params=PARAMS,
        name="aquifer",
    )(zone, press, temp, seen, edge, up, down, edge_up, edge_down, up2, down2, source, heat, table)

    totals = spread_sum(sums[0:1], ("season", "gx"))
    totals = spread_sum(totals, "gy")
    cells = lax.axis_size("season") * NZ * grid_rows * grid_cols
    gradient = totals.reshape(2, 64) * (cells / 64) ** (-0.5)
    return (temp_end.reshape(temp_start.shape), sens.reshape(temp_start.shape), gradient)


def solution(mesh):
    in_specs = (
        P(None, "gx", "gy"),
        P(),
        P(),
        P("season", None, "gx", "gy"),
        P("season", None, "gx", "gy"),
        P("season", None, "gx", "gy"),
        P(),
        P(),
        P("season", None),
        P("season", None),
    )
    out_specs = (P("season", None, "gx", "gy"), P("season", None, "gx", "gy"), P())
    return jax.shard_map(body, mesh=mesh, in_specs=in_specs, out_specs=out_specs, check_vma=False)
```

time: 123 us -> 95.9 us (0.78); the launches traced: 121 us -> 95.4 us
  Pallas kernels: 39.6 us -> 19.5 us
  starting transfers between devices: 17.8 us -> 25.7 us
  waiting for transfers between devices: 9.22 us -> 2.47 us
  local copies, waits for them, and re-layouts: 5.04 us -> 1.37 us
  blocking collectives: 48.3 us -> 45.5 us
    pallas_call x1, Pallas kernels: 31 us -> 12.7 us  [body(): pl.pallas_call(main_kernel, out_shape=(f32(*flat), f32(*flat), f32(8, BY)...]
    psum x1 -> x0, blocking collectives: 7.83 us -> none  [body(): totals = lax.psum(sums[0:1], 'season')]
    ppermute x6 -> x8, starting transfers between devices: 17.8 us -> 25.7 us  [shifted(): return lax.ppermute(array, axis, pairs)]
    ppermute x6 -> x8, waiting for transfers between devices: 9.22 us -> 2.47 us  [shifted(): return lax.ppermute(array, axis, pairs)]
    pallas_call x1, Pallas kernels: 7.68 us -> 2.28 us  [body(): pl.pallas_call(lambda *refs: wells_kernel(grid_rows, grid_cols, *refs), o...]
    all_to_all x2, blocking collectives: 40.4 us -> 45.5 us  [spread_sum(): return lax.all_to_all(copies, axis, 0, 0).sum(0)]
    pallas_call x2 -> x3, Pallas kernels: 0.86 us -> 4.51 us  [the longest x1 2.32 us: body(): pl.pallas_call(pack_rows_kernel, out_shape=(f32(SIDE, NZ, BY), f32(SIDE,...]
    unnamed x28 -> x20, local copies, waits for them, and re-layouts: 4.31 us -> 0.7 us
  transfers between devices with their start and end apart: 6 -> 8, of which waited for: 3 -> 2; matrix products, arithmetic and copies ran while one was open for 0% -> 0% of each run, Pallas kernels for 6% -> 5%
where the time goes in v2:
time: 95.9 us; the launch traced here: 95.4 us
  blocking collectives  45.5 us (47%)
  starting transfers between devices  25.7 us (27%)
  Pallas kernels  19.5 us (20%)
  waiting for transfers between devices  2.47 us (3%)
  local copies, waits for them, and re-layouts  1.37 us (1%)
    all_to_all x2, blocking collectives, spread_sum(): return lax.all_to_all(copies, axis, 0, 0).sum(0)  45.5 us
    ppermute x8, starting transfers between devices, shifted(): return lax.ppermute(array, axis, pairs)  25.7 us
    pallas_call x1, Pallas kernels, body(): pl.pallas_call(main_kernel, out_shape=(f32(*flat), f32(*flat), f32(8, BY)...  12.7 us
    ppermute x8, waiting for transfers between devices, shifted(): return lax.ppermute(array, axis, pairs)  2.47 us
    pallas_call x1, Pallas kernels, body(): pl.pallas_call(pack_rows_kernel, out_shape=(f32(SIDE, NZ, BY), f32(SIDE,...  2.32 us
    pallas_call x1, Pallas kernels, body(): pl.pallas_call(lambda *refs: wells_kernel(grid_rows, grid_cols, *refs), o...  2.28 us
    pallas_call x1, Pallas kernels, body(): pl.pallas_call(pack_columns_kernel, out_shape=(f32(4, NZ, BY), f32(4, NZ,...  2.09 us
  transfers between devices with their start and end apart: 8, of which 2 were waited for; matrix products, arithmetic and copies ran while one was open for 0% of the time, Pallas kernels for 5%

profile of v2, /device:TPU:1, one launch (start us, length us, event | category | flops | bytes accessed | tf_op | source)
XLA Modules:
  0.0 95.4 jit_solution(15438713188241805705)
XLA Ops:
  0.6 2.3 %pack_rows.1 = (f32[27,32,128]{2,1,0:T(8,128)}, f32[27,32,128]{2,1,0:T(8,128)}) custom-call(s32[256,128]{1,0:T(8,128)} %bitcast.16, f32[256,128]{1,0:T(8,128)} %bitcast.20, f32[256,128]{1,0:T(8,128)} %bitcast.24, f32[256,128]{1,0:T(8,128)} %bitcast.27), custom_call_target="tpu_custom_call" | custom-call | tf_op jit(solution)/shard_map/pack_rows/pallas_call | solution.py:476
  3.0 1.3 %collective-permute-start.3 = (f32[27,32,128]{2,1,0:T(8,128)}, f32[27,32,128]{2,1,0:T(8,128)S(1)}, u32[]{:S(2)}, u32[]{:S(2)}) collective-permute-start(f32[27,32,128]{2,1,0:T(8,128)} %get-tuple-element.21), channel_id=1, source_target_pairs={{16,0},{32,16},{48,32},{64,48},{80,64},{96,80},{112,96},{17,1},{33... | collective-permute-start | bytes 1327112 | tf_op jit(solution)/shard_map/ppermute | solution.py:450
  4.2 6.1 %collective-permute-start.2 = (f32[27,32,128]{2,1,0:T(8,128)}, f32[27,32,128]{2,1,0:T(8,128)S(1)}, u32[]{:S(2)}, u32[]{:S(2)}) collective-permute-start(f32[27,32,128]{2,1,0:T(8,128)} %get-tuple-element.16.after), channel_id=1, source_target_pairs={{0,16},{16,32},{32,48},{48,64},{64,80},{80,96},{96,112},{1,17},{17... | collective-permute-start | bytes 1327112 | tf_op jit(solution)/shard_map/ppermute | solution.py:450
  10.4 0.0 copy-start.6
  10.4 0.0 copy-start.7
  10.4 2.1 %pack_columns.1 = (f32[4,32,128]{2,1,0:T(8,128)}, f32[4,32,128]{2,1,0:T(8,128)}) custom-call(s32[256,128]{1,0:T(8,128)} %bitcast.17, f32[256,128]{1,0:T(8,128)} %bitcast.21, f32[256,128]{1,0:T(8,128)} %bitcast.25, f32[256,128]{1,0:T(8,128)} %bitcast.28, f32[27,32,128]{2,1,0:T(8,128)} %get-tuple-element.16.after), custom_call_target="tpu_custom_call" | custom-call | tf_op jit(solution)/shard_map/pack_columns/pallas_call | solution.py:486
  12.5 3.7 %collective-permute-start = (f32[4,32,128]{2,1,0:T(8,128)}, f32[4,32,128]{2,1,0:T(8,128)S(1)}, u32[]{:S(2)}, u32[]{:S(2)}) collective-permute-start(f32[4,32,128]{2,1,0:T(8,128)} %get-tuple-element.17), channel_id=1, source_target_pairs={{0,1},{1,2},{2,3},{3,4},{4,5},{5,6},{6,7},{7,8},{8,9},{9,10},{10,1... | collective-permute-start | bytes 196616 | tf_op jit(solution)/shard_map/ppermute | solution.py:450
  16.3 1.3 %collective-permute-start.1 = (f32[4,32,128]{2,1,0:T(8,128)}, f32[4,32,128]{2,1,0:T(8,128)S(1)}, u32[]{:S(2)}, u32[]{:S(2)}) collective-permute-start(f32[4,32,128]{2,1,0:T(8,128)} %get-tuple-element.18), channel_id=1, source_target_pairs={{1,0},{2,1},{3,2},{4,3},{5,4},{6,5},{7,6},{8,7},{9,8},{10,9},{11,1... | collective-permute-start | bytes 196616 | tf_op jit(solution)/shard_map/ppermute | solution.py:450
  17.6 0.0 copy-start.5
  17.6 0.0 copy-start.4
  17.6 0.1 pad_add_fusion.refs_0_
  17.7 0.6 copy-done.5
  18.3 0.0 copy-done.4
  18.3 0.0 copy-done.8
  18.3 0.0 copy-done.9
  18.3 2.3 %wells.1 = (f32[28,32,256]{2,1,0:T(8,128)S(1)}, f32[28,32,256]{2,1,0:T(8,128)S(1)}, f32[8,128]{1,0:T(8,128)S(1)}) custom-call(s32[2]{0:T(128)S(1)} %pad_add_fusion.refs_0_, s32[1,2048]{1,0:T(1,128)S(1)} %bitcast.30, f32[1,2048]{1,0:T(1,128)S(1)} %bitcast.31, s32[1,2048]{1,0:T(1,128)S(1)} %copy-done.6, f32[1,2048]{1,0:T(1,128)S(1)} %copy-done.7, ...), custom_call_target="tpu_custom_call" | custom-call | flops 268435456 | bytes 2097152 | tf_op jit(solution)/shard_map/wells/pallas_call | solution.py:497
  20.6 0.0 collective-permute-done.left
  20.6 1.3 %collective-permute-done.1.right = f32[4,32,128]{2,1,0:T(8,128)S(1)} collective-permute-done((f32[4,32,128]{2,1,0:T(8,128)}, f32[4,32,128]{2,1,0:T(8,128)S(1)}, u32[]{:S(2)}, u32[]{:S(2)}) %collective-permute-start.1) | collective-permute-done | bytes 65568 | tf_op jit(solution)/shard_map/ppermute | solution.py:450
  22.0 0.1 corners.1
  22.1 1.4 %collective-permute-start.5 = (f32[4,32,128]{2,1,0:T(8,128)S(1)}, f32[4,32,128]{2,1,0:T(8,128)S(1)}, u32[]{:S(2)}, u32[]{:S(2)}) collective-permute-start(f32[4,32,128]{2,1,0:T(8,128)S(1)} %get-tuple-element.20.edge), channel_id=1, source_target_pairs={{16,0},{32,16},{48,32},{64,48},{80,64},{96,80},{112,96},{17,1},{33... | collective-permute-start | bytes 196616 | tf_op jit(solution)/shard_map/ppermute | solution.py:450
  23.5 7.3 %collective-permute-start.6 = (f32[5,32,128]{2,1,0:T(8,128)S(1)}, f32[5,32,128]{2,1,0:T(8,128)S(1)}, u32[]{:S(2)}, u32[]{:S(2)}) collective-permute-start(f32[5,32,128]{2,1,0:T(8,128)S(1)} %get-tuple-element.22), channel_id=1, source_target_pairs={{0,32},{16,48},{32,64},{48,80},{64,96},{80,112},{1,33},{17,49},{33... | collective-permute-start | bytes 245768 | tf_op jit(solution)/shard_map/ppermute | solution.py:450
  30.8 1.3 %collective-permute-start.7 = (f32[5,32,128]{2,1,0:T(8,128)S(1)}, f32[5,32,128]{2,1,0:T(8,128)S(1)}, u32[]{:S(2)}, u32[]{:S(2)}) collective-permute-start(f32[5,32,128]{2,1,0:T(8,128)S(1)} %get-tuple-element.23), channel_id=1, source_target_pairs={{32,0},{48,16},{64,32},{80,48},{96,64},{112,80},{33,1},{49,17},{65... | collective-permute-start | bytes 245768 | tf_op jit(solution)/shard_map/ppermute | solution.py:450
  32.1 0.0 collective-permute-done.5.edge_down
  32.1 3.2 %collective-permute-start.4 = (f32[4,32,128]{2,1,0:T(8,128)S(1)}, f32[4,32,128]{2,1,0:T(8,128)S(1)}, u32[]{:S(2)}, u32[]{:S(2)}) collective-permute-start(f32[4,32,128]{2,1,0:T(8,128)S(1)} %get-tuple-element.20.edge), channel_id=1, source_target_pairs={{0,16},{16,32},{32,48},{48,64},{64,80},{80,96},{96,112},{1,17},{17... | collective-permute-start | bytes 196616 | tf_op jit(solution)/shard_map/ppermute | solution.py:450
  35.3 1.1 %collective-permute-done.4.edge_up = f32[4,32,128]{2,1,0:T(8,128)S(1)} collective-permute-done((f32[4,32,128]{2,1,0:T(8,128)S(1)}, f32[4,32,128]{2,1,0:T(8,128)S(1)}, u32[]{:S(2)}, u32[]{:S(2)}) %collective-permute-start.4) | collective-permute-done | bytes 65568 | tf_op jit(solution)/shard_map/ppermute | solution.py:450
  36.4 0.0 collective-permute-done.6.up2
  36.5 0.0 collective-permute-done.7.down2
  36.5 0.0 collective-permute-done.3.down
  36.5 12.7 %aquifer.1 = (f32[256,128]{1,0:T(8,128)}, f32[256,128]{1,0:T(8,128)}, f32[8,128]{1,0:T(8,128)S(1)}) custom-call(s32[256,128]{1,0:T(8,128)S(1)} %bitcast.19, f32[256,128]{1,0:T(8,128)S(1)} %bitcast.23, f32[256,128]{1,0:T(8,128)S(1)} %bitcast.26, f32[256,128]{1,0:T(8,128)S(1)} %bitcast.29, f32[4,32,128]{2,1,0:T(8,128)S(1)} %get-tuple-element.20.edge, ...), custom_call_target="tpu_custom_call" | custom-call | tf_op jit(solution)/shard_map/aquifer/pallas_call | solution.py:520
  49.2 19.6 %all_to_all.10 = f32[32,1,128]{2,1,0:T(1,128)S(1)} all-to-all(f32[32,1,128]{2,1,0:T(1,128)S(1)} %broadcast_in_dim.31), channel_id=1, replica_groups=mesh['season'=4,'gx'=8,'gy'=16] {'season','gx'}, dimensions={0} | all-to-all | bytes 32768 | tf_op jit(solution)/shard_map/all_to_all | solution.py:456
  68.9 25.9 %all_to_all.11 = f32[16,1,128]{2,1,0:T(1,128)S(1)} all-to-all(f32[16,1,128]{2,1,0:T(1,128)S(1)} %broadcast_in_dim.32), channel_id=1, replica_groups=mesh['season'=4,'gx'=8,'gy'=16] {'gy'}, dimensions={0} | all-to-all | bytes 16384 | tf_op jit(solution)/shard_map/all_to_all | solution.py:456
  94.8 0.6 mul.19
  (19 shorter events, 0.1 us)
Async XLA Ops:
  3.0 33.5 %collective-permute-start.3 = (f32[27,32,128]{2,1,0:T(8,128)}, f32[27,32,128]{2,1,0:T(8,128)S(1)}, u32[]{:S(2)}, u32[]{:S(2)}) collective-permute-start(f32[27,32,128]{2,1,0:T(8,128)} %get-tuple-element.21), channel_id=1, source_target_pairs={{16,0},{32,16},{48,32},{64,48},{80,64},{96,80},{112,96},{17,1},{33... | collective-permute-start | bytes 1327112 | tf_op jit(solution)/shard_map/ppermute | solution.py:450
  4.2 32.2 %collective-permute-start.2 = (f32[27,32,128]{2,1,0:T(8,128)}, f32[27,32,128]{2,1,0:T(8,128)S(1)}, u32[]{:S(2)}, u32[]{:S(2)}) collective-permute-start(f32[27,32,128]{2,1,0:T(8,128)} %get-tuple-element.16.after), channel_id=1, source_target_pairs={{0,16},{16,32},{32,48},{48,64},{64,80},{80,96},{96,112},{1,17},{17... | collective-permute-start | bytes 1327112 | tf_op jit(solution)/shard_map/ppermute | solution.py:450
  10.4 7.3 %copy-start.6 = (s32[1,2048]{1,0:T(1,128)S(1)}, s32[1,2048]{1,0:T(1,128)}, u32[]{:S(2)}) copy-start(s32[1,2048]{1,0:T(1,128)} %refs_3_.1) | copy-start | bytes 24580
  10.4 7.3 %copy-start.7 = (f32[1,2048]{1,0:T(1,128)S(1)}, f32[1,2048]{1,0:T(1,128)}, u32[]{:S(2)}) copy-start(f32[1,2048]{1,0:T(1,128)} %refs_4_.1) | copy-start | bytes 24580
  12.5 8.1 %collective-permute-start = (f32[4,32,128]{2,1,0:T(8,128)}, f32[4,32,128]{2,1,0:T(8,128)S(1)}, u32[]{:S(2)}, u32[]{:S(2)}) collective-permute-start(f32[4,32,128]{2,1,0:T(8,128)} %get-tuple-element.17), channel_id=1, source_target_pairs={{0,1},{1,2},{2,3},{3,4},{4,5},{5,6},{6,7},{7,8},{8,9},{9,10},{10,1... | collective-permute-start | bytes 196616 | tf_op jit(solution)/shard_map/ppermute | solution.py:450
  16.3 5.7 %collective-permute-start.1 = (f32[4,32,128]{2,1,0:T(8,128)}, f32[4,32,128]{2,1,0:T(8,128)S(1)}, u32[]{:S(2)}, u32[]{:S(2)}) collective-permute-start(f32[4,32,128]{2,1,0:T(8,128)} %get-tuple-element.18), channel_id=1, source_target_pairs={{1,0},{2,1},{3,2},{4,3},{5,4},{6,5},{7,6},{8,7},{9,8},{10,9},{11,1... | collective-permute-start | bytes 196616 | tf_op jit(solution)/shard_map/ppermute | solution.py:450
  17.6 0.7 copy-start.5
  17.6 0.7 copy-start.4
  17.7 0.7 copy-start.8
  17.7 0.7 copy-start.9
  18.3 3.6 %copy-start = (s32[32,8,128]{2,1,0:T(8,128)S(1)}, s32[32,8,128]{2,1,0:T(8,128)}, u32[]{:S(2)}) copy-start(s32[32,8,128]{2,1,0:T(8,128)} %param.10) | copy-start | bytes 393220
  18.3 3.6 %copy-start.1 = (f32[1,32,8,128]{3,2,1,0:T(8,128)S(1)}, f32[1,32,8,128]{3,2,1,0:T(8,128)}, u32[]{:S(2)}) copy-start(f32[1,32,8,128]{3,2,1,0:T(8,128)} %param.14) | copy-start | bytes 393220
  22.0 14.5 %copy-start.2 = (f32[1,32,8,128]{3,2,1,0:T(8,128)S(1)}, f32[1,32,8,128]{3,2,1,0:T(8,128)}, u32[]{:S(2)}) copy-start(f32[1,32,8,128]{3,2,1,0:T(8,128)} %param.13) | copy-start | bytes 393220
  22.0 14.5 %copy-start.3 = (f32[1,32,8,128]{3,2,1,0:T(8,128)S(1)}, f32[1,32,8,128]{3,2,1,0:T(8,128)}, u32[]{:S(2)}) copy-start(f32[1,32,8,128]{3,2,1,0:T(8,128)} %param.15) | copy-start | bytes 393220
  22.1 10.1 %collective-permute-start.5 = (f32[4,32,128]{2,1,0:T(8,128)S(1)}, f32[4,32,128]{2,1,0:T(8,128)S(1)}, u32[]{:S(2)}, u32[]{:S(2)}) collective-permute-start(f32[4,32,128]{2,1,0:T(8,128)S(1)} %get-tuple-element.20.edge), channel_id=1, source_target_pairs={{16,0},{32,16},{48,32},{64,48},{80,64},{96,80},{112,96},{17,1},{33... | collective-permute-start | bytes 196616 | tf_op jit(solution)/shard_map/ppermute | solution.py:450
  23.5 13.0 %collective-permute-start.6 = (f32[5,32,128]{2,1,0:T(8,128)S(1)}, f32[5,32,128]{2,1,0:T(8,128)S(1)}, u32[]{:S(2)}, u32[]{:S(2)}) collective-permute-start(f32[5,32,128]{2,1,0:T(8,128)S(1)} %get-tuple-element.22), channel_id=1, source_target_pairs={{0,32},{16,48},{32,64},{48,80},{64,96},{80,112},{1,33},{17,49},{33... | collective-permute-start | bytes 245768 | tf_op jit(solution)/shard_map/ppermute | solution.py:450
  30.8 5.6 %collective-permute-start.7 = (f32[5,32,128]{2,1,0:T(8,128)S(1)}, f32[5,32,128]{2,1,0:T(8,128)S(1)}, u32[]{:S(2)}, u32[]{:S(2)}) collective-permute-start(f32[5,32,128]{2,1,0:T(8,128)S(1)} %get-tuple-element.23), channel_id=1, source_target_pairs={{32,0},{48,16},{64,32},{80,48},{96,64},{112,80},{33,1},{49,17},{65... | collective-permute-start | bytes 245768 | tf_op jit(solution)/shard_map/ppermute | solution.py:450
  32.1 4.3 %collective-permute-start.4 = (f32[4,32,128]{2,1,0:T(8,128)S(1)}, f32[4,32,128]{2,1,0:T(8,128)S(1)}, u32[]{:S(2)}, u32[]{:S(2)}) collective-permute-start(f32[4,32,128]{2,1,0:T(8,128)S(1)} %get-tuple-element.20.edge), channel_id=1, source_target_pairs={{0,16},{16,32},{32,48},{48,64},{64,80},{80,96},{96,112},{1,17},{17... | collective-permute-start | bytes 196616 | tf_op jit(solution)/shard_map/ppermute | solution.py:450

commit v3 on v2

v3 whole, which is shorter than its diff:
```python
import jax
import jax.numpy as jnp
from jax import lax
from jax.experimental import pallas as pl
from jax.experimental.pallas import tpu as pltpu
from jax.sharding import PartitionSpec as P

STORAGE = 0.5
CONDUCT = 0.1
SMOOTH = 0.01
TIME_STEP = 0.02
HEAT_GAIN = 10.0

NZ = 32
BX = 8
BY = 128
RAD = 10
WX = BX + 2 * RAD
RIM = 22
SHIFT = 52
OWN = RAD
SIDE = 27
FAR = 4
EDGE = 11
MIDDLE = range(RAD - 4, RAD + BX + 4)
OTHERS = [r for r in range(WX) if r not in MIDDLE]


def edge_place(r):
    if r in MIDDLE:
        pair, base = (r - MIDDLE[0]) // 2, 62 * (r % 2)
        return pair, {"p": (base, 10), "z": (base + 20, 10), "t": (base + 36, 6), "o": (base + 47, 5)}
    place = OTHERS.index(r)
    base = 32 * (place % 4)
    return 8 + place // 4, {"p": (base + 5, 5), "z": (base + 15, 5), "t": (base + 21, 1)}


NWELL = 2048
PICK = 256

VMEM = pl.BlockSpec(memory_space=pltpu.VMEM)
SMEM = pl.BlockSpec(memory_space=pltpu.SMEM)
FULL = pltpu.CompilerParams(vmem_limit_bytes=60 * 1024 * 1024)
PARAMS = pltpu.CompilerParams(vmem_limit_bytes=48 * 1024 * 1024)


def lanes(shape):
    return lax.broadcasted_iota(jnp.int32, shape, len(shape) - 1)


def rows_of(ref, x):
    return jnp.concatenate([ref[pl.ds(x + BX * v, 8, stride=4 * BX), :] for v in range(4)], axis=0)


def put_rows(ref, x, value):
    for v in range(4):
        ref[pl.ds(x + BX * v, 8, stride=4 * BX), :] = value[8 * v : 8 * v + 8]


def roll(a, by, axis):
    return pltpu.roll(a, by % a.shape[axis], axis)


def between(lane, low, high):
    if low < 0:
        return (lane >= low + BY) | (lane < high)
    return (lane >= low) & (lane < high)


def pack_rows_kernel(zone, press, temp, seen, up_o, down_o, up2_o, down2_o):
    for x in range(BX):
        p = rows_of(press, x)
        z = (rows_of(zone, x) + 1).astype(jnp.float32)
        t = rows_of(temp, x)
        o = rows_of(seen, x)
        up_o[x] = p
        down_o[x] = p
        up_o[8 + x] = z
        down_o[8 + x] = z
        if x >= 2:
            up_o[14 + x] = t
        if x < 6:
            down_o[16 + x] = t
        if x >= 3:
            up_o[19 + x] = o
        if x < 5:
            down_o[22 + x] = o
        if x >= 6:
            up2_o[x - 6] = p
            up2_o[x - 4] = z
        if x < 2:
            down2_o[x] = p
            down2_o[x + 2] = z


def grid_row(r, zone, press, temp, seen, up, down, up2, down2):
    row = {}
    if r < 2:
        row["p"], z = up2[r], up2[2 + r]
    elif r < 10:
        j = r - 2
        row["p"], z = up[j], up[8 + j]
        if j >= 2:
            row["t"] = up[14 + j]
        if j >= 3:
            row["o"] = up[19 + j]
    elif r < 18:
        j = r - 10
        row["p"], z = rows_of(press, j), rows_of(zone, j) + 1
        row["t"], row["o"] = rows_of(temp, j), rows_of(seen, j)
    elif r < 26:
        j = r - 18
        row["p"], z = down[j], down[8 + j]
        if j < 6:
            row["t"] = down[16 + j]
        if j < 5:
            row["o"] = down[22 + j]
    else:
        j = r - 26
        row["p"], z = down2[j], down2[2 + j]
    row["z"] = z
    return row


def pack_columns_kernel(zone, press, temp, seen, up, down, up2, down2, after, right_o, left_o):
    lane = lanes((NZ, BY))
    right, left = {}, {}
    for r in range(WX):
        row = grid_row(r, zone, press, temp, seen, up, down, up2, down2)
        index, places = edge_place(r)
        if index not in right:
            right[index] = left[index] = jnp.zeros((NZ, BY), jnp.float32)
        for name, (spot, reach) in places.items():
            if name not in row:
                continue
            field = row[name].astype(jnp.float32)
            moved = roll(field, spot, 1) if spot else field
            start = spot - reach if spot else BY - reach
            right[index] = jnp.where(between(lane, start, start + reach), moved, right[index])
            left[index] = jnp.where(between(lane, spot, spot + reach), moved, left[index])
    for index in range(EDGE):
        right_o[index] = right[index]
        left_o[index] = left[index]


def wells_kernel(grid_rows, grid_cols, where_ref, cells, flow, plan, inject, perm_logs, disp_logs, q_o, h_o, q_rim_o, h_rim_o, table_o):
    lane = lanes((1, BY))
    for i, logs in enumerate((perm_logs, disp_logs)):
        row = jnp.concatenate([jnp.exp(logs[...]), jnp.zeros((1, BY - 64), jnp.float32)], axis=1)
        table_o[i : i + 1, :] = roll(row, 1, 1)

    cell = cells[...]
    layer = cell // (grid_rows * grid_cols)
    layer = layer % 4 * 8 + layer // 4
    x = cell // grid_cols % grid_rows - (where_ref[0] - RAD)
    y = cell % grid_cols - where_ref[1]
    near = (x >= 0) & (x < WX) & (y >= -RAD) & (y < BY + RAD)
    near = jnp.where(near, 1.0, 0.0)
    rate = plan[...].astype(jnp.float32) * flow[...]
    warm = jnp.maximum(rate, 0.0) * inject[...]

    def halves(field):
        high = field.astype(jnp.bfloat16).astype(jnp.float32)
        return [high, field - high]

    place = [x.astype(jnp.float32), layer.astype(jnp.float32), (y + RAD).astype(jnp.float32)]
    facts = jnp.concatenate(place + [near] + halves(rate) + halves(warm), axis=0).astype(jnp.bfloat16)

    chunks = [slice(c, c + PICK) for c in range(0, NWELL, PICK)]
    across = lax.broadcasted_iota(jnp.int32, (PICK, PICK), 1)
    down = lax.broadcasted_iota(jnp.int32, (PICK, PICK), 0)
    upto = jnp.where(down <= across, 1.0, 0.0).astype(jnp.bfloat16)
    marks = jnp.concatenate([near[:, c] for c in chunks], axis=0)
    counts = jnp.dot(marks.astype(jnp.bfloat16), upto, preferred_element_type=jnp.float32)
    before = jnp.zeros((1, 1), jnp.float32)
    number = []
    for i, c in enumerate(chunks):
        number.append(jnp.where(near[:, c] > 0.0, counts[i : i + 1] + (before - 1.0), -1.0).astype(jnp.int32))
        before = before + counts[i : i + 1, PICK - 1 : PICK]
    total = jnp.sum(near).astype(jnp.int32)

    def slab(start, first):
        picked = jnp.zeros((8, PICK), jnp.float32)
        for i, c in enumerate(chunks):
            chosen = jnp.where(down + start == number[i], 1.0, 0.0).astype(jnp.bfloat16)
            picked = picked + lax.dot_general(
                facts[:, c], chosen, (((1,), (1,)), ((), ())), preferred_element_type=jnp.float32
            )
        px, layer, py = (picked[i : i + 1].astype(jnp.int32) for i in range(3))
        py = py - RAD
        real = picked[3:4] > 0.5
        in_middle = real & (py >= 0) & (py < BY)
        in_rim = real & ((py < RIM) | (py >= BY - RIM))
        rim_lane = jnp.where(py < 0, py + BY, jnp.where(py < RIM, py, py - SHIFT))
        for spot, column, rows, outs in (
            (jnp.where(in_middle, px * NZ + layer, -1), py, NZ, (q_o, h_o)),
            (jnp.where(in_rim, px * NZ + layer, -1), rim_lane, NZ, (q_rim_o, h_rim_o)),
        ):
            there = lax.broadcasted_iota(jnp.int32, (BY, PICK), 0) == column
            for i, out in enumerate(outs):
                parts = [jnp.where(there, picked[4 + 2 * i + j : 5 + 2 * i + j], 0.0).astype(jnp.bfloat16) for j in range(2)]
                for x0, x1 in ((1, 14), (14, 27)) if i == 0 else ((5, 14), (14, 23)):
                    index = lax.broadcasted_iota(jnp.int32, ((x1 - x0) * rows, PICK), 0) + x0 * rows
                    hit = jnp.where(index == spot, 1.0, 0.0).astype(jnp.bfloat16)
                    value = jnp.zeros(((x1 - x0) * rows, BY), jnp.float32)
                    for part in parts:
                        value = value + lax.dot_general(
                            hit, part, (((1,), (1,)), ((), ())), preferred_element_type=jnp.float32
                        )
                    value = value.reshape(x1 - x0, rows, BY)
                    out[x0:x1] = value if first else out[x0:x1] + value

    slab(0, True)

    @pl.loop(1, (total + (PICK - 1)) // PICK)
    def _(i):
        slab(i * PICK, False)


def face(t, pi, pj, ti, tj, di, dj):
    dp = pi - pj
    u = t * dp
    v = u * u + SMOOTH
    inv = lax.rsqrt(v)
    speed = v * inv
    db = 0.5 * (di + dj)
    dt = ti - tj
    st = 0.5 * (ti + tj)
    flux = (CONDUCT + db * speed) * dt + u * st
    e = db * (u * inv) * dt + st
    return flux, e * t, e * dp, speed * dt


def solve(scratch, source, heat, ends, perm_sens, disp_sens):
    (
        K, D, T, O, P0, P1, P2, P3, P4, TX, TY, TZ, R, M, U0, U1, U2, U3, W,
        AX, AY, AZ, AB, BXX, BYY, BZZ, BBB, CXX, CYY, CZZ, CBB,
    ) = scratch
    PR = (P0, P1, P2, P3, P4)
    MU = (U0, U1, U2, U3)
    at = lax.broadcasted_iota(jnp.int32, (NZ, BY), 0)
    top = at == NZ - 1
    bottom = at == 0

    def above(a):
        return jnp.concatenate([a[8:], roll(a[:8], -1, 0)], axis=0)

    def below(a):
        return jnp.concatenate([roll(a[24:], 1, 0), a[:24]], axis=0)

    def ahead(a):
        return roll(a, -1, 1)

    def behind(a):
        return roll(a, 1, 1)

    def coefficients(x, before):
        k = K[x]
        tx = 0.5 * (k + K[x + 1])
        ty = 0.5 * (k + ahead(k))
        half = 0.5 * k
        tz = jnp.where(top, 0.0, half + above(half))
        total = STORAGE + before + tx + ty + behind(ty) + tz + below(tz)
        total = total + jnp.where(top | bottom, half, 0.0)
        TX[x] = tx
        TY[x] = ty
        TZ[x] = tz
        R[x] = jnp.where(k > 0.0, 1.0 / total, 0.0)
        return tx

    TX[0] = 0.5 * (K[0] + K[1])
    lax.fori_loop(1, WX - 1, coefficients, 0.5 * (K[0] + K[1]), unroll=13)

    def spread(ref, x):
        a = ref[x]
        ty, tz = TY[x], TZ[x]
        return (
            TX[x] * ref[x + 1]
            + TX[x - 1] * ref[x - 1]
            + ty * ahead(a)
            + behind(ty * a)
            + tz * above(a)
            + below(tz * a)
        )

    for s in range(1, 5):

        def sweep(x, carry, s=s):
            PR[s][x] = (source[x] + spread(PR[s - 1], x)) * R[x]
            return carry

        lax.fori_loop(s, WX - s, sweep, 0, unroll=True)

    PE = PR[4]

    def face_x(x):
        return face(TX[x], PE[x], PE[x + 1], T[x], T[x + 1], D[x], D[x + 1])

    def transport(keep):
        def step(x, before):
            t, p, d = T[x], PE[x], D[x]
            fx, ax, bx, cx = face_x(x)
            fy, ay, by, cy = face(TY[x], p, ahead(p), t, ahead(t), d, ahead(d))
            half = 0.5 * K[x]
            tz = TZ[x] + jnp.where(top, half, 0.0)

            def over(a):
                return jnp.where(top, 0.0, above(a))

            fz, az, bz, cz = face(tz, p, over(p), t, over(t), d, over(d))
            fb, ab, bb, cb = face(half[0:8], p[0:8], 0.0, t[0:8], 0.0, d[0:8], 0.0)
            fall = jnp.concatenate([-fb, jnp.zeros((NZ - 8, BY), jnp.float32)], axis=0)
            out = fx - before + fy - behind(fy) + fz - jnp.where(bottom, fall, below(fz))
            end = t + TIME_STEP * (HEAT_GAIN * heat[x] - out)
            M[x] = jnp.where(R[x] > 0.0, (-TIME_STEP) * (end - O[x]), 0.0)
            AX[x], AY[x], AZ[x], AB[x] = ax, ay, az, ab
            if keep:
                BXX[x], BYY[x], BZZ[x], BBB[x] = bx, by, bz, bb
                CXX[x], CYY[x], CZZ[x], CBB[x] = cx, cy, cz, cb
                ends[x - 9] = end
            return fx

        return step

    first = face_x(4)[0]
    first = lax.fori_loop(5, 9, transport(False), first, unroll=True)
    first = lax.fori_loop(9, 18, transport(True), first, unroll=True)
    lax.fori_loop(18, 23, transport(False), first, unroll=True)

    def lift(a, b8):
        wide = jnp.concatenate([b8, jnp.zeros((NZ - 8, BY), jnp.float32)], axis=0)
        return jnp.where(bottom, wide, a)

    def pull_press(x, before):
        m = M[x]
        gx = (m - M[x + 1]) * AX[x]
        gy = (m - ahead(m)) * AY[x]
        gz = (m - jnp.where(top, 0.0, above(m))) * AZ[x]
        gb = m[0:8] * AB[x]
        lam = gx - before + gy - behind(gy) + gz + lift(-below(gz), gb)
        MU[3][x] = lam * R[x]
        return gx

    lax.fori_loop(6, 22, pull_press, (M[5] - M[6]) * AX[5], unroll=8)

    for s in range(3, 0, -1):

        def sweep_back(x, carry, s=s):
            MU[s - 1][x] = spread(MU[s], x) * R[x]
            return carry

        lax.fori_loop(10 - s, 18 + s, sweep_back, 0, unroll=True)

    def products(x, carry):
        total = MU[0][x] * PR[1][x]
        for s in range(1, 4):
            total = total + MU[s][x] * PR[s + 1][x]
        W[x] = total
        return carry

    lax.fori_loop(9, 19, products, 0, unroll=True)

    def around(ref, x):
        a = ref[x]
        return (
            ref[x - 1]
            + ref[x + 1]
            + ahead(a)
            + behind(a)
            + jnp.where(top, 0.0, above(a))
            + jnp.where(bottom, 0.0, below(a))
        )

    def sensitivities(x, carry):
        m = M[x]
        gx = m - M[x + 1]
        gw = M[x - 1] - m
        gy = m - ahead(m)
        gz = m - jnp.where(top, 0.0, above(m))
        gb = m[0:8]

        def both(fx, fy, fz, fb):
            ay = gy * fy[x]
            az = gz * fz[x]
            return gx * fx[x] + gw * fx[x - 1] + ay + behind(ay) + az + lift(below(az), gb * fb[x])

        gk = both(BXX, BYY, BZZ, BBB)
        gd = both(CXX, CYY, CZZ, CBB)
        gk = gk - 6.0 * W[x] - around(W, x)
        for s in range(4):
            gk = gk + MU[s][x] * around(PR[s], x) + PR[s][x] * around(MU[s], x)
        perm_sens[x - OWN] = 0.5 * gk * K[x]
        disp_sens[x - OWN] = 0.5 * gd * D[x]
        return carry

    lax.fori_loop(OWN, OWN + BX, sensitivities, 0, unroll=True)


def look(table, i, index):
    wide = jnp.broadcast_to(table[i : i + 1], index.shape)
    return jnp.take_along_axis(wide, index, axis=1, mode="promise_in_bounds")


def middle_kernel(zone, press, temp, seen, up, down, up2, down2, after, source, heat, table, ends, perm_sens, disp_sens, *scratch):
    K, D, T, O, start = scratch[:5]
    for r in range(WX):
        row = grid_row(r, zone, press, temp, seen, up, down, up2, down2)
        z = row["z"].astype(jnp.int32)
        start[r] = row["p"]
        K[r] = look(table, 0, z)
        if 4 <= r < 24:
            D[r] = look(table, 1, z)
            T[r] = row["t"]
        if 5 <= r < 23:
            O[r] = row["o"]

    solve(scratch, source, heat, ends, perm_sens, disp_sens)


def rim_kernel(
    zone, press, temp, seen, up, down, up2, down2, left, right, source, heat, table, mid_ends, mid_perm, mid_disp,
    temp_o, sens_o, sums_o, ends, perm_sens, disp_sens, SP, SD, Z, PART, temp_v, sens_v, sems, *scratch,
):
    K, D, T, O, start = scratch[:5]
    lane = lanes((NZ, BY))

    moved = (lane >= 54) & (lane < 86)
    patterns = {}

    def rims(field, packed, spot, reach):
        part = jnp.where(moved, roll(field, -SHIFT, 1), field)
        if packed is None:
            return part
        if (spot, reach) not in patterns:
            index = (jnp.where(lane < 86, lane - (BY - SHIFT), lane) + spot) & (BY - 1)
            patterns[spot, reach] = index, (lane >= BY - reach) | ((lane >= 76) & (lane < 76 + reach))
        index, here = patterns[spot, reach]
        return jnp.where(here, jnp.take_along_axis(packed, index, axis=1, mode="promise_in_bounds"), part)

    sides = {}
    for r in range(WX):
        row = grid_row(r, zone, press, temp, seen, up, down, up2, down2)
        index, places = edge_place(r)

        if index not in sides:
            sides[index] = left[index] + right[index]

        def both(name, index=index, places=places, row=row):
            return rims(row[name].astype(jnp.float32), sides[index], *places[name])

        start[r] = both("p")
        z = both("z").astype(jnp.int32)
        K[r] = look(table, 0, z)
        if 4 <= r < 24:
            D[r] = look(table, 1, z)
            T[r] = both("t")
        if 5 <= r < 23:
            O[r] = both("o") if "o" in places else rims(row["o"], None, 0, 0)

    solve(scratch, source, heat, ends, perm_sens, disp_sens)

    def joined(middle, rim):
        return jnp.where(lane < RAD, rim, jnp.where(lane >= BY - RAD, roll(rim, SHIFT, 1), middle))

    for x in range(BX):
        put_rows(temp_v, x, joined(mid_ends[x + 1], ends[x + 1]))
        SP[x] = joined(mid_perm[x], perm_sens[x])
        SD[x] = joined(mid_disp[x], disp_sens[x])
        put_rows(sens_v, x, SP[x])
        Z[x] = rows_of(zone, x).astype(jnp.float32)

    copies = [
        pltpu.make_async_copy(temp_v, temp_o, sems.at[0]),
        pltpu.make_async_copy(sens_v, sens_o, sems.at[1]),
    ]
    for copy in copies:
        copy.start()

    def of_zone(z, carry):
        zf = z.astype(jnp.float32)
        total_p = jnp.zeros((NZ, BY), jnp.float32)
        total_d = jnp.zeros((NZ, BY), jnp.float32)
        for x in range(BX):
            here = Z[x] == zf
            total_p = total_p + jnp.where(here, SP[x], 0.0)
            total_d = total_d + jnp.where(here, SD[x], 0.0)
        PART[z] = jnp.sum(total_p.reshape(4, 8, BY), axis=0)
        PART[z + 64] = jnp.sum(total_d.reshape(4, 8, BY), axis=0)
        return carry

    lax.fori_loop(0, 64, of_zone, 0, unroll=8)
    per_lane = jnp.sum(PART[...], axis=1)
    sums_o[...] = lax.dot_general(
        jnp.ones((8, BY), jnp.float32),
        per_lane,
        (((1,), (1,)), ((), ())),
        precision=lax.Precision.HIGHEST,
        preferred_element_type=jnp.float32,
    )
    for copy in copies:
        copy.wait()


def shifted(array, axis, by):
    size = lax.axis_size(axis)
    pairs = [(i, i + by) for i in range(size) if 0 <= i + by < size]
    return lax.ppermute(array, axis, pairs)


def spread_sum(array, axis):
    size = lax.axis_size(axis)
    copies = jnp.broadcast_to(array[None], (size,) + array.shape)
    return lax.all_to_all(copies, axis, 0, 0).sum(0)


def f32(*shape):
    return jax.ShapeDtypeStruct(shape, jnp.float32)


def buf(*shape):
    return pltpu.VMEM(shape, jnp.float32)


SOLVE = [buf(WX, NZ, BY)] * 19 + ([buf(23, NZ, BY)] * 3 + [buf(23, 8, BY)]) * 3


def body(zone_ids, log_perm, log_disp, temp_start, pressure_start, temp_observed, well_cells, well_flow, plan, inject_temp):
    flat = (NZ * BX, BY)
    zone = zone_ids.reshape(flat)
    press = pressure_start.reshape(flat)
    temp = temp_start.reshape(flat)
    seen = temp_observed.reshape(flat)
    grid_rows = BX * lax.axis_size("gx")
    grid_cols = BY * lax.axis_size("gy")

    to_up, to_down, to_up2, to_down2 = pl.pallas_call(
        pack_rows_kernel,
        out_shape=(f32(SIDE, NZ, BY), f32(SIDE, NZ, BY), f32(FAR, NZ, BY), f32(FAR, NZ, BY)),
        in_specs=[VMEM] * 4,
        out_specs=(VMEM,) * 4,
        compiler_params=FULL,
        name="pack_rows",
    )(zone, press, temp, seen)
    up = shifted(to_up, "gx", 1)
    down = shifted(to_down, "gx", -1)
    up2 = shifted(to_up2, "gx", 2)
    down2 = shifted(to_down2, "gx", -2)

    corner = jnp.stack([lax.axis_index("gx") * BX, lax.axis_index("gy") * BY]).astype(jnp.int32)
    source, heat, rim_source, rim_heat, table = pl.pallas_call(
        lambda *refs: wells_kernel(grid_rows, grid_cols, *refs),
        out_shape=(f32(WX, NZ, BY),) * 4 + (f32(8, BY),),
        in_specs=[SMEM] + [VMEM] * 6,
        out_specs=(VMEM,) * 5,
        compiler_params=PARAMS,
        cost_estimate=pl.CostEstimate(flops=1 << 28, bytes_accessed=2 << 20, transcendentals=0),
        name="wells",
    )(corner, well_cells[None], well_flow[None], plan, inject_temp, log_perm[None], log_disp[None])

    to_right, to_left = pl.pallas_call(
        pack_columns_kernel,
        out_shape=(f32(EDGE, NZ, BY), f32(EDGE, NZ, BY)),
        in_specs=[VMEM] * 8 + [pl.BlockSpec(memory_space=pl.ANY)],
        out_specs=(VMEM,) * 2,
        compiler_params=PARAMS,
        name="pack_columns",
    )(zone, press, temp, seen, up, down, up2, down2, table)
    left = shifted(to_right, "gy", 1)
    right = shifted(to_left, "gy", -1)

    own = (f32(9, NZ, BY), f32(BX, NZ, BY), f32(BX, NZ, BY))
    mid_ends, mid_perm, mid_disp = pl.pallas_call(
        middle_kernel,
        out_shape=own,
        in_specs=[VMEM] * 8 + [pl.BlockSpec(memory_space=pl.ANY)] + [VMEM] * 3,
        out_specs=(VMEM,) * 3,
        scratch_shapes=SOLVE,
        compiler_params=PARAMS,
        cost_estimate=pl.CostEstimate(flops=1 << 28, bytes_accessed=4 << 20, transcendentals=0),
        name="middle",
    )(zone, press, temp, seen, up, down, up2, down2, to_right, source, heat, table)
    temp_end, sens, sums = pl.pallas_call(
        rim_kernel,
        out_shape=(f32(*flat), f32(*flat), f32(8, BY)),
        in_specs=[VMEM] * 16,
        out_specs=(pl.BlockSpec(memory_space=pl.ANY), pl.BlockSpec(memory_space=pl.ANY), VMEM),
        scratch_shapes=[buf(9, NZ, BY), buf(BX, NZ, BY), buf(BX, NZ, BY)]
        + [buf(BX, NZ, BY)] * 3
        + [buf(128, 8, BY), buf(*flat), buf(*flat), pltpu.SemaphoreType.DMA((2,))]
        + SOLVE,
        compiler_params=PARAMS,
        name="rims",
    )(
        zone, press, temp, seen, up, down, up2, down2, left, right, rim_source, rim_heat, table,
        mid_ends, mid_perm, mid_disp,
    )

    totals = spread_sum(sums[0:1], ("season", "gx"))
    totals = spread_sum(totals, "gy")
    cells = lax.axis_size("season") * NZ * grid_rows * grid_cols
    gradient = totals.reshape(2, 64) * (cells / 64) ** (-0.5)
    return (temp_end.reshape(temp_start.shape), sens.reshape(temp_start.shape), gradient)


def solution(mesh):
    in_specs = (
        P(None, "gx", "gy"),
        P(),
        P(),
        P("season", None, "gx", "gy"),
        P("season", None, "gx", "gy"),
        P("season", None, "gx", "gy"),
        P(),
        P(),
        P("season", None),
        P("season", None),
    )
    out_specs = (P("season", None, "gx", "gy"), P("season", None, "gx", "gy"), P())
    return jax.shard_map(body, mesh=mesh, in_specs=in_specs, out_specs=out_specs, check_vma=False)
```

time: 95.9 us -> 94.1 us (0.981)
  waiting for transfers between devices: 2.47 us -> 9.52 us
  starting transfers between devices: 25.7 us -> 18.8 us
  blocking collectives: 45.5 us -> 41.6 us
  Pallas kernels: 19.5 us -> 21.5 us
    ppermute x8 -> x6, waiting for transfers between devices: 2.47 us -> 9.52 us  [shifted(): return lax.ppermute(array, axis, pairs)]
    ppermute x8 -> x6, starting transfers between devices: 25.7 us -> 18.8 us  [shifted(): return lax.ppermute(array, axis, pairs)]
    all_to_all x2, blocking collectives: 45.5 us -> 41.6 us  [spread_sum(): return lax.all_to_all(copies, axis, 0, 0).sum(0)]
    pallas_call x3, Pallas kernels: 14.9 us -> 16.6 us  [the longest x1 10.5 us: body(): pl.pallas_call(rim_kernel, out_shape=(f32(*flat), f32(*flat), f32(8, BY))...]
  transfers between devices with their start and end apart: 8 -> 6, of which waited for: 2 -> 2; matrix products, arithmetic and copies ran while one was open for 0% -> 0% of each run, Pallas kernels for 5% -> 9%
where the time goes in v3:
time: 94.1 us; the launch traced here: 93.7 us
  blocking collectives  41.6 us (44%)
  Pallas kernels  21.5 us (23%)
  starting transfers between devices  18.8 us (20%)
  waiting for transfers between devices  9.52 us (10%)
  local copies, waits for them, and re-layouts  1.32 us (1%)
    all_to_all x2, blocking collectives, spread_sum(): return lax.all_to_all(copies, axis, 0, 0).sum(0)  41.6 us
    ppermute x6, starting transfers between devices, shifted(): return lax.ppermute(array, axis, pairs)  18.8 us
    pallas_call x1, Pallas kernels, body(): pl.pallas_call(rim_kernel, out_shape=(f32(*flat), f32(*flat), f32(8, BY))...  10.5 us
    ppermute x6, waiting for transfers between devices, shifted(): return lax.ppermute(array, axis, pairs)  9.52 us
    pallas_call x1, Pallas kernels, body(): pl.pallas_call(middle_kernel, out_shape=own, in_specs=[VMEM] * 8 + [pl.Bl...  5.49 us
    pallas_call x1, Pallas kernels, body(): pl.pallas_call(lambda *refs: wells_kernel(grid_rows, grid_cols, *refs), o...  2.65 us
    pallas_call x1, Pallas kernels, body(): pl.pallas_call(pack_rows_kernel, out_shape=(f32(SIDE, NZ, BY), f32(SIDE,...  2.31 us
  transfers between devices with their start and end apart: 6, of which 2 were waited for; matrix products, arithmetic and copies ran while one was open for 0% of the time, Pallas kernels for 9%

profile of v3, /device:TPU:1, one launch (start us, length us, event | category | flops | bytes accessed | tf_op | source)
XLA Modules:
  0.0 93.7 jit_solution(16718898428226371257)
XLA Ops:
  0.6 2.3 %pack_rows.1 = (f32[27,32,128]{2,1,0:T(8,128)}, f32[27,32,128]{2,1,0:T(8,128)}, f32[4,32,128]{2,1,0:T(8,128)}, f32[4,32,128]{2,1,0:T(8,128)}) custom-call(s32[256,128]{1,0:T(8,128)} %bitcast.16, f32[256,128]{1,0:T(8,128)} %bitcast.20, f32[256,128]{1,0:T(8,128)} %bitcast.24, f32[256,128]{1,0:T(8,128)} %bitcast.28), custom_call_target="tpu_custom_call" | custom-call | tf_op jit(solution)/shard_map/pack_rows/pallas_call | solution.py:536
  2.9 5.6 %collective-permute-start = (f32[27,32,128]{2,1,0:T(8,128)}, f32[27,32,128]{2,1,0:T(8,128)S(1)}, u32[]{:S(2)}, u32[]{:S(2)}) collective-permute-start(f32[27,32,128]{2,1,0:T(8,128)} %get-tuple-element.20), channel_id=1, source_target_pairs={{0,16},{16,32},{32,48},{48,64},{64,80},{80,96},{96,112},{1,17},{17... | collective-permute-start | bytes 1327112 | tf_op jit(solution)/shard_map/ppermute | solution.py:507
  8.6 1.3 %collective-permute-start.1 = (f32[27,32,128]{2,1,0:T(8,128)}, f32[27,32,128]{2,1,0:T(8,128)S(1)}, u32[]{:S(2)}, u32[]{:S(2)}) collective-permute-start(f32[27,32,128]{2,1,0:T(8,128)} %get-tuple-element.21), channel_id=1, source_target_pairs={{16,0},{32,16},{48,32},{64,48},{80,64},{96,80},{112,96},{17,1},{33... | collective-permute-start | bytes 1327112 | tf_op jit(solution)/shard_map/ppermute | solution.py:507
  9.9 0.0 copy-start.7
  9.9 4.9 %collective-permute-start.2 = (f32[4,32,128]{2,1,0:T(8,128)}, f32[4,32,128]{2,1,0:T(8,128)S(1)}, u32[]{:S(2)}, u32[]{:S(2)}) collective-permute-start(f32[4,32,128]{2,1,0:T(8,128)} %get-tuple-element.22), channel_id=1, source_target_pairs={{0,32},{16,48},{32,64},{48,80},{64,96},{80,112},{1,33},{17,49},{33... | collective-permute-start | bytes 196616 | tf_op jit(solution)/shard_map/ppermute | solution.py:507
  14.8 1.3 %collective-permute-start.3 = (f32[4,32,128]{2,1,0:T(8,128)}, f32[4,32,128]{2,1,0:T(8,128)S(1)}, u32[]{:S(2)}, u32[]{:S(2)}) collective-permute-start(f32[4,32,128]{2,1,0:T(8,128)} %get-tuple-element.23), channel_id=1, source_target_pairs={{32,0},{48,16},{64,32},{80,48},{96,64},{112,80},{33,1},{49,17},{65... | collective-permute-start | bytes 196616 | tf_op jit(solution)/shard_map/ppermute | solution.py:507
  16.1 0.0 copy-start.6
  16.1 0.0 copy-start.5
  16.2 0.0 copy-start.4
  16.2 0.1 pad_add_fusion.refs_0_
  16.2 0.0 copy-done.8
  16.2 0.0 copy-done.9
  16.2 0.0 copy-done.7
  16.2 0.6 copy-done.6
  16.8 0.0 copy-done.5
  16.8 0.0 copy-done.4
  16.9 2.6 %wells.1 = (f32[28,32,128]{2,1,0:T(8,128)S(1)}, f32[28,32,128]{2,1,0:T(8,128)S(1)}, f32[28,32,128]{2,1,0:T(8,128)S(1)}, f32[28,32,128]{2,1,0:T(8,128)S(1)}, f32[8,128]{1,0:T(8,128)S(1)}) custom-call(s32[2]{0:T(128)S(1)} %pad_add_fusion.refs_0_, s32[1,2048]{1,0:T(1,128)S(1)} %bitcast.32, f32[1,2048]{1,0:T(1,128)S(1)} %bitcast.33, s32[1,2048]{1,0:T(1,128)S(1)} %copy-done.6, ...), custom_call_target="tpu_custom_call" | custom-call | flops 268435456 | bytes 2097152 | tf_op jit(solution)/shard_map/wells/pallas_call | solution.py:550
  19.5 1.2 %collective-permute-done.2.up2 = f32[4,32,128]{2,1,0:T(8,128)S(1)} collective-permute-done((f32[4,32,128]{2,1,0:T(8,128)}, f32[4,32,128]{2,1,0:T(8,128)S(1)}, u32[]{:S(2)}, u32[]{:S(2)}) %collective-permute-start.2) | collective-permute-done | bytes 65568 | tf_op jit(solution)/shard_map/ppermute | solution.py:507
  20.7 0.0 collective-permute-done.3.down2
  20.7 0.0 collective-permute-done.up
  20.7 8.3 %collective-permute-done.1.down = f32[27,32,128]{2,1,0:T(8,128)S(1)} collective-permute-done((f32[27,32,128]{2,1,0:T(8,128)}, f32[27,32,128]{2,1,0:T(8,128)S(1)}, u32[]{:S(2)}, u32[]{:S(2)}) %collective-permute-start.1) | collective-permute-done | bytes 442400 | tf_op jit(solution)/shard_map/ppermute | solution.py:507
  29.0 0.0 copy-done.2
  29.1 0.6 pack_columns.1
  29.6 1.3 %collective-permute-start.5 = (f32[11,32,128]{2,1,0:T(8,128)S(1)}, f32[11,32,128]{2,1,0:T(8,128)S(1)}, u32[]{:S(2)}, u32[]{:S(2)}) collective-permute-start(f32[11,32,128]{2,1,0:T(8,128)S(1)} %get-tuple-element.26), channel_id=1, source_target_pairs={{1,0},{2,1},{3,2},{4,3},{5,4},{6,5},{7,6},{8,7},{9,8},{10,9},{11,1... | collective-permute-start | bytes 540680 | tf_op jit(solution)/shard_map/ppermute | solution.py:507
  30.9 4.4 %collective-permute-start.4 = (f32[11,32,128]{2,1,0:T(8,128)S(1)}, f32[11,32,128]{2,1,0:T(8,128)S(1)}, u32[]{:S(2)}, u32[]{:S(2)}) collective-permute-start(f32[11,32,128]{2,1,0:T(8,128)S(1)} %get-tuple-element.25.after), channel_id=1, source_target_pairs={{0,1},{1,2},{2,3},{3,4},{4,5},{5,6},{6,7},{7,8},{8,9},{9,10},{10,1... | collective-permute-start | bytes 540680 | tf_op jit(solution)/shard_map/ppermute | solution.py:507
  35.3 5.5 %middle.1 = (f32[9,32,128]{2,1,0:T(8,128)S(1)}, f32[8,32,128]{2,1,0:T(8,128)S(1)}, f32[8,32,128]{2,1,0:T(8,128)S(1)}) custom-call(s32[256,128]{1,0:T(8,128)S(1)} %bitcast.18, f32[256,128]{1,0:T(8,128)S(1)} %bitcast.22, f32[256,128]{1,0:T(8,128)S(1)} %bitcast.26, f32[256,128]{1,0:T(8,128)S(1)} %bitcast.30, f32[27,32,128]{2,1,0:T(8,128)S(1)} %collective-permute-done.up, ...), custom_call_target="tpu_custom_call" | custom-call | flops 268435456 | bytes 4194304 | tf_op jit(solution)/shard_map/middle/pallas_call | solution.py:572
  40.8 0.0 collective-permute-done.5.right
  40.8 0.0 collective-permute-done.4.left
  40.8 10.5 %rims.1 = (f32[256,128]{1,0:T(8,128)}, f32[256,128]{1,0:T(8,128)}, f32[8,128]{1,0:T(8,128)S(1)}) custom-call(s32[256,128]{1,0:T(8,128)S(1)} %bitcast.19, f32[256,128]{1,0:T(8,128)S(1)} %bitcast.23, f32[256,128]{1,0:T(8,128)S(1)} %bitcast.27, f32[256,128]{1,0:T(8,128)S(1)} %bitcast.31, f32[27,32,128]{2,1,0:T(8,128)S(1)} %collective-permute-done.up, ...), custom_call_target="tpu_custom_call" | custom-call | tf_op jit(solution)/shard_map/rims/pallas_call | solution.py:582
  51.4 15.6 %all_to_all.10 = f32[32,1,128]{2,1,0:T(1,128)S(1)} all-to-all(f32[32,1,128]{2,1,0:T(1,128)S(1)} %broadcast_in_dim.31), channel_id=1, replica_groups=mesh['season'=4,'gx'=8,'gy'=16] {'season','gx'}, dimensions={0} | all-to-all | bytes 32768 | tf_op jit(solution)/shard_map/all_to_all | solution.py:513
  67.0 26.0 %all_to_all.11 = f32[16,1,128]{2,1,0:T(1,128)S(1)} all-to-all(f32[16,1,128]{2,1,0:T(1,128)S(1)} %broadcast_in_dim.32), channel_id=1, replica_groups=mesh['season'=4,'gx'=8,'gy'=16] {'gy'}, dimensions={0} | all-to-all | bytes 16384 | tf_op jit(solution)/shard_map/all_to_all | solution.py:513
  93.1 0.6 mul.19
  (15 shorter events, 0.1 us)
Async XLA Ops:
  2.9 13.3 %copy-start.8 = (f32[64]{0:T(128)S(1)}, f32[64]{0:T(128)}, u32[]{:S(2)}) copy-start(f32[64]{0:T(128)} %param.11) | copy-start | bytes 772
  2.9 13.3 %copy-start.9 = (f32[64]{0:T(128)S(1)}, f32[64]{0:T(128)}, u32[]{:S(2)}) copy-start(f32[64]{0:T(128)} %param.12) | copy-start | bytes 772
  2.9 17.8 %collective-permute-start = (f32[27,32,128]{2,1,0:T(8,128)}, f32[27,32,128]{2,1,0:T(8,128)S(1)}, u32[]{:S(2)}, u32[]{:S(2)}) collective-permute-start(f32[27,32,128]{2,1,0:T(8,128)} %get-tuple-element.20), channel_id=1, source_target_pairs={{0,16},{16,32},{32,48},{48,64},{64,80},{80,96},{96,112},{1,17},{17... | collective-permute-start | bytes 1327112 | tf_op jit(solution)/shard_map/ppermute | solution.py:507
  8.6 20.5 %collective-permute-start.1 = (f32[27,32,128]{2,1,0:T(8,128)}, f32[27,32,128]{2,1,0:T(8,128)S(1)}, u32[]{:S(2)}, u32[]{:S(2)}) collective-permute-start(f32[27,32,128]{2,1,0:T(8,128)} %get-tuple-element.21), channel_id=1, source_target_pairs={{16,0},{32,16},{48,32},{64,48},{80,64},{96,80},{112,96},{17,1},{33... | collective-permute-start | bytes 1327112 | tf_op jit(solution)/shard_map/ppermute | solution.py:507
  9.9 6.4 %copy-start.7 = (f32[1,2048]{1,0:T(1,128)S(1)}, f32[1,2048]{1,0:T(1,128)}, u32[]{:S(2)}) copy-start(f32[1,2048]{1,0:T(1,128)} %refs_4_.1) | copy-start | bytes 24580
  9.9 10.8 %collective-permute-start.2 = (f32[4,32,128]{2,1,0:T(8,128)}, f32[4,32,128]{2,1,0:T(8,128)S(1)}, u32[]{:S(2)}, u32[]{:S(2)}) collective-permute-start(f32[4,32,128]{2,1,0:T(8,128)} %get-tuple-element.22), channel_id=1, source_target_pairs={{0,32},{16,48},{32,64},{48,80},{64,96},{80,112},{1,33},{17,49},{33... | collective-permute-start | bytes 196616 | tf_op jit(solution)/shard_map/ppermute | solution.py:507
  14.8 5.9 %collective-permute-start.3 = (f32[4,32,128]{2,1,0:T(8,128)}, f32[4,32,128]{2,1,0:T(8,128)S(1)}, u32[]{:S(2)}, u32[]{:S(2)}) collective-permute-start(f32[4,32,128]{2,1,0:T(8,128)} %get-tuple-element.23), channel_id=1, source_target_pairs={{32,0},{48,16},{64,32},{80,48},{96,64},{112,80},{33,1},{49,17},{65... | collective-permute-start | bytes 196616 | tf_op jit(solution)/shard_map/ppermute | solution.py:507
  16.1 0.7 copy-start.6
  16.1 0.7 copy-start.5
  16.2 0.7 copy-start.4
  16.9 12.2 %copy-start = (s32[32,8,128]{2,1,0:T(8,128)S(1)}, s32[32,8,128]{2,1,0:T(8,128)}, u32[]{:S(2)}) copy-start(s32[32,8,128]{2,1,0:T(8,128)} %param.10) | copy-start | bytes 393220
  16.9 12.2 %copy-start.1 = (f32[1,32,8,128]{3,2,1,0:T(8,128)S(1)}, f32[1,32,8,128]{3,2,1,0:T(8,128)}, u32[]{:S(2)}) copy-start(f32[1,32,8,128]{3,2,1,0:T(8,128)} %param.14) | copy-start | bytes 393220
  16.9 12.2 %copy-start.2 = (f32[1,32,8,128]{3,2,1,0:T(8,128)S(1)}, f32[1,32,8,128]{3,2,1,0:T(8,128)}, u32[]{:S(2)}) copy-start(f32[1,32,8,128]{3,2,1,0:T(8,128)} %param.13) | copy-start | bytes 393220
  16.9 12.2 %copy-start.3 = (f32[1,32,8,128]{3,2,1,0:T(8,128)S(1)}, f32[1,32,8,128]{3,2,1,0:T(8,128)}, u32[]{:S(2)}) copy-start(f32[1,32,8,128]{3,2,1,0:T(8,128)} %param.15) | copy-start | bytes 393220
  29.6 11.2 %collective-permute-start.5 = (f32[11,32,128]{2,1,0:T(8,128)S(1)}, f32[11,32,128]{2,1,0:T(8,128)S(1)}, u32[]{:S(2)}, u32[]{:S(2)}) collective-permute-start(f32[11,32,128]{2,1,0:T(8,128)S(1)} %get-tuple-element.26), channel_id=1, source_target_pairs={{1,0},{2,1},{3,2},{4,3},{5,4},{6,5},{7,6},{8,7},{9,8},{10,9},{11,1... | collective-permute-start | bytes 540680 | tf_op jit(solution)/shard_map/ppermute | solution.py:507
  30.9 9.9 %collective-permute-start.4 = (f32[11,32,128]{2,1,0:T(8,128)S(1)}, f32[11,32,128]{2,1,0:T(8,128)S(1)}, u32[]{:S(2)}, u32[]{:S(2)}) collective-permute-start(f32[11,32,128]{2,1,0:T(8,128)S(1)} %get-tuple-element.25.after), channel_id=1, source_target_pairs={{0,1},{1,2},{2,3},{3,4},{4,5},{5,6},{6,7},{7,8},{8,9},{9,10},{10,1... | collective-permute-start | bytes 540680 | tf_op jit(solution)/shard_map/ppermute | solution.py:507

commit v4 on v3

--- a/solution.py
+++ b/solution.py
@@ -324,7 +324,7 @@
 
     first = face_x(4)[0]
     first = lax.fori_loop(5, 9, transport(False), first, unroll=True)
-    first = lax.fori_loop(9, 18, transport(True), first, unroll=True)
+    first = lax.fori_loop(9, 18, transport(True), first, unroll=3)
     lax.fori_loop(18, 23, transport(False), first, unroll=True)
 
     def lift(a, b8):
@@ -488,7 +488,7 @@
         PART[z + 64] = jnp.sum(total_d.reshape(4, 8, BY), axis=0)
         return carry
 
-    lax.fori_loop(0, 64, of_zone, 0, unroll=8)
+    lax.fori_loop(0, 64, of_zone, 0, unroll=16)
     per_lane = jnp.sum(PART[...], axis=1)
     sums_o[...] = lax.dot_general(
         jnp.ones((8, BY), jnp.float32),

time: 94.1 us -> 93.6 us (level)
  transfers between devices with their start and end apart: 6 -> 6, of which waited for: 2 -> 2; matrix products, arithmetic and copies ran while one was open for 0% -> 0% of each run, Pallas kernels for 9% -> 8%
where the time goes in v4:
time: 93.6 us; the launch traced here: 93.2 us
  blocking collectives  41.6 us (44%)
  Pallas kernels  21 us (22%)
  starting transfers between devices  18.8 us (20%)
  waiting for transfers between devices  9.52 us (10%)
  local copies, waits for them, and re-layouts  1.32 us (1%)
    all_to_all x2, blocking collectives, spread_sum(): return lax.all_to_all(copies, axis, 0, 0).sum(0)  41.6 us
    ppermute x6, starting transfers between devices, shifted(): return lax.ppermute(array, axis, pairs)  18.8 us
    pallas_call x1, Pallas kernels, body(): pl.pallas_call(rim_kernel, out_shape=(f32(*flat), f32(*flat), f32(8, BY))...  10.2 us
    ppermute x6, waiting for transfers between devices, shifted(): return lax.ppermute(array, axis, pairs)  9.52 us
    pallas_call x1, Pallas kernels, body(): pl.pallas_call(middle_kernel, out_shape=own, in_specs=[VMEM] * 8 + [pl.Bl...  5.24 us
    pallas_call x1, Pallas kernels, body(): pl.pallas_call(lambda *refs: wells_kernel(grid_rows, grid_cols, *refs), o...  2.65 us
    pallas_call x1, Pallas kernels, body(): pl.pallas_call(pack_rows_kernel, out_shape=(f32(SIDE, NZ, BY), f32(SIDE,...  2.31 us
  transfers between devices with their start and end apart: 6, of which 2 were waited for; matrix products, arithmetic and copies ran while one was open for 0% of the time, Pallas kernels for 8%

profile of v4, /device:TPU:1, one launch (start us, length us, event | category | flops | bytes accessed | tf_op | source)
XLA Modules:
  0.0 93.2 jit_solution(13541227321899310665)
XLA Ops:
  0.6 2.3 %pack_rows.1 = (f32[27,32,128]{2,1,0:T(8,128)}, f32[27,32,128]{2,1,0:T(8,128)}, f32[4,32,128]{2,1,0:T(8,128)}, f32[4,32,128]{2,1,0:T(8,128)}) custom-call(s32[256,128]{1,0:T(8,128)} %bitcast.16, f32[256,128]{1,0:T(8,128)} %bitcast.20, f32[256,128]{1,0:T(8,128)} %bitcast.24, f32[256,128]{1,0:T(8,128)} %bitcast.28), custom_call_target="tpu_custom_call" | custom-call | tf_op jit(solution)/shard_map/pack_rows/pallas_call | solution.py:536
  2.9 5.6 %collective-permute-start = (f32[27,32,128]{2,1,0:T(8,128)}, f32[27,32,128]{2,1,0:T(8,128)S(1)}, u32[]{:S(2)}, u32[]{:S(2)}) collective-permute-start(f32[27,32,128]{2,1,0:T(8,128)} %get-tuple-element.20), channel_id=1, source_target_pairs={{0,16},{16,32},{32,48},{48,64},{64,80},{80,96},{96,112},{1,17},{17... | collective-permute-start | bytes 1327112 | tf_op jit(solution)/shard_map/ppermute | solution.py:507
  8.6 1.3 %collective-permute-start.1 = (f32[27,32,128]{2,1,0:T(8,128)}, f32[27,32,128]{2,1,0:T(8,128)S(1)}, u32[]{:S(2)}, u32[]{:S(2)}) collective-permute-start(f32[27,32,128]{2,1,0:T(8,128)} %get-tuple-element.21), channel_id=1, source_target_pairs={{16,0},{32,16},{48,32},{64,48},{80,64},{96,80},{112,96},{17,1},{33... | collective-permute-start | bytes 1327112 | tf_op jit(solution)/shard_map/ppermute | solution.py:507
  9.9 0.0 copy-start.7
  9.9 4.9 %collective-permute-start.2 = (f32[4,32,128]{2,1,0:T(8,128)}, f32[4,32,128]{2,1,0:T(8,128)S(1)}, u32[]{:S(2)}, u32[]{:S(2)}) collective-permute-start(f32[4,32,128]{2,1,0:T(8,128)} %get-tuple-element.22), channel_id=1, source_target_pairs={{0,32},{16,48},{32,64},{48,80},{64,96},{80,112},{1,33},{17,49},{33... | collective-permute-start | bytes 196616 | tf_op jit(solution)/shard_map/ppermute | solution.py:507
  14.8 1.3 %collective-permute-start.3 = (f32[4,32,128]{2,1,0:T(8,128)}, f32[4,32,128]{2,1,0:T(8,128)S(1)}, u32[]{:S(2)}, u32[]{:S(2)}) collective-permute-start(f32[4,32,128]{2,1,0:T(8,128)} %get-tuple-element.23), channel_id=1, source_target_pairs={{32,0},{48,16},{64,32},{80,48},{96,64},{112,80},{33,1},{49,17},{65... | collective-permute-start | bytes 196616 | tf_op jit(solution)/shard_map/ppermute | solution.py:507
  16.1 0.0 copy-start.6
  16.1 0.0 copy-start.5
  16.2 0.0 copy-start.4
  16.2 0.1 pad_add_fusion.refs_0_
  16.2 0.0 copy-done.8
  16.2 0.0 copy-done.9
  16.2 0.0 copy-done.7
  16.2 0.6 copy-done.6
  16.8 0.0 copy-done.5
  16.8 0.0 copy-done.4
  16.9 2.6 %wells.1 = (f32[28,32,128]{2,1,0:T(8,128)S(1)}, f32[28,32,128]{2,1,0:T(8,128)S(1)}, f32[28,32,128]{2,1,0:T(8,128)S(1)}, f32[28,32,128]{2,1,0:T(8,128)S(1)}, f32[8,128]{1,0:T(8,128)S(1)}) custom-call(s32[2]{0:T(128)S(1)} %pad_add_fusion.refs_0_, s32[1,2048]{1,0:T(1,128)S(1)} %bitcast.32, f32[1,2048]{1,0:T(1,128)S(1)} %bitcast.33, s32[1,2048]{1,0:T(1,128)S(1)} %copy-done.6, ...), custom_call_target="tpu_custom_call" | custom-call | flops 268435456 | bytes 2097152 | tf_op jit(solution)/shard_map/wells/pallas_call | solution.py:550
  19.5 1.2 %collective-permute-done.2.up2 = f32[4,32,128]{2,1,0:T(8,128)S(1)} collective-permute-done((f32[4,32,128]{2,1,0:T(8,128)}, f32[4,32,128]{2,1,0:T(8,128)S(1)}, u32[]{:S(2)}, u32[]{:S(2)}) %collective-permute-start.2) | collective-permute-done | bytes 65568 | tf_op jit(solution)/shard_map/ppermute | solution.py:507
  20.7 0.0 collective-permute-done.3.down2
  20.7 0.0 collective-permute-done.up
  20.7 8.3 %collective-permute-done.1.down = f32[27,32,128]{2,1,0:T(8,128)S(1)} collective-permute-done((f32[27,32,128]{2,1,0:T(8,128)}, f32[27,32,128]{2,1,0:T(8,128)S(1)}, u32[]{:S(2)}, u32[]{:S(2)}) %collective-permute-start.1) | collective-permute-done | bytes 442400 | tf_op jit(solution)/shard_map/ppermute | solution.py:507
  29.1 0.0 copy-done.3
  29.1 0.6 pack_columns.1
  29.6 1.3 %collective-permute-start.5 = (f32[11,32,128]{2,1,0:T(8,128)S(1)}, f32[11,32,128]{2,1,0:T(8,128)S(1)}, u32[]{:S(2)}, u32[]{:S(2)}) collective-permute-start(f32[11,32,128]{2,1,0:T(8,128)S(1)} %get-tuple-element.26), channel_id=1, source_target_pairs={{1,0},{2,1},{3,2},{4,3},{5,4},{6,5},{7,6},{8,7},{9,8},{10,9},{11,1... | collective-permute-start | bytes 540680 | tf_op jit(solution)/shard_map/ppermute | solution.py:507
  30.9 4.4 %collective-permute-start.4 = (f32[11,32,128]{2,1,0:T(8,128)S(1)}, f32[11,32,128]{2,1,0:T(8,128)S(1)}, u32[]{:S(2)}, u32[]{:S(2)}) collective-permute-start(f32[11,32,128]{2,1,0:T(8,128)S(1)} %get-tuple-element.25.after), channel_id=1, source_target_pairs={{0,1},{1,2},{2,3},{3,4},{4,5},{5,6},{6,7},{7,8},{8,9},{9,10},{10,1... | collective-permute-start | bytes 540680 | tf_op jit(solution)/shard_map/ppermute | solution.py:507
  35.3 5.2 %middle.1 = (f32[9,32,128]{2,1,0:T(8,128)S(1)}, f32[8,32,128]{2,1,0:T(8,128)S(1)}, f32[8,32,128]{2,1,0:T(8,128)S(1)}) custom-call(s32[256,128]{1,0:T(8,128)S(1)} %bitcast.18, f32[256,128]{1,0:T(8,128)S(1)} %bitcast.22, f32[256,128]{1,0:T(8,128)S(1)} %bitcast.26, f32[256,128]{1,0:T(8,128)S(1)} %bitcast.30, f32[27,32,128]{2,1,0:T(8,128)S(1)} %collective-permute-done.up, ...), custom_call_target="tpu_custom_call" | custom-call | flops 268435456 | bytes 4194304 | tf_op jit(solution)/shard_map/middle/pallas_call | solution.py:572
  40.6 0.0 collective-permute-done.5.right
  40.6 0.0 collective-permute-done.4.left
  40.6 10.2 %rims.1 = (f32[256,128]{1,0:T(8,128)}, f32[256,128]{1,0:T(8,128)}, f32[8,128]{1,0:T(8,128)S(1)}) custom-call(s32[256,128]{1,0:T(8,128)S(1)} %bitcast.19, f32[256,128]{1,0:T(8,128)S(1)} %bitcast.23, f32[256,128]{1,0:T(8,128)S(1)} %bitcast.27, f32[256,128]{1,0:T(8,128)S(1)} %bitcast.31, f32[27,32,128]{2,1,0:T(8,128)S(1)} %collective-permute-done.up, ...), custom_call_target="tpu_custom_call" | custom-call | tf_op jit(solution)/shard_map/rims/pallas_call | solution.py:582
  50.9 15.6 %all_to_all.10 = f32[32,1,128]{2,1,0:T(1,128)S(1)} all-to-all(f32[32,1,128]{2,1,0:T(1,128)S(1)} %broadcast_in_dim.31), channel_id=1, replica_groups=mesh['season'=4,'gx'=8,'gy'=16] {'season','gx'}, dimensions={0} | all-to-all | bytes 32768 | tf_op jit(solution)/shard_map/all_to_all | solution.py:513
  66.5 26.0 %all_to_all.11 = f32[16,1,128]{2,1,0:T(1,128)S(1)} all-to-all(f32[16,1,128]{2,1,0:T(1,128)S(1)} %broadcast_in_dim.32), channel_id=1, replica_groups=mesh['season'=4,'gx'=8,'gy'=16] {'gy'}, dimensions={0} | all-to-all | bytes 16384 | tf_op jit(solution)/shard_map/all_to_all | solution.py:513
  92.6 0.6 mul.19
  (15 shorter events, 0.1 us)
Async XLA Ops:
  2.9 13.3 %copy-start.8 = (f32[64]{0:T(128)S(1)}, f32[64]{0:T(128)}, u32[]{:S(2)}) copy-start(f32[64]{0:T(128)} %param.11) | copy-start | bytes 772
  2.9 13.3 %copy-start.9 = (f32[64]{0:T(128)S(1)}, f32[64]{0:T(128)}, u32[]{:S(2)}) copy-start(f32[64]{0:T(128)} %param.12) | copy-start | bytes 772
  2.9 17.8 %collective-permute-start = (f32[27,32,128]{2,1,0:T(8,128)}, f32[27,32,128]{2,1,0:T(8,128)S(1)}, u32[]{:S(2)}, u32[]{:S(2)}) collective-permute-start(f32[27,32,128]{2,1,0:T(8,128)} %get-tuple-element.20), channel_id=1, source_target_pairs={{0,16},{16,32},{32,48},{48,64},{64,80},{80,96},{96,112},{1,17},{17... | collective-permute-start | bytes 1327112 | tf_op jit(solution)/shard_map/ppermute | solution.py:507
  8.6 20.5 %collective-permute-start.1 = (f32[27,32,128]{2,1,0:T(8,128)}, f32[27,32,128]{2,1,0:T(8,128)S(1)}, u32[]{:S(2)}, u32[]{:S(2)}) collective-permute-start(f32[27,32,128]{2,1,0:T(8,128)} %get-tuple-element.21), channel_id=1, source_target_pairs={{16,0},{32,16},{48,32},{64,48},{80,64},{96,80},{112,96},{17,1},{33... | collective-permute-start | bytes 1327112 | tf_op jit(solution)/shard_map/ppermute | solution.py:507
  9.9 6.4 %copy-start.7 = (f32[1,2048]{1,0:T(1,128)S(1)}, f32[1,2048]{1,0:T(1,128)}, u32[]{:S(2)}) copy-start(f32[1,2048]{1,0:T(1,128)} %refs_4_.1) | copy-start | bytes 24580
  9.9 10.8 %collective-permute-start.2 = (f32[4,32,128]{2,1,0:T(8,128)}, f32[4,32,128]{2,1,0:T(8,128)S(1)}, u32[]{:S(2)}, u32[]{:S(2)}) collective-permute-start(f32[4,32,128]{2,1,0:T(8,128)} %get-tuple-element.22), channel_id=1, source_target_pairs={{0,32},{16,48},{32,64},{48,80},{64,96},{80,112},{1,33},{17,49},{33... | collective-permute-start | bytes 196616 | tf_op jit(solution)/shard_map/ppermute | solution.py:507
  14.8 5.9 %collective-permute-start.3 = (f32[4,32,128]{2,1,0:T(8,128)}, f32[4,32,128]{2,1,0:T(8,128)S(1)}, u32[]{:S(2)}, u32[]{:S(2)}) collective-permute-start(f32[4,32,128]{2,1,0:T(8,128)} %get-tuple-element.23), channel_id=1, source_target_pairs={{32,0},{48,16},{64,32},{80,48},{96,64},{112,80},{33,1},{49,17},{65... | collective-permute-start | bytes 196616 | tf_op jit(solution)/shard_map/ppermute | solution.py:507
  16.1 0.7 copy-start.6
  16.1 0.7 copy-start.5
  16.2 0.7 copy-start.4
  16.9 12.2 %copy-start = (s32[32,8,128]{2,1,0:T(8,128)S(1)}, s32[32,8,128]{2,1,0:T(8,128)}, u32[]{:S(2)}) copy-start(s32[32,8,128]{2,1,0:T(8,128)} %param.10) | copy-start | bytes 393220
  16.9 12.2 %copy-start.1 = (f32[1,32,8,128]{3,2,1,0:T(8,128)S(1)}, f32[1,32,8,128]{3,2,1,0:T(8,128)}, u32[]{:S(2)}) copy-start(f32[1,32,8,128]{3,2,1,0:T(8,128)} %param.14) | copy-start | bytes 393220
  16.9 12.2 %copy-start.2 = (f32[1,32,8,128]{3,2,1,0:T(8,128)S(1)}, f32[1,32,8,128]{3,2,1,0:T(8,128)}, u32[]{:S(2)}) copy-start(f32[1,32,8,128]{3,2,1,0:T(8,128)} %param.13) | copy-start | bytes 393220
  16.9 12.2 %copy-start.3 = (f32[1,32,8,128]{3,2,1,0:T(8,128)S(1)}, f32[1,32,8,128]{3,2,1,0:T(8,128)}, u32[]{:S(2)}) copy-start(f32[1,32,8,128]{3,2,1,0:T(8,128)} %param.15) | copy-start | bytes 393220
  29.6 10.9 %collective-permute-start.5 = (f32[11,32,128]{2,1,0:T(8,128)S(1)}, f32[11,32,128]{2,1,0:T(8,128)S(1)}, u32[]{:S(2)}, u32[]{:S(2)}) collective-permute-start(f32[11,32,128]{2,1,0:T(8,128)S(1)} %get-tuple-element.26), channel_id=1, source_target_pairs={{1,0},{2,1},{3,2},{4,3},{5,4},{6,5},{7,6},{8,7},{9,8},{10,9},{11,1... | collective-permute-start | bytes 540680 | tf_op jit(solution)/shard_map/ppermute | solution.py:507
  30.9 9.6 %collective-permute-start.4 = (f32[11,32,128]{2,1,0:T(8,128)S(1)}, f32[11,32,128]{2,1,0:T(8,128)S(1)}, u32[]{:S(2)}, u32[]{:S(2)}) collective-permute-start(f32[11,32,128]{2,1,0:T(8,128)S(1)} %get-tuple-element.25.after), channel_id=1, source_target_pairs={{0,1},{1,2},{2,3},{3,4},{4,5},{5,6},{6,7},{7,8},{8,9},{9,10},{10,1... | collective-permute-start | bytes 540680 | tf_op jit(solution)/shard_map/ppermute | solution.py:507

commit v5 on v4

--- a/solution.py
+++ b/solution.py
@@ -595,7 +595,7 @@
         mid_ends, mid_perm, mid_disp,
     )
 
-    totals = spread_sum(sums[0:1], ("season", "gx"))
+    totals = spread_sum(sums[0:1], ("gx", "season"))
     totals = spread_sum(totals, "gy")
     cells = lax.axis_size("season") * NZ * grid_rows * grid_cols
     gradient = totals.reshape(2, 64) * (cells / 64) ** (-0.5)

time: 93.6 us -> 93.6 us (level)
  no operation moved by 1% of the time
where the time goes in v5:
time: 93.6 us; the launch traced here: 93.2 us
  blocking collectives  41.6 us (44%)
  Pallas kernels  21 us (22%)
  starting transfers between devices  18.8 us (20%)
  waiting for transfers between devices  9.52 us (10%)
  local copies, waits for them, and re-layouts  1.32 us (1%)
    all_to_all x2, blocking collectives, spread_sum(): return lax.all_to_all(copies, axis, 0, 0).sum(0)  41.6 us
    ppermute x6, starting transfers between devices, shifted(): return lax.ppermute(array, axis, pairs)  18.8 us
    pallas_call x1, Pallas kernels, body(): pl.pallas_call(rim_kernel, out_shape=(f32(*flat), f32(*flat), f32(8, BY))...  10.2 us
    ppermute x6, waiting for transfers between devices, shifted(): return lax.ppermute(array, axis, pairs)  9.52 us
    pallas_call x1, Pallas kernels, body(): pl.pallas_call(middle_kernel, out_shape=own, in_specs=[VMEM] * 8 + [pl.Bl...  5.24 us
    pallas_call x1, Pallas kernels, body(): pl.pallas_call(lambda *refs: wells_kernel(grid_rows, grid_cols, *refs), o...  2.65 us
    pallas_call x1, Pallas kernels, body(): pl.pallas_call(pack_rows_kernel, out_shape=(f32(SIDE, NZ, BY), f32(SIDE,...  2.31 us
  transfers between devices with their start and end apart: 6, of which 2 were waited for; matrix products, arithmetic and copies ran while one was open for 0% of the time, Pallas kernels for 8%

profile of v5, /device:TPU:1, one launch (start us, length us, event | category | flops | bytes accessed | tf_op | source)
XLA Modules:
  0.0 93.2 jit_solution(6040881932163444153)
XLA Ops:
  0.6 2.3 %pack_rows.1 = (f32[27,32,128]{2,1,0:T(8,128)}, f32[27,32,128]{2,1,0:T(8,128)}, f32[4,32,128]{2,1,0:T(8,128)}, f32[4,32,128]{2,1,0:T(8,128)}) custom-call(s32[256,128]{1,0:T(8,128)} %bitcast.16, f32[256,128]{1,0:T(8,128)} %bitcast.20, f32[256,128]{1,0:T(8,128)} %bitcast.24, f32[256,128]{1,0:T(8,128)} %bitcast.28), custom_call_target="tpu_custom_call" | custom-call | tf_op jit(solution)/shard_map/pack_rows/pallas_call | solution.py:536
  2.9 5.6 %collective-permute-start = (f32[27,32,128]{2,1,0:T(8,128)}, f32[27,32,128]{2,1,0:T(8,128)S(1)}, u32[]{:S(2)}, u32[]{:S(2)}) collective-permute-start(f32[27,32,128]{2,1,0:T(8,128)} %get-tuple-element.20), channel_id=1, source_target_pairs={{0,16},{16,32},{32,48},{48,64},{64,80},{80,96},{96,112},{1,17},{17... | collective-permute-start | bytes 1327112 | tf_op jit(solution)/shard_map/ppermute | solution.py:507
  8.6 1.3 %collective-permute-start.1 = (f32[27,32,128]{2,1,0:T(8,128)}, f32[27,32,128]{2,1,0:T(8,128)S(1)}, u32[]{:S(2)}, u32[]{:S(2)}) collective-permute-start(f32[27,32,128]{2,1,0:T(8,128)} %get-tuple-element.21), channel_id=1, source_target_pairs={{16,0},{32,16},{48,32},{64,48},{80,64},{96,80},{112,96},{17,1},{33... | collective-permute-start | bytes 1327112 | tf_op jit(solution)/shard_map/ppermute | solution.py:507
  9.9 0.0 copy-start.7
  9.9 4.9 %collective-permute-start.2 = (f32[4,32,128]{2,1,0:T(8,128)}, f32[4,32,128]{2,1,0:T(8,128)S(1)}, u32[]{:S(2)}, u32[]{:S(2)}) collective-permute-start(f32[4,32,128]{2,1,0:T(8,128)} %get-tuple-element.22), channel_id=1, source_target_pairs={{0,32},{16,48},{32,64},{48,80},{64,96},{80,112},{1,33},{17,49},{33... | collective-permute-start | bytes 196616 | tf_op jit(solution)/shard_map/ppermute | solution.py:507
  14.8 1.3 %collective-permute-start.3 = (f32[4,32,128]{2,1,0:T(8,128)}, f32[4,32,128]{2,1,0:T(8,128)S(1)}, u32[]{:S(2)}, u32[]{:S(2)}) collective-permute-start(f32[4,32,128]{2,1,0:T(8,128)} %get-tuple-element.23), channel_id=1, source_target_pairs={{32,0},{48,16},{64,32},{80,48},{96,64},{112,80},{33,1},{49,17},{65... | collective-permute-start | bytes 196616 | tf_op jit(solution)/shard_map/ppermute | solution.py:507
  16.1 0.0 copy-start.6
  16.1 0.0 copy-start.5
  16.2 0.0 copy-start.4
  16.2 0.1 pad_add_fusion.refs_0_
  16.2 0.0 copy-done.8
  16.2 0.0 copy-done.9
  16.2 0.0 copy-done.7
  16.2 0.6 copy-done.6
  16.8 0.0 copy-done.5
  16.8 0.0 copy-done.4
  16.9 2.6 %wells.1 = (f32[28,32,128]{2,1,0:T(8,128)S(1)}, f32[28,32,128]{2,1,0:T(8,128)S(1)}, f32[28,32,128]{2,1,0:T(8,128)S(1)}, f32[28,32,128]{2,1,0:T(8,128)S(1)}, f32[8,128]{1,0:T(8,128)S(1)}) custom-call(s32[2]{0:T(128)S(1)} %pad_add_fusion.refs_0_, s32[1,2048]{1,0:T(1,128)S(1)} %bitcast.32, f32[1,2048]{1,0:T(1,128)S(1)} %bitcast.33, s32[1,2048]{1,0:T(1,128)S(1)} %copy-done.6, ...), custom_call_target="tpu_custom_call" | custom-call | flops 268435456 | bytes 2097152 | tf_op jit(solution)/shard_map/wells/pallas_call | solution.py:550
  19.5 1.2 %collective-permute-done.2.up2 = f32[4,32,128]{2,1,0:T(8,128)S(1)} collective-permute-done((f32[4,32,128]{2,1,0:T(8,128)}, f32[4,32,128]{2,1,0:T(8,128)S(1)}, u32[]{:S(2)}, u32[]{:S(2)}) %collective-permute-start.2) | collective-permute-done | bytes 65568 | tf_op jit(solution)/shard_map/ppermute | solution.py:507
  20.7 0.0 collective-permute-done.3.down2
  20.7 0.0 collective-permute-done.up
  20.7 8.3 %collective-permute-done.1.down = f32[27,32,128]{2,1,0:T(8,128)S(1)} collective-permute-done((f32[27,32,128]{2,1,0:T(8,128)}, f32[27,32,128]{2,1,0:T(8,128)S(1)}, u32[]{:S(2)}, u32[]{:S(2)}) %collective-permute-start.1) | collective-permute-done | bytes 442400 | tf_op jit(solution)/shard_map/ppermute | solution.py:507
  29.1 0.0 copy-done.3
  29.1 0.6 pack_columns.1
  29.6 1.3 %collective-permute-start.5 = (f32[11,32,128]{2,1,0:T(8,128)S(1)}, f32[11,32,128]{2,1,0:T(8,128)S(1)}, u32[]{:S(2)}, u32[]{:S(2)}) collective-permute-start(f32[11,32,128]{2,1,0:T(8,128)S(1)} %get-tuple-element.26), channel_id=1, source_target_pairs={{1,0},{2,1},{3,2},{4,3},{5,4},{6,5},{7,6},{8,7},{9,8},{10,9},{11,1... | collective-permute-start | bytes 540680 | tf_op jit(solution)/shard_map/ppermute | solution.py:507
  30.9 4.4 %collective-permute-start.4 = (f32[11,32,128]{2,1,0:T(8,128)S(1)}, f32[11,32,128]{2,1,0:T(8,128)S(1)}, u32[]{:S(2)}, u32[]{:S(2)}) collective-permute-start(f32[11,32,128]{2,1,0:T(8,128)S(1)} %get-tuple-element.25.after), channel_id=1, source_target_pairs={{0,1},{1,2},{2,3},{3,4},{4,5},{5,6},{6,7},{7,8},{8,9},{9,10},{10,1... | collective-permute-start | bytes 540680 | tf_op jit(solution)/shard_map/ppermute | solution.py:507
  35.3 5.2 %middle.1 = (f32[9,32,128]{2,1,0:T(8,128)S(1)}, f32[8,32,128]{2,1,0:T(8,128)S(1)}, f32[8,32,128]{2,1,0:T(8,128)S(1)}) custom-call(s32[256,128]{1,0:T(8,128)S(1)} %bitcast.18, f32[256,128]{1,0:T(8,128)S(1)} %bitcast.22, f32[256,128]{1,0:T(8,128)S(1)} %bitcast.26, f32[256,128]{1,0:T(8,128)S(1)} %bitcast.30, f32[27,32,128]{2,1,0:T(8,128)S(1)} %collective-permute-done.up, ...), custom_call_target="tpu_custom_call" | custom-call | flops 268435456 | bytes 4194304 | tf_op jit(solution)/shard_map/middle/pallas_call | solution.py:572
  40.6 0.0 collective-permute-done.5.right
  40.6 0.0 collective-permute-done.4.left
  40.6 10.2 %rims.1 = (f32[256,128]{1,0:T(8,128)}, f32[256,128]{1,0:T(8,128)}, f32[8,128]{1,0:T(8,128)S(1)}) custom-call(s32[256,128]{1,0:T(8,128)S(1)} %bitcast.19, f32[256,128]{1,0:T(8,128)S(1)} %bitcast.23, f32[256,128]{1,0:T(8,128)S(1)} %bitcast.27, f32[256,128]{1,0:T(8,128)S(1)} %bitcast.31, f32[27,32,128]{2,1,0:T(8,128)S(1)} %collective-permute-done.up, ...), custom_call_target="tpu_custom_call" | custom-call | tf_op jit(solution)/shard_map/rims/pallas_call | solution.py:582
  50.9 15.6 %all_to_all.10 = f32[32,1,128]{2,1,0:T(1,128)S(1)} all-to-all(f32[32,1,128]{2,1,0:T(1,128)S(1)} %broadcast_in_dim.31), channel_id=1, replica_groups=mesh['season'=4,'gx'=8,'gy'=16] {'gx','season'}, dimensions={0} | all-to-all | bytes 32768 | tf_op jit(solution)/shard_map/all_to_all | solution.py:513
  66.5 26.0 %all_to_all.11 = f32[16,1,128]{2,1,0:T(1,128)S(1)} all-to-all(f32[16,1,128]{2,1,0:T(1,128)S(1)} %broadcast_in_dim.32), channel_id=1, replica_groups=mesh['season'=4,'gx'=8,'gy'=16] {'gy'}, dimensions={0} | all-to-all | bytes 16384 | tf_op jit(solution)/shard_map/all_to_all | solution.py:513
  92.5 0.6 mul.19
  (15 shorter events, 0.1 us)
Async XLA Ops:
  2.9 13.3 %copy-start.8 = (f32[64]{0:T(128)S(1)}, f32[64]{0:T(128)}, u32[]{:S(2)}) copy-start(f32[64]{0:T(128)} %param.11) | copy-start | bytes 772
  2.9 13.3 %copy-start.9 = (f32[64]{0:T(128)S(1)}, f32[64]{0:T(128)}, u32[]{:S(2)}) copy-start(f32[64]{0:T(128)} %param.12) | copy-start | bytes 772
  2.9 17.8 %collective-permute-start = (f32[27,32,128]{2,1,0:T(8,128)}, f32[27,32,128]{2,1,0:T(8,128)S(1)}, u32[]{:S(2)}, u32[]{:S(2)}) collective-permute-start(f32[27,32,128]{2,1,0:T(8,128)} %get-tuple-element.20), channel_id=1, source_target_pairs={{0,16},{16,32},{32,48},{48,64},{64,80},{80,96},{96,112},{1,17},{17... | collective-permute-start | bytes 1327112 | tf_op jit(solution)/shard_map/ppermute | solution.py:507
  8.6 20.5 %collective-permute-start.1 = (f32[27,32,128]{2,1,0:T(8,128)}, f32[27,32,128]{2,1,0:T(8,128)S(1)}, u32[]{:S(2)}, u32[]{:S(2)}) collective-permute-start(f32[27,32,128]{2,1,0:T(8,128)} %get-tuple-element.21), channel_id=1, source_target_pairs={{16,0},{32,16},{48,32},{64,48},{80,64},{96,80},{112,96},{17,1},{33... | collective-permute-start | bytes 1327112 | tf_op jit(solution)/shard_map/ppermute | solution.py:507
  9.9 6.4 %copy-start.7 = (f32[1,2048]{1,0:T(1,128)S(1)}, f32[1,2048]{1,0:T(1,128)}, u32[]{:S(2)}) copy-start(f32[1,2048]{1,0:T(1,128)} %refs_4_.1) | copy-start | bytes 24580
  9.9 10.8 %collective-permute-start.2 = (f32[4,32,128]{2,1,0:T(8,128)}, f32[4,32,128]{2,1,0:T(8,128)S(1)}, u32[]{:S(2)}, u32[]{:S(2)}) collective-permute-start(f32[4,32,128]{2,1,0:T(8,128)} %get-tuple-element.22), channel_id=1, source_target_pairs={{0,32},{16,48},{32,64},{48,80},{64,96},{80,112},{1,33},{17,49},{33... | collective-permute-start | bytes 196616 | tf_op jit(solution)/shard_map/ppermute | solution.py:507
  14.8 5.9 %collective-permute-start.3 = (f32[4,32,128]{2,1,0:T(8,128)}, f32[4,32,128]{2,1,0:T(8,128)S(1)}, u32[]{:S(2)}, u32[]{:S(2)}) collective-permute-start(f32[4,32,128]{2,1,0:T(8,128)} %get-tuple-element.23), channel_id=1, source_target_pairs={{32,0},{48,16},{64,32},{80,48},{96,64},{112,80},{33,1},{49,17},{65... | collective-permute-start | bytes 196616 | tf_op jit(solution)/shard_map/ppermute | solution.py:507
  16.1 0.7 copy-start.6
  16.1 0.7 copy-start.5
  16.2 0.7 copy-start.4
  16.9 12.2 %copy-start = (s32[32,8,128]{2,1,0:T(8,128)S(1)}, s32[32,8,128]{2,1,0:T(8,128)}, u32[]{:S(2)}) copy-start(s32[32,8,128]{2,1,0:T(8,128)} %param.10) | copy-start | bytes 393220
  16.9 12.2 %copy-start.1 = (f32[1,32,8,128]{3,2,1,0:T(8,128)S(1)}, f32[1,32,8,128]{3,2,1,0:T(8,128)}, u32[]{:S(2)}) copy-start(f32[1,32,8,128]{3,2,1,0:T(8,128)} %param.14) | copy-start | bytes 393220
  16.9 12.2 %copy-start.2 = (f32[1,32,8,128]{3,2,1,0:T(8,128)S(1)}, f32[1,32,8,128]{3,2,1,0:T(8,128)}, u32[]{:S(2)}) copy-start(f32[1,32,8,128]{3,2,1,0:T(8,128)} %param.13) | copy-start | bytes 393220
  16.9 12.2 %copy-start.3 = (f32[1,32,8,128]{3,2,1,0:T(8,128)S(1)}, f32[1,32,8,128]{3,2,1,0:T(8,128)}, u32[]{:S(2)}) copy-start(f32[1,32,8,128]{3,2,1,0:T(8,128)} %param.15) | copy-start | bytes 393220
  29.6 10.9 %collective-permute-start.5 = (f32[11,32,128]{2,1,0:T(8,128)S(1)}, f32[11,32,128]{2,1,0:T(8,128)S(1)}, u32[]{:S(2)}, u32[]{:S(2)}) collective-permute-start(f32[11,32,128]{2,1,0:T(8,128)S(1)} %get-tuple-element.26), channel_id=1, source_target_pairs={{1,0},{2,1},{3,2},{4,3},{5,4},{6,5},{7,6},{8,7},{9,8},{10,9},{11,1... | collective-permute-start | bytes 540680 | tf_op jit(solution)/shard_map/ppermute | solution.py:507
  30.9 9.6 %collective-permute-start.4 = (f32[11,32,128]{2,1,0:T(8,128)S(1)}, f32[11,32,128]{2,1,0:T(8,128)S(1)}, u32[]{:S(2)}, u32[]{:S(2)}) collective-permute-start(f32[11,32,128]{2,1,0:T(8,128)S(1)} %get-tuple-element.25.after), channel_id=1, source_target_pairs={{0,1},{1,2},{2,3},{3,4},{4,5},{5,6},{6,7},{7,8},{8,9},{9,10},{10,1... | collective-permute-start | bytes 540680 | tf_op jit(solution)/shard_map/ppermute | solution.py:507
